TPU v7x, 768 devices: a whole 4x8x12 slice. The times are simulated.
768 devices in a mesh: grp: 96 (over y_lo, z, core), intra: 8 (over y_hi, x).
Axes of the slice: x: 4, y: 8 (y_hi: 2, y_lo: 4; y = y_hi * 4 + y_lo), z: 12, core: 2. Of those that a mesh axis runs over, the one named last changes fastest.
Arguments:
- grads: bfloat16 [768, 192, 2048], P(('grp', 'intra')), may hold values from -4 to 4
- sign_rows: int32 [192, 16], replicated, may hold values from 0 to 1
- sign_cols: int32 [192, 128], replicated, may hold values from 0 to 1
- block_order: int32 [192], replicated, may hold values from 0 to 191, each once
- master: float32 [192, 2048], P('grp'), may hold values from -6 to 6
- first_moment: float32 [192, 2048], P('grp'), may hold values from -6 to 6
- second_moment: float32 [192, 2048], P('grp'), may hold values from 0.5 to 4
Outputs:
- new_master: float32 [192, 2048], P('grp')
- new_first: float32 [192, 2048], P('grp')
- new_second: float32 [192, 2048], P('grp')
- params: bfloat16 [192, 2048], replicated
Inputs may be any that keep to these rules, and one draw needn't show every extreme that they name: `block_order`: each block id appears in exactly one slot.
All inputs are finite; a program needn't handle non-finite values.
Results may differ from a plain program's by a relative error of at most 0.0029.
Values may be sent and summed in bfloat16 or wider, within the bound.
No kernel may reach another device: no remote copies, remote signals or barrier semaphores. Data moves between devices by JAX's collectives and lax.ppermute only.
A program may use at most 32 MiB of HBM per device.

v0:
```python
import math

import jax
import jax.numpy as jnp
from jax import lax
from jax.sharding import PartitionSpec as P

beta_one = 0.9
beta_two = 0.95
first_fix = 1.0 - math.exp(100.0 * math.log(0.9))
second_fix = 1.0 - math.exp(100.0 * math.log(0.95))
learn_rate = 0.25
weight_decay = 0.1
epsilon = 1e-08


def hadamard_table(length, dtype):
    index = jnp.arange(length, dtype=jnp.int32)
    both = index[:, None] & index[None, :]
    parity = jnp.zeros((length, length), jnp.int32)
    for bit in range(length.bit_length() - 1):
        parity = parity + (jnp.right_shift(both, bit) & 1)
    parity = parity & 1
    return (1 - 2 * parity).astype(dtype)


def sign_table(picked_rows, picked_cols, dtype):
    table = (2 * picked_rows - 1)[:, :, None] * (2 * picked_cols - 1)[:, None, :]
    return table.astype(dtype)


def on_device(grads, sign_rows, sign_cols, block_order, master, first_moment, second_moment):
    held_grad = grads[0]
    block_count = held_grad.shape[0]
    block_len = held_grad.shape[1]
    sub_count = sign_rows.shape[1]
    lane_count = sign_cols.shape[1]
    owned_rows = master.shape[0]
    inv_root = 1.0 / math.sqrt(block_len)
    lane_bf16 = hadamard_table(lane_count, jnp.bfloat16)
    lane_float = hadamard_table(lane_count, jnp.float32)
    sub_float = hadamard_table(sub_count, jnp.float32)
    grad_rows = jnp.take(held_grad, block_order, axis=0).reshape(block_count, sub_count, lane_count)
    signed = grad_rows * sign_table(
        jnp.take(sign_rows, block_order, axis=0),
        jnp.take(sign_cols, block_order, axis=0),
        jnp.bfloat16,
    )
    mixed_rows = jnp.einsum("rac,cd->rad", signed, lane_bf16, preferred_element_type=jnp.float32)
    mixed_rows = jnp.einsum("ba,rad->rbd", sub_float, mixed_rows, precision=lax.Precision.HIGHEST)
    rotated_half = (mixed_rows * inv_root).astype(jnp.bfloat16).reshape(block_count, block_len)
    rotated = rotated_half.astype(jnp.float32)
    partial_value = lax.psum_scatter(rotated, "grp", scatter_dimension=0, tiled=True)
    summed = lax.psum(partial_value, "intra")
    slot_base = lax.axis_index("grp") * owned_rows
    owned_blocks = lax.dynamic_slice_in_dim(block_order, slot_base, owned_rows)
    owned_signs = sign_table(
        jnp.take(sign_rows, owned_blocks, axis=0),
        jnp.take(sign_cols, owned_blocks, axis=0),
        jnp.float32,
    )
    gradient = summed.reshape(owned_rows, sub_count, lane_count)
    first_old = first_moment.reshape(owned_rows, sub_count, lane_count)
    second_old = second_moment.reshape(owned_rows, sub_count, lane_count)
    new_first = beta_one * first_old + (1.0 - beta_one) * gradient
    new_second = beta_two * second_old + (1.0 - beta_two) * gradient * gradient
    update = new_first / first_fix / (jnp.sqrt(new_second / second_fix) + epsilon)
    restored = jnp.einsum("ba,rad->rbd", sub_float, update, precision=lax.Precision.HIGHEST)
    restored = jnp.einsum("rbc,cd->rbd", restored, lane_float, precision=lax.Precision.HIGHEST)
    restored = (restored * inv_root * owned_signs).reshape(owned_rows, block_len)
    new_master = master - learn_rate * (restored + weight_decay * master)
    held_bf16 = new_master.astype(jnp.bfloat16)
    gathered = lax.all_gather(held_bf16, "grp", axis=0, tiled=True)
    inverse = (
        jnp.zeros((block_count,), jnp.int32)
        .at[block_order]
        .set(jnp.arange(block_count, dtype=jnp.int32))
    )
    params = jnp.take(gathered, inverse, axis=0)
    return (
        new_master,
        new_first.reshape(owned_rows, block_len),
        new_second.reshape(owned_rows, block_len),
        params,
    )


def solution(mesh):
    placed = (
        P(("grp", "intra"), None, None),
        P(),
        P(),
        P(),
        P("grp", None),
        P("grp", None),
        P("grp", None),
    )
    return jax.shard_map(
        on_device,
        mesh=mesh,
        in_specs=placed,
        out_specs=(P("grp", None), P("grp", None), P("grp", None), P()),
        check_vma=False,
    )
```

profile of v0, /device:TPU:1, one launch (start us, length us, event | category | flops | bytes accessed | tf_op | source)
XLA Modules:
  0.0 1005.7 jit_solution(201998934785086108)
XLA Ops:
  7.2 0.0 copy-start
  7.2 0.0 all-reduce.3.cloned.1.call-start
  7.2 0.8 compare_and_fusion.1
  8.0 0.7 compare_select_fusion.1
  8.7 0.8 copy.13
  9.5 0.7 gather_fusion
  10.2 1.6 gather_fusion.1
  11.8 0.1 multiply_add_fusion.1
  11.9 0.1 multiply_add_fusion
  12.0 0.0 copy-done
  12.0 1.1 gather_fusion.4
  13.1 0.1 select_bitcast_fusion
  13.3 0.2 copy.16
  13.4 0.6 fusion.4
  14.1 1.5 fusion
  15.5 1.8 copy.36
  17.3 0.0 copy-start.4
  17.3 0.0 copy-start.1
  17.3 0.0 copy-start.2
  17.3 0.0 copy-start.3
  17.3 0.0 all-reduce.3.cloned.1.call-update
  17.3 0.6 copy-done.4
  18.0 0.1 compare_and_fusion.2
  18.0 1.5 gather_fusion.3
  19.5 0.6 gather_fusion.2
  20.1 1.2 scatter_custom_fusion
  21.3 1.3 dynamic-slice
  23.2 0.1 multiply_add_fusion.3
  23.3 0.1 multiply_add_fusion.4
  23.4 801.6 %all-reduce.3.cloned.1.call-done = f32[192,2048]{1,0:T(8,128)} async-done(((f32[192,2048]{1,0:T(8,128)}), f32[192,2048]{1,0:T(8,128)}) %all-reduce.3.cloned.1.call-update) | async-done | bytes 1572880
  825.0 0.8 constant_dynamic-slice_fusion
  825.8 44.7 %psum.7 = f32[2,2048]{1,0:T(2,128)S(1)} all-reduce(f32[2,2048]{1,0:T(2,128)S(1)} %constant_dynamic-slice_fusion), channel_id=1, replica_groups=mesh['grp'=96,'intra'=8] {'intra'}, use_global_device_ids=true, to_apply=%region_1.3 | all-reduce | flops 4096 | bytes 32768 | tf_op jit(solution)/shard_map/psum | solution.py:54
  870.5 0.0 copy-done.1
  870.5 0.0 copy-done.2
  870.5 0.6 fusion.18
  871.2 0.2 convolution_bitcast_fusion
  871.3 0.2 fusion.2
  871.6 0.0 copy-done.3
  871.6 0.6 convert_bitcast_fusion
  872.2 124.2 %all-gather = bf16[96,2,2048]{2,1,0:T(2,128)(2,1)S(1)} all-gather(bf16[1,2,2048]{2,1,0:T(2,128)(2,1)S(1)} %get-tuple-element.5), channel_id=1, replica_groups=mesh['grp'=96,'intra'=8] {'grp'}, dimensions={0}, use_global_device_ids=true | all-gather | bytes 794624 | tf_op jit(solution)/shard_map/all_gather | solution.py:73
  996.4 0.3 reshape.177
  996.7 1.1 gather_fusion.5
  997.9 1.0 broadcast_select_fusion
  (6 shorter events, 0.0 us)
Async XLA Ops:
  7.2 4.8 copy-start
  7.2 817.8 %all-reduce.3.cloned.1.call-start = ((), (), s32[]{:S(2)}) async-start(), calls=%async_computation | async-start | bytes 3145728
  17.3 0.7 copy-start.4
  17.3 853.3 %copy-start.1 = (f32[2,2048]{1,0:T(2,128)S(1)}, f32[2,2048]{1,0:T(2,128)}, u32[]{:S(2)}) copy-start(f32[2,2048]{1,0:T(2,128)} %param.15) | copy-start | bytes 49156
  17.3 853.3 %copy-start.2 = (f32[2,2048]{1,0:T(2,128)S(1)}, f32[2,2048]{1,0:T(2,128)}, u32[]{:S(2)}) copy-start(f32[2,2048]{1,0:T(2,128)} %param.14) | copy-start | bytes 49156
  17.3 854.3 %copy-start.3 = (f32[2,2048]{1,0:T(2,128)S(1)}, f32[2,2048]{1,0:T(2,128)}, u32[]{:S(2)}) copy-start(f32[2,2048]{1,0:T(2,128)} %param.13) | copy-start | bytes 49156
Sparse Core Ops, SparseCore 0:
  17.4 807.5 all-reduce.2
where the time goes:
time: 1010 us
  waiting for transfers between devices  802 us (79%)
  blocking collectives  169 us (17%)
  between operations  14.8 us (1%)
  local copies, waits for them, and re-layouts  13.6 us (1%)
    unnamed x2, waiting for transfers between devices  802 us
    all_gather x1, blocking collectives, on_device(): gathered = lax.all_gather(held_bf16, 'grp', axis=0, tiled=True)  124 us
    psum x1, blocking collectives, on_device(): summed = lax.psum(partial_value, 'intra')  44.7 us
  transfers between devices with their start and end apart: 1, of which 1 were waited for; matrix products, arithmetic and copies ran while one was open for 0% of the time, Pallas kernels for 0%

commit v1 on v0

v1 whole, which is shorter than its diff:
```python
import math

import jax
import jax.numpy as jnp
import numpy as np
from jax import lax
from jax.sharding import Mesh, PartitionSpec as P

beta_one = 0.9
beta_two = 0.95
first_fix = 1.0 - math.exp(100.0 * math.log(0.9))
second_fix = 1.0 - math.exp(100.0 * math.log(0.95))
learn_rate = 0.25
weight_decay = 0.1
epsilon = 1e-08

AXES = ("y_lo", "z", "core", "y_hi", "x")
SIZES = (4, 12, 2, 2, 4)


def hadamard_table(length, dtype):
    index = jnp.arange(length, dtype=jnp.int32)
    both = index[:, None] & index[None, :]
    parity = jnp.zeros((length, length), jnp.int32)
    for bit in range(length.bit_length() - 1):
        parity = parity + (jnp.right_shift(both, bit) & 1)
    parity = parity & 1
    return (1 - 2 * parity).astype(dtype)


def on_device(grads, sign_rows, sign_cols, block_order, master, first_moment, second_moment):
    held_grad = grads[0]
    block_len = held_grad.shape[1]
    inv_root = 1.0 / math.sqrt(block_len)
    lane_bf16 = hadamard_table(128, jnp.bfloat16)
    lane_float = hadamard_table(128, jnp.float32)
    sub_float = hadamard_table(16, jnp.float32)

    order_cm = block_order.reshape(48, 2, 2).transpose(1, 0, 2).reshape(192)
    pick = (order_cm[:, None] == jnp.arange(192, dtype=jnp.int32)[None, :]).astype(jnp.bfloat16)
    picked = jnp.dot(pick, held_grad, preferred_element_type=jnp.float32).astype(jnp.bfloat16)
    both_signs = jnp.concatenate([2 * sign_rows - 1, 2 * sign_cols - 1], axis=1).astype(jnp.bfloat16)
    signs = jnp.dot(pick, both_signs, preferred_element_type=jnp.float32).astype(jnp.bfloat16)
    signed = picked.reshape(192, 16, 128) * signs[:, :16, None] * signs[:, None, 16:]
    mixed = jnp.einsum("rac,cd->rad", signed, lane_bf16, preferred_element_type=jnp.float32)
    mixed = jnp.einsum("ba,rad->rbd", sub_float, mixed, precision=lax.Precision.HIGHEST)
    rotated = (mixed * inv_root).astype(jnp.bfloat16)
    sent = rotated.reshape(2, 96, 4, 4, 128).transpose(0, 2, 1, 3, 4).reshape(8, 384, 128)
    got = lax.all_to_all(sent, ("core", "x"), 0, 0, tiled=True)
    part = jnp.sum(got.astype(jnp.float32), axis=0).astype(jnp.bfloat16)
    sent = jnp.broadcast_to(part.reshape(48, 1, 8, 128), (48, 2, 8, 128)).reshape(96, 8, 128)
    got = lax.all_to_all(sent, ("y_lo", "z", "y_hi"), 0, 0, tiled=True)
    quarter = jnp.sum(got.astype(jnp.float32), axis=0)
    sent = jnp.broadcast_to(quarter[None], (4, 8, 128))
    got = lax.all_to_all(sent, "x", 0, 0, tiled=True)
    gradient = got.reshape(4, 2, 4, 128).transpose(1, 0, 2, 3).reshape(2, 16, 128)

    owner = (lax.axis_index("y_lo") * 12 + lax.axis_index("z")) * 2 + lax.axis_index("core")
    owned_blocks = lax.dynamic_slice_in_dim(block_order, owner * 2, 2)
    owned_signs = (
        (2 * jnp.take(sign_rows, owned_blocks, axis=0) - 1)[:, :, None]
        * (2 * jnp.take(sign_cols, owned_blocks, axis=0) - 1)[:, None, :]
    ).astype(jnp.float32)
    first_old = first_moment.reshape(2, 16, 128)
    second_old = second_moment.reshape(2, 16, 128)
    new_first = beta_one * first_old + (1.0 - beta_one) * gradient
    new_second = beta_two * second_old + (1.0 - beta_two) * gradient * gradient
    update = new_first / first_fix / (jnp.sqrt(new_second / second_fix) + epsilon)
    restored = jnp.einsum("ba,rad->rbd", sub_float, update, precision=lax.Precision.HIGHEST)
    restored = jnp.einsum("rbc,cd->rbd", restored, lane_float, precision=lax.Precision.HIGHEST)
    restored = (restored * inv_root * owned_signs).reshape(2, block_len)
    new_master = master - learn_rate * (restored + weight_decay * master)

    held = new_master.astype(jnp.bfloat16).reshape(2, 4, 4, 128)
    mine = lax.dynamic_slice_in_dim(held, lax.axis_index("x"), 1, axis=1).reshape(1, 8, 128)
    got = lax.all_to_all(jnp.broadcast_to(mine, (48, 8, 128)), ("y_lo", "z"), 0, 0, tiled=True)
    sent = jnp.broadcast_to(got.reshape(1, 384, 128), (4, 384, 128))
    got = lax.all_to_all(sent, "x", 0, 0, tiled=True)
    got = lax.all_gather(got.reshape(4 * 384, 128), "core", axis=0, tiled=True)
    by_slot = got.reshape(2, 4, 96, 4, 128).transpose(0, 2, 1, 3, 4).reshape(192, block_len)
    place = (jnp.arange(192, dtype=jnp.int32)[:, None] == order_cm[None, :]).astype(jnp.bfloat16)
    params = jnp.dot(place, by_slot, preferred_element_type=jnp.float32).astype(jnp.bfloat16)
    return (
        new_master,
        new_first.reshape(2, block_len),
        new_second.reshape(2, block_len),
        params,
    )


def solution(mesh):
    fine = Mesh(np.asarray(mesh.devices).reshape(SIZES), AXES)
    group = ("y_lo", "z", "core")
    placed = (
        P(AXES, None, None),
        P(),
        P(),
        P(),
        P(group, None),
        P(group, None),
        P(group, None),
    )
    return jax.shard_map(
        on_device,
        mesh=fine,
        in_specs=placed,
        out_specs=(P(group, None), P(group, None), P(group, None), P()),
        check_vma=False,
    )
```

time: 1010 us -> 109 us (0.11)
  waiting for transfers between devices: 802 us -> 16.3 us
  blocking collectives: 169 us -> 59.4 us
  starting transfers between devices: 0.04 us -> 17.6 us
  between operations: 14.8 us -> 0.88 us
    unnamed x2 -> x0, waiting for transfers between devices: 802 us -> none
    all_gather x1, blocking collectives: 124 us -> 6.97 us  [on_device(): got = lax.all_gather(got.reshape(4 * 384, 128), 'core', axis=0, tiled=True)]
    all_to_all x0 -> x3, blocking collectives: none -> 52.5 us  [the longest x1 25.2 us: on_device(): got = lax.all_to_all(sent, ('core', 'x'), 0, 0, tiled=True)]
    psum x1 -> x0, blocking collectives: 44.7 us -> none  [on_device(): summed = lax.psum(partial_value, 'intra')]
    all_to_all x0 -> x2, starting transfers between devices: none -> 17.6 us  [the longest x1 14.4 us: on_device(): got = lax.all_to_all(sent, ('y_lo', 'z', 'y_hi'), 0, 0, tiled=True)]
    all_to_all x0 -> x2, waiting for transfers between devices: none -> 16.3 us  [the longest x1 12.1 us: on_device(): got = lax.all_to_all(sent, ('y_lo', 'z', 'y_hi'), 0, 0, tiled=True)]
  transfers between devices with their start and end apart: 1 -> 2, of which waited for: 1 -> 2; matrix products, arithmetic and copies ran while one was open for 0% -> 2% of each run, Pallas kernels for 0% -> 0%
where the time goes in v1:
time: 109 us
  blocking collectives  59.4 us (54%)
  starting transfers between devices  17.6 us (16%)
  waiting for transfers between devices  16.3 us (15%)
  local copies, waits for them, and re-layouts  6.28 us (6%)
  matrix products  4.24 us (4%)
  other arithmetic  3.84 us (4%)
    all_to_all x1, blocking collectives, on_device(): got = lax.all_to_all(sent, ('core', 'x'), 0, 0, tiled=True)  25.2 us
    all_to_all x1, blocking collectives, on_device(): lax.all_to_all(jnp.broadcast_to(mine, (48, 8, 128)), ('y_lo', 'z'), 0, 0,...  18.6 us
    all_to_all x1, starting transfers between devices, on_device(): got = lax.all_to_all(sent, ('y_lo', 'z', 'y_hi'), 0, 0, tiled=True)  14.4 us
    all_to_all x1, waiting for transfers between devices, on_device(): got = lax.all_to_all(sent, ('y_lo', 'z', 'y_hi'), 0, 0, tiled=True)  12.1 us
    all_to_all x1, blocking collectives, on_device(): got = lax.all_to_all(sent, 'x', 0, 0, tiled=True)  8.62 us
    all_gather x1, blocking collectives, on_device(): got = lax.all_gather(got.reshape(4 * 384, 128), 'core', axis=0, tiled=True)  6.97 us
    all_to_all x1, waiting for transfers between devices, on_device(): got = lax.all_to_all(sent, 'x', 0, 0, tiled=True)  4.1 us
    all_to_all x1, starting transfers between devices, on_device(): got = lax.all_to_all(sent, 'x', 0, 0, tiled=True)  3.25 us
  transfers between devices with their start and end apart: 2, of which 2 were waited for; matrix products, arithmetic and copies ran while one was open for 2% of the time, Pallas kernels for 0%

profile of v1, /device:TPU:1, one launch (start us, length us, event | category | flops | bytes accessed | tf_op | source)
XLA Modules:
  0.0 108.6 jit_solution(7115658523206105229)
XLA Ops:
  0.6 0.0 copy-start
  0.6 0.9 reshape.105
  1.6 0.1 eq.28
  1.7 0.9 add_convert_fusion
  2.6 0.7 add_convert_fusion.1
  3.4 0.1 copy.48
  3.5 0.3 convolution_convert_fusion.2
  3.8 0.0 copy-done
  3.8 0.4 fusion
  4.2 0.2 copy.57
  4.4 0.1 copy.50
  4.5 0.1 copy.49
  4.6 0.5 fusion.3
  5.1 0.4 fusion.13
  5.5 1.5 %multiply_convert_fusion = bf16[192,128,16]{1,2,0:T(8,128)(2,1)S(1)} fusion(f32[192,16,128]{2,1,0:T(8,128)S(1)} %fusion.13), kind=kOutput, calls=%fused_computation.4 | convolution fusion | flops 76288000 | bytes 2359296 | tf_op jit(solution)/shard_map/ba,rad->rbd/dot_general | solution.py:46
  7.0 0.3 copy.51
  7.3 0.0 copy-start.1
  7.3 0.0 copy-start.5
  7.3 0.0 copy-start.2
  7.3 0.0 copy-start.3
  7.3 25.2 %all_to_all.25 = bf16[8,384,128]{2,1,0:T(8,128)(2,1)S(1)} all-to-all(bf16[8,384,128]{2,1,0:T(8,128)(2,1)S(1)} %bitcast.70), channel_id=1, replica_groups=mesh['y_lo'=4,'z'=12,'core'=2,'y_hi'=2,'x'=4] {'core','x'}, dimensions={0} | all-to-all | bytes 1572864 | tf_op jit(solution)/shard_map/all_to_all | solution.py:49
  32.6 0.0 copy-start.4
  32.6 0.1 reduce_sum.21
  32.7 0.7 broadcast_in_dim.62
  33.4 14.4 %all-to-all-start.1 = ((bf16[96,8,128]{2,1,0:T(8,128)(2,1)}), bf16[96,8,128]{2,1,0:T(8,128)(2,1)S(1)}, u32[]{:S(2)}, u32[]{:S(2)}) async-start(bf16[96,8,128]{2,1,0:T(8,128)(2,1)} %bitcast.9), calls=%async_computation.1 | async-start | bytes 393216 | tf_op jit(solution)/shard_map/all_to_all | solution.py:52
  47.8 0.0 copy-done.1
  47.8 0.1 copy.53
  47.9 0.0 copy-done.5
  47.9 0.1 compare_and_fusion
  48.0 1.5 %gather_fusion.1 = s32[2,128]{1,0:T(2,128)S(1)} fusion(s32[192,128]{1,0:T(8,128)} %param.9, s32[1024]{0:T(1024)S(1)} %pad_clamp_fusion), kind=kCustom, calls=%fused_computation.1 | custom fusion | bytes 2056 | tf_op jit(solution)/shard_map/jit(_take)/gather | solution.py:62
  49.5 0.6 gather_fusion
  50.0 0.1 multiply_add_fusion.1
  50.1 12.1 %all-to-all-done.1 = bf16[96,8,128]{2,1,0:T(8,128)(2,1)S(1)} async-done(((bf16[96,8,128]{2,1,0:T(8,128)(2,1)}), bf16[96,8,128]{2,1,0:T(8,128)(2,1)S(1)}, u32[]{:S(2)}, u32[]{:S(2)}) %all-to-all-start.1) | async-done | bytes 196640 | tf_op jit(solution)/shard_map/all_to_all | solution.py:52
  62.2 0.1 convert_reduce_fusion
  62.3 0.6 broadcast_in_dim.63
  63.0 3.3 %all-to-all-start.2 = ((f32[4,8,128]{2,1,0:T(8,128)}), f32[4,8,128]{2,1,0:T(8,128)S(1)}, u32[]{:S(2)}, u32[]{:S(2)}) async-start(f32[4,8,128]{2,1,0:T(8,128)} %broadcast_in_dim.63), calls=%async_computation.2 | async-start | bytes 32768 | tf_op jit(solution)/shard_map/all_to_all | solution.py:55
  66.2 0.1 multiply_add_fusion.2
  66.3 4.1 %all-to-all-done.2 = f32[4,8,128]{2,1,0:T(8,128)S(1)} async-done(((f32[4,8,128]{2,1,0:T(8,128)}), f32[4,8,128]{2,1,0:T(8,128)S(1)}, u32[]{:S(2)}, u32[]{:S(2)}) %all-to-all-start.2) | async-done | bytes 16416 | tf_op jit(solution)/shard_map/all_to_all | solution.py:55
  70.4 0.0 copy-done.2
  70.4 0.0 copy-done.3
  70.4 0.6 fusion.22
  71.1 0.2 convolution_bitcast_fusion
  71.2 0.2 fusion.2
  71.5 0.0 copy-done.4
  71.5 0.6 fusion.76
  72.2 18.6 %all_to_all.26 = bf16[48,8,128]{2,1,0:T(8,128)(2,1)S(1)} all-to-all(bf16[48,8,128]{2,1,0:T(8,128)(2,1)S(1)} %broadcast_in_dim.70), channel_id=1, replica_groups=mesh['y_lo'=4,'z'=12,'core'=2,'y_hi'=2,'x'=4] {'y_lo','z'}, dimensions={0} | all-to-all | bytes 196608 | tf_op jit(solution)/shard_map/all_to_all | solution.py:76
  90.8 0.1 broadcast_in_dim.72
  90.8 8.6 %all_to_all.27 = bf16[4,384,128]{2,1,0:T(8,128)(2,1)S(1)} all-to-all(bf16[4,384,128]{2,1,0:T(8,128)(2,1)S(1)} %broadcast_in_dim.72), channel_id=1, replica_groups=mesh['y_lo'=4,'z'=12,'core'=2,'y_hi'=2,'x'=4] {'x'}, dimensions={0} | all-to-all | bytes 786432 | tf_op jit(solution)/shard_map/all_to_all | solution.py:78
  99.5 7.0 %all_gather.3 = bf16[3072,128]{1,0:T(8,128)(2,1)S(1)} all-gather(bf16[1536,128]{1,0:T(8,128)(2,1)S(1)} %bitcast.73), channel_id=1, replica_groups=mesh['y_lo'=4,'z'=12,'core'=2,'y_hi'=2,'x'=4] {'core'}, dimensions={0}, use_global_device_ids=true | all-gather | bytes 1179648 | tf_op jit(solution)/shard_map/all_gather | solution.py:79
  106.4 0.3 copy.55
  106.7 0.6 reshape.117
  107.3 1.2 %convolution_convert_fusion = bf16[192,2048]{1,0:T(8,128)(2,1)} fusion(bf16[192,2048]{1,0:T(8,128)(2,1)S(1)} %reshape.117, s32[192]{0:T(256)S(1)} %eq.28), kind=kOutput, calls=%fused_computation.2 | convolution fusion | flops 151425024 | bytes 1573632 | tf_op jit(solution)/shard_map/dot_general | solution.py:82
  (9 shorter events, 0.1 us)
Async XLA Ops:
  0.6 3.2 %copy-start = (bf16[1,192,2048]{2,1,0:T(8,128)(2,1)S(1)}, bf16[1,192,2048]{2,1,0:T(8,128)(2,1)}, u32[]{:S(2)}) copy-start(bf16[1,192,2048]{2,1,0:T(8,128)(2,1)} %param.7) | copy-start | bytes 2359300
  7.3 40.5 %copy-start.1 = (s32[192,16]{0,1:T(8,128)S(1)}, s32[192,16]{0,1:T(8,128)}, u32[]{:S(2)}) copy-start(s32[192,16]{0,1:T(8,128)} %param.8) | copy-start | bytes 36868
  7.3 40.6 %copy-start.5 = (s32[192]{0:T(256)S(1)}, s32[192]{0:T(256)}, u32[]{:S(2)}) copy-start(s32[192]{0:T(256)} %param.10) | copy-start | bytes 2308
  7.3 63.1 %copy-start.2 = (f32[2,2048]{1,0:T(2,128)S(1)}, f32[2,2048]{1,0:T(2,128)}, u32[]{:S(2)}) copy-start(f32[2,2048]{1,0:T(2,128)} %param.13) | copy-start | bytes 49156
  7.3 63.1 %copy-start.3 = (f32[2,2048]{1,0:T(2,128)S(1)}, f32[2,2048]{1,0:T(2,128)}, u32[]{:S(2)}) copy-start(f32[2,2048]{1,0:T(2,128)} %param.12) | copy-start | bytes 49156
  32.6 38.9 %copy-start.4 = (f32[2,2048]{1,0:T(2,128)S(1)}, f32[2,2048]{1,0:T(2,128)}, u32[]{:S(2)}) copy-start(f32[2,2048]{1,0:T(2,128)} %param.11) | copy-start | bytes 49156
  33.4 28.8 %all-to-all-start.1 = ((bf16[96,8,128]{2,1,0:T(8,128)(2,1)}), bf16[96,8,128]{2,1,0:T(8,128)(2,1)S(1)}, u32[]{:S(2)}, u32[]{:S(2)}) async-start(bf16[96,8,128]{2,1,0:T(8,128)(2,1)} %bitcast.9), calls=%async_computation.1 | async-start | bytes 393216 | tf_op jit(solution)/shard_map/all_to_all | solution.py:52
  63.0 7.4 %all-to-all-start.2 = ((f32[4,8,128]{2,1,0:T(8,128)}), f32[4,8,128]{2,1,0:T(8,128)S(1)}, u32[]{:S(2)}, u32[]{:S(2)}) async-start(f32[4,8,128]{2,1,0:T(8,128)} %broadcast_in_dim.63), calls=%async_computation.2 | async-start | bytes 32768 | tf_op jit(solution)/shard_map/all_to_all | solution.py:55

commit v2 on v1

--- a/solution.py
+++ b/solution.py
@@ -36,8 +36,10 @@
     lane_float = hadamard_table(128, jnp.float32)
     sub_float = hadamard_table(16, jnp.float32)
 
-    order_cm = block_order.reshape(48, 2, 2).transpose(1, 0, 2).reshape(192)
-    pick = (order_cm[:, None] == jnp.arange(192, dtype=jnp.int32)[None, :]).astype(jnp.bfloat16)
+    core = lax.axis_index("core")
+    order_table = block_order.reshape(4, 12, 2, 2).transpose(2, 1, 0, 3).reshape(2, 96)
+    order_sent = jnp.where(core == 0, order_table[::-1], order_table).reshape(192)
+    pick = (order_sent[:, None] == jnp.arange(192, dtype=jnp.int32)[None, :]).astype(jnp.bfloat16)
     picked = jnp.dot(pick, held_grad, preferred_element_type=jnp.float32).astype(jnp.bfloat16)
     both_signs = jnp.concatenate([2 * sign_rows - 1, 2 * sign_cols - 1], axis=1).astype(jnp.bfloat16)
     signs = jnp.dot(pick, both_signs, preferred_element_type=jnp.float32).astype(jnp.bfloat16)
@@ -45,15 +47,18 @@
     mixed = jnp.einsum("rac,cd->rad", signed, lane_bf16, preferred_element_type=jnp.float32)
     mixed = jnp.einsum("ba,rad->rbd", sub_float, mixed, precision=lax.Precision.HIGHEST)
     rotated = (mixed * inv_root).astype(jnp.bfloat16)
-    sent = rotated.reshape(2, 96, 4, 4, 128).transpose(0, 2, 1, 3, 4).reshape(8, 384, 128)
-    got = lax.all_to_all(sent, ("core", "x"), 0, 0, tiled=True)
+    halves = rotated.reshape(2, 96, 4, 4, 128).transpose(0, 2, 1, 3, 4).reshape(2, 1536, 128)
+    got = lax.all_gather(halves[0], "core", axis=0, tiled=True).reshape(2, 1536, 128)
+    other = lax.dynamic_index_in_dim(got, 1 - core, 0, keepdims=False)
+    part = (halves[1].astype(jnp.float32) + other.astype(jnp.float32)).astype(jnp.bfloat16)
+    got = lax.all_to_all(part.reshape(4, 384, 128), "x", 0, 0, tiled=True)
     part = jnp.sum(got.astype(jnp.float32), axis=0).astype(jnp.bfloat16)
-    sent = jnp.broadcast_to(part.reshape(48, 1, 8, 128), (48, 2, 8, 128)).reshape(96, 8, 128)
-    got = lax.all_to_all(sent, ("y_lo", "z", "y_hi"), 0, 0, tiled=True)
-    quarter = jnp.sum(got.astype(jnp.float32), axis=0)
-    sent = jnp.broadcast_to(quarter[None], (4, 8, 128))
-    got = lax.all_to_all(sent, "x", 0, 0, tiled=True)
-    gradient = got.reshape(4, 2, 4, 128).transpose(1, 0, 2, 3).reshape(2, 16, 128)
+    got = lax.all_to_all(part.reshape(12, 32, 128), "z", 0, 0, tiled=True)
+    part = jnp.sum(got.astype(jnp.float32), axis=0)
+    sent = jnp.broadcast_to(part.reshape(4, 1, 8, 128), (4, 8, 8, 128)).reshape(32, 8, 128)
+    got = lax.all_to_all(sent, ("y_lo", "y_hi", "x"), 0, 0, tiled=True)
+    quarters = jnp.sum(got.reshape(8, 4, 8, 128), axis=0)
+    gradient = quarters.reshape(4, 2, 4, 128).transpose(1, 0, 2, 3).reshape(2, 16, 128)
 
     owner = (lax.axis_index("y_lo") * 12 + lax.axis_index("z")) * 2 + lax.axis_index("core")
     owned_blocks = lax.dynamic_slice_in_dim(block_order, owner * 2, 2)
@@ -78,7 +83,8 @@
     got = lax.all_to_all(sent, "x", 0, 0, tiled=True)
     got = lax.all_gather(got.reshape(4 * 384, 128), "core", axis=0, tiled=True)
     by_slot = got.reshape(2, 4, 96, 4, 128).transpose(0, 2, 1, 3, 4).reshape(192, block_len)
-    place = (jnp.arange(192, dtype=jnp.int32)[:, None] == order_cm[None, :]).astype(jnp.bfloat16)
+    order_got = block_order.reshape(48, 2, 2).transpose(1, 0, 2).reshape(192)
+    place = (jnp.arange(192, dtype=jnp.int32)[:, None] == order_got[None, :]).astype(jnp.bfloat16)
     params = jnp.dot(place, by_slot, preferred_element_type=jnp.float32).astype(jnp.bfloat16)
     return (
         new_master,

time: 109 us -> 106 us (0.972)
  blocking collectives: 59.4 us -> 47.7 us
  waiting for transfers between devices: 16.3 us -> 23.2 us
    all_to_all x2 -> x1, blocking collectives: 33.9 us -> 10.2 us  [on_device(): got = lax.all_to_all(part.reshape(4, 384, 128), 'x', 0, 0, tiled=True)]
    all_gather x0 -> x1, blocking collectives: none -> 12.5 us  [on_device(): lax.all_gather(halves[0], 'core', axis=0, tiled=True).reshape(2, 1536, 128)]
    all_to_all x1 -> x2, waiting for transfers between devices: 12.1 us -> 17.3 us  [the longest x1 9.33 us: on_device(): got = lax.all_to_all(part.reshape(12, 32, 128), 'z', 0, 0, tiled=True)]
    all_to_all x1, blocking collectives: 18.6 us -> 16 us  [on_device(): lax.all_to_all(jnp.broadcast_to(mine, (48, 8, 128)), ('y_lo', 'z'), 0, 0,...]
    all_gather x1, blocking collectives: 6.97 us -> 8.94 us  [on_device(): got = lax.all_gather(got.reshape(4 * 384, 128), 'core', axis=0, tiled=True)]
    all_to_all x1, waiting for transfers between devices: 4.1 us -> 5.88 us  [on_device(): got = lax.all_to_all(sent, 'x', 0, 0, tiled=True)]
    all_to_all x1 -> x2, starting transfers between devices: 14.4 us -> 14.5 us  [the longest x1 7.81 us: on_device(): got = lax.all_to_all(sent, ('y_lo', 'y_hi', 'x'), 0, 0, tiled=True)]
  transfers between devices with their start and end apart: 2 -> 3, of which waited for: 2 -> 3; matrix products, arithmetic and copies ran while one was open for 2% -> 3% of each run, Pallas kernels for 0% -> 0%
where the time goes in v2:
time: 106 us
  blocking collectives  47.7 us (45%)
  waiting for transfers between devices  23.2 us (22%)
  starting transfers between devices  17.9 us (17%)
  local copies, waits for them, and re-layouts  7.09 us (7%)
  other arithmetic  4.48 us (4%)
  matrix products  4.24 us (4%)
    all_to_all x1, blocking collectives, on_device(): lax.all_to_all(jnp.broadcast_to(mine, (48, 8, 128)), ('y_lo', 'z'), 0, 0,...  16 us
    all_gather x1, blocking collectives, on_device(): lax.all_gather(halves[0], 'core', axis=0, tiled=True).reshape(2, 1536, 128)  12.5 us
    all_to_all x1, blocking collectives, on_device(): got = lax.all_to_all(part.reshape(4, 384, 128), 'x', 0, 0, tiled=True)  10.2 us
    all_to_all x1, waiting for transfers between devices, on_device(): got = lax.all_to_all(part.reshape(12, 32, 128), 'z', 0, 0, tiled=True)  9.33 us
    all_gather x1, blocking collectives, on_device(): got = lax.all_gather(got.reshape(4 * 384, 128), 'core', axis=0, tiled=True)  8.94 us
    all_to_all x1, waiting for transfers between devices, on_device(): got = lax.all_to_all(sent, ('y_lo', 'y_hi', 'x'), 0, 0, tiled=True)  7.99 us
    all_to_all x1, starting transfers between devices, on_device(): got = lax.all_to_all(sent, ('y_lo', 'y_hi', 'x'), 0, 0, tiled=True)  7.81 us
    all_to_all x1, starting transfers between devices, on_device(): got = lax.all_to_all(part.reshape(12, 32, 128), 'z', 0, 0, tiled=True)  6.67 us
  transfers between devices with their start and end apart: 3, of which 3 were waited for; matrix products, arithmetic and copies ran while one was open for 3% of the time, Pallas kernels for 0%

profile of v2, /device:TPU:1, one launch (start us, length us, event | category | flops | bytes accessed | tf_op | source)
XLA Modules:
  0.0 105.5 jit_solution(9072300039963554875)
XLA Ops:
  0.6 0.0 copy-start
  0.7 0.9 reshape.128
  1.6 0.1 reshape.129
  1.8 0.1 eq.34
  1.8 0.7 add_convert_fusion.1
  2.6 0.1 copy.51
  2.7 0.9 add_convert_fusion
  3.6 0.3 convolution_convert_fusion.2
  3.9 0.1 copy.53
  4.0 0.1 copy.52
  4.2 0.0 copy-done
  4.2 0.4 fusion
  4.6 0.2 copy.61
  4.8 0.5 fusion.3
  5.2 0.4 fusion.14
  5.6 1.5 %multiply_convert_fusion = bf16[192,128,16]{1,2,0:T(8,128)(2,1)S(1)} fusion(f32[192,16,128]{2,1,0:T(8,128)S(1)} %fusion.14), kind=kOutput, calls=%fused_computation.4 | convolution fusion | flops 76288000 | bytes 2359296 | tf_op jit(solution)/shard_map/ba,rad->rbd/dot_general | solution.py:48
  7.1 0.3 copy.75
  7.4 0.3 fusion.79
  7.7 12.5 %all_gather.6 = bf16[3072,128]{1,0:T(8,128)(2,1)S(1)} all-gather(bf16[1536,128]{1,0:T(8,128)(2,1)S(1)} %bitcast.86), channel_id=1, replica_groups=mesh['y_lo'=4,'z'=12,'core'=2,'y_hi'=2,'x'=4] {'core'}, dimensions={0}, use_global_device_ids=true | all-gather | bytes 1179648 | tf_op jit(solution)/shard_map/all_gather | solution.py:51
  20.2 0.0 copy-start.1
  20.3 0.0 copy-start.5
  20.3 0.0 copy-start.2
  20.3 0.0 copy-start.3
  20.3 0.1 fusion.4
  20.4 0.0 copy-start.4
  20.4 10.2 %all_to_all.25 = bf16[4,384,128]{2,1,0:T(8,128)(2,1)S(1)} all-to-all(bf16[4,384,128]{2,1,0:T(8,128)(2,1)S(1)} %fusion.4), channel_id=1, replica_groups=mesh['y_lo'=4,'z'=12,'core'=2,'y_hi'=2,'x'=4] {'x'}, dimensions={0} | all-to-all | bytes 786432 | tf_op jit(solution)/shard_map/all_to_all | solution.py:54
  30.6 0.7 reduce_sum.30
  31.3 6.7 %all-to-all-start.1 = ((bf16[12,32,128]{2,1,0:T(8,128)(2,1)}), bf16[12,32,128]{2,1,0:T(8,128)(2,1)S(1)}, u32[]{:S(2)}, u32[]{:S(2)}) async-start(bf16[12,32,128]{2,1,0:T(8,128)(2,1)} %bitcast.11), calls=%async_computation.1 | async-start | bytes 196608 | tf_op jit(solution)/shard_map/all_to_all | solution.py:56
  38.0 0.0 copy-done.1
  38.0 0.1 copy.56
  38.1 0.0 copy-done.5
  38.1 0.1 compare_and_fusion
  38.2 0.6 gather_fusion
  38.8 9.3 %all-to-all-done.1 = bf16[12,32,128]{2,1,0:T(8,128)(2,1)S(1)} async-done(((bf16[12,32,128]{2,1,0:T(8,128)(2,1)}), bf16[12,32,128]{2,1,0:T(8,128)(2,1)S(1)}, u32[]{:S(2)}, u32[]{:S(2)}) %all-to-all-start.1) | async-done | bytes 98336 | tf_op jit(solution)/shard_map/all_to_all | solution.py:56
  48.1 0.7 broadcast_in_dim.56
  48.8 7.8 %all-to-all-start.2 = ((f32[32,8,128]{2,1,0:T(8,128)}), f32[32,8,128]{2,1,0:T(8,128)S(1)}, u32[]{:S(2)}, u32[]{:S(2)}) async-start(f32[32,8,128]{2,1,0:T(8,128)} %bitcast.13), calls=%async_computation.2 | async-start | bytes 262144 | tf_op jit(solution)/shard_map/all_to_all | solution.py:59
  56.6 0.1 multiply_add_fusion.2
  56.7 1.4 %gather_fusion.1 = s32[2,128]{1,0:T(2,128)S(1)} fusion(s32[192,128]{1,0:T(8,128)} %param.9, s32[1024]{0:T(1024)S(1)} %pad_clamp_fusion), kind=kCustom, calls=%fused_computation.1 | custom fusion | bytes 2056 | tf_op jit(solution)/shard_map/jit(_take)/gather | solution.py:67
  58.2 0.1 multiply_add_fusion.1
  58.2 8.0 %all-to-all-done.2 = f32[32,8,128]{2,1,0:T(8,128)S(1)} async-done(((f32[32,8,128]{2,1,0:T(8,128)}), f32[32,8,128]{2,1,0:T(8,128)S(1)}, u32[]{:S(2)}, u32[]{:S(2)}) %all-to-all-start.2) | async-done | bytes 131104 | tf_op jit(solution)/shard_map/all_to_all | solution.py:59
  66.3 0.0 copy-done.2
  66.3 0.0 copy-done.3
  66.3 0.6 fusion.23
  66.9 0.2 convolution_bitcast_fusion
  67.1 0.2 fusion.2
  67.3 0.0 copy-done.4
  67.3 0.6 fusion.77
  68.0 16.0 %all_to_all.26 = bf16[48,8,128]{2,1,0:T(8,128)(2,1)S(1)} all-to-all(bf16[48,8,128]{2,1,0:T(8,128)(2,1)S(1)} %broadcast_in_dim.63), channel_id=1, replica_groups=mesh['y_lo'=4,'z'=12,'core'=2,'y_hi'=2,'x'=4] {'y_lo','z'}, dimensions={0} | all-to-all | bytes 196608 | tf_op jit(solution)/shard_map/all_to_all | solution.py:81
  84.0 0.8 broadcast_in_dim.65
  84.8 3.5 %all-to-all-start.4 = ((bf16[4,384,128]{2,1,0:T(8,128)(2,1)}), bf16[4,384,128]{2,1,0:T(8,128)(2,1)S(1)}, u32[]{:S(2)}, u32[]{:S(2)}) async-start(bf16[4,384,128]{2,1,0:T(8,128)(2,1)} %broadcast_in_dim.65), calls=%async_computation.4 | async-start | bytes 786432 | tf_op jit(solution)/shard_map/all_to_all | solution.py:83
  88.3 0.2 reshape.140
  88.5 0.1 eq.39
  88.6 5.9 %all-to-all-done.4 = bf16[4,384,128]{2,1,0:T(8,128)(2,1)S(1)} async-done(((bf16[4,384,128]{2,1,0:T(8,128)(2,1)}), bf16[4,384,128]{2,1,0:T(8,128)(2,1)S(1)}, u32[]{:S(2)}, u32[]{:S(2)}) %all-to-all-start.4) | async-done | bytes 393248 | tf_op jit(solution)/shard_map/all_to_all | solution.py:83
  94.5 8.9 %all_gather.7 = bf16[3072,128]{1,0:T(8,128)(2,1)S(1)} all-gather(bf16[1536,128]{1,0:T(8,128)(2,1)S(1)} %bitcast.83), channel_id=1, replica_groups=mesh['y_lo'=4,'z'=12,'core'=2,'y_hi'=2,'x'=4] {'core'}, dimensions={0}, use_global_device_ids=true | all-gather | bytes 1179648 | tf_op jit(solution)/shard_map/all_gather | solution.py:84
  103.4 0.3 copy.59
  103.7 0.6 reshape.144
  104.3 1.2 %convolution_convert_fusion = bf16[192,2048]{1,0:T(8,128)(2,1)} fusion(bf16[192,2048]{1,0:T(8,128)(2,1)S(1)} %reshape.144, s32[192]{0:T(256)S(1)} %eq.39), kind=kOutput, calls=%fused_computation.2 | convolution fusion | flops 151425024 | bytes 1573632 | tf_op jit(solution)/shard_map/dot_general | solution.py:88
  (15 shorter events, 0.2 us)
Async XLA Ops:
  0.6 3.5 %copy-start = (bf16[1,192,2048]{2,1,0:T(8,128)(2,1)S(1)}, bf16[1,192,2048]{2,1,0:T(8,128)(2,1)}, u32[]{:S(2)}) copy-start(bf16[1,192,2048]{2,1,0:T(8,128)(2,1)} %param.7) | copy-start | bytes 2359300
  20.2 17.8 %copy-start.1 = (s32[192,16]{0,1:T(8,128)S(1)}, s32[192,16]{0,1:T(8,128)}, u32[]{:S(2)}) copy-start(s32[192,16]{0,1:T(8,128)} %param.8) | copy-start | bytes 36868
  20.3 17.9 %copy-start.5 = (s32[192]{0:T(256)S(1)}, s32[192]{0:T(256)}, u32[]{:S(2)}) copy-start(s32[192]{0:T(256)} %param.10) | copy-start | bytes 2308
  20.3 46.0 %copy-start.2 = (f32[2,2048]{1,0:T(2,128)S(1)}, f32[2,2048]{1,0:T(2,128)}, u32[]{:S(2)}) copy-start(f32[2,2048]{1,0:T(2,128)} %param.13) | copy-start | bytes 49156
  20.3 46.0 %copy-start.3 = (f32[2,2048]{1,0:T(2,128)S(1)}, f32[2,2048]{1,0:T(2,128)}, u32[]{:S(2)}) copy-start(f32[2,2048]{1,0:T(2,128)} %param.12) | copy-start | bytes 49156
  20.4 46.9 %copy-start.4 = (f32[2,2048]{1,0:T(2,128)S(1)}, f32[2,2048]{1,0:T(2,128)}, u32[]{:S(2)}) copy-start(f32[2,2048]{1,0:T(2,128)} %param.11) | copy-start | bytes 49156
  31.3 16.8 %all-to-all-start.1 = ((bf16[12,32,128]{2,1,0:T(8,128)(2,1)}), bf16[12,32,128]{2,1,0:T(8,128)(2,1)S(1)}, u32[]{:S(2)}, u32[]{:S(2)}) async-start(bf16[12,32,128]{2,1,0:T(8,128)(2,1)} %bitcast.11), calls=%async_computation.1 | async-start | bytes 196608 | tf_op jit(solution)/shard_map/all_to_all | solution.py:56
  48.8 17.4 %all-to-all-start.2 = ((f32[32,8,128]{2,1,0:T(8,128)}), f32[32,8,128]{2,1,0:T(8,128)S(1)}, u32[]{:S(2)}, u32[]{:S(2)}) async-start(f32[32,8,128]{2,1,0:T(8,128)} %bitcast.13), calls=%async_computation.2 | async-start | bytes 262144 | tf_op jit(solution)/shard_map/all_to_all | solution.py:59
  84.8 9.7 %all-to-all-start.4 = ((bf16[4,384,128]{2,1,0:T(8,128)(2,1)}), bf16[4,384,128]{2,1,0:T(8,128)(2,1)S(1)}, u32[]{:S(2)}, u32[]{:S(2)}) async-start(bf16[4,384,128]{2,1,0:T(8,128)(2,1)} %broadcast_in_dim.65), calls=%async_computation.4 | async-start | bytes 786432 | tf_op jit(solution)/shard_map/all_to_all | solution.py:83

commit v3 on v1

v3 whole, which is shorter than its diff:
```python
import math

import jax
import jax.numpy as jnp
import numpy as np
from jax import lax
from jax.experimental import pallas as pl
from jax.experimental.pallas import tpu as pltpu
from jax.sharding import Mesh, PartitionSpec as P

beta_one = 0.9
beta_two = 0.95
first_fix = 1.0 - math.exp(100.0 * math.log(0.9))
second_fix = 1.0 - math.exp(100.0 * math.log(0.95))
learn_rate = 0.25
weight_decay = 0.1
epsilon = 1e-08

AXES = ("y_lo", "z", "core", "y_hi", "x")
SIZES = (4, 12, 2, 2, 4)
BLOCKS = 192
BLOCK = 2048
LANE = 128
INV_ROOT = 1.0 / math.sqrt(BLOCK)
F32 = jnp.float32
BF16 = jnp.bfloat16


def iota(shape, axis):
    return lax.broadcasted_iota(jnp.int32, shape, axis)


def parity_sign(both, bits):
    for shift in bits:
        both = both ^ jnp.right_shift(both, shift)
    return (1 - 2 * (both & 1)).astype(F32)


def rotate_kernel(order_ref, rows_ref, cols_ref, grad_ref, out_ref):
    core = lax.axis_index("core")
    row = iota((BLOCKS, BLOCKS), 0)
    lane = iota((BLOCKS, BLOCKS), 1)
    half = (row >= 96).astype(jnp.int32)
    place = row - 96 * half
    y_lo = jnp.right_shift(place, 1) & 3
    z = jnp.right_shift(place, 3)
    owner = jnp.where(half == 1, core, 1 - core)
    slot = ((y_lo * 12 + z) * 2 + owner) * 2 + (place & 1)
    order = order_ref[...].astype(F32)
    block = jnp.sum(jnp.where(slot == lane, order, 0.0), axis=1, keepdims=True)
    pick = jnp.where(block == lane.astype(F32), 1.0, 0.0).astype(BF16)
    row_bits = (2 * rows_ref[...] - 1).astype(F32).astype(BF16)
    col_bits = (2 * cols_ref[...] - 1).astype(F32).astype(BF16)
    row_signs = lax.dot_general(pick, row_bits, (((1,), (1,)), ((), ())), preferred_element_type=F32)
    col_signs = jnp.dot(pick, col_bits, preferred_element_type=F32)
    table = parity_sign(iota((LANE, LANE), 0) & iota((LANE, LANE), 1), (4, 2, 1)).astype(BF16)
    mixed = []
    for a in range(16):
        picked = jnp.dot(pick, grad_ref[:, a * LANE : (a + 1) * LANE], preferred_element_type=F32)
        signed = (picked * col_signs * row_signs[:, a : a + 1]).astype(BF16)
        mixed.append(jnp.dot(signed, table, preferred_element_type=F32))
    span = 1
    while span < 16:
        for a in range(16):
            if not a & span:
                low, high = mixed[a], mixed[a + span]
                mixed[a], mixed[a + span] = low + high, low - high
        span *= 2
    for a in range(16):
        rotated = (mixed[a] * INV_ROOT).astype(BF16)
        quarter, column = a // 4, (a % 4) * LANE
        out_ref[0, quarter, :, column : column + LANE] = rotated[:96]
        out_ref[1, quarter, :, column : column + LANE] = rotated[96:]


def owned_signs_kernel(owned_ref, rows_ref, cols_ref, out_ref):
    row = iota((32, BLOCKS), 0)
    lane = iota((32, BLOCKS), 1)
    wanted = jnp.where((row & 1) == 0, owned_ref[0], owned_ref[1])
    pick = jnp.where(lane == wanted, 1.0, 0.0)
    spread = jnp.where(iota((32, 16), 1) == jnp.right_shift(iota((32, 16), 0), 1), 1.0, 0.0).astype(BF16)
    row_bits = (2 * rows_ref[...] - 1).astype(F32).astype(BF16)
    col_bits = (2 * cols_ref[...] - 1).astype(F32).astype(BF16)
    wide = jnp.dot(spread, row_bits, preferred_element_type=F32)
    row_signs = jnp.sum(wide * pick, axis=1, keepdims=True)
    col_signs = jnp.dot(pick.astype(BF16), col_bits, preferred_element_type=F32)
    out_ref[...] = row_signs * col_signs


def adam_kernel(got_ref, signs_ref, master_ref, first_ref, second_ref, new_master_ref, new_first_ref, new_second_ref, sent_ref, held_ref):
    total = got_ref[0:4]
    for y in range(1, 8):
        total = total + got_ref[4 * y : 4 * y + 4]
    gradient = total.reshape(32, LANE)
    new_first = beta_one * first_ref[...] + (1.0 - beta_one) * gradient
    new_second = beta_two * second_ref[...] + (1.0 - beta_two) * gradient * gradient
    new_first_ref[...] = new_first
    new_second_ref[...] = new_second
    update = new_first / first_fix / (jnp.sqrt(new_second / second_fix) + epsilon)
    row, col = iota((32, 32), 0), iota((32, 32), 1)
    same = ((row ^ col) & 1) == 0
    sub = jnp.where(same, parity_sign(jnp.right_shift(row & col, 1), (2, 1)), 0.0)
    table = parity_sign(iota((LANE, LANE), 0) & iota((LANE, LANE), 1), (4, 2, 1))
    restored = jnp.dot(sub, update, precision=lax.Precision.HIGHEST, preferred_element_type=F32)
    restored = jnp.dot(restored, table, precision=lax.Precision.HIGHEST, preferred_element_type=F32)
    restored = restored * INV_ROOT * signs_ref[...]
    master = master_ref[...]
    new_master = master - learn_rate * (restored + weight_decay * master)
    new_master_ref[...] = new_master
    held_ref[...] = new_master
    start = pl.multiple_of(lax.axis_index("x") * 8, 8)
    mine = held_ref[pl.ds(start, 8), :].astype(BF16)
    for member in range(48):
        sent_ref[member] = mine


def place_kernel(order_ref, out_ref):
    col = iota((BLOCKS, 768), 1)
    core = (col >= 384).astype(jnp.int32)
    rest = col - 384 * core
    slot = (jnp.right_shift(rest, 3) * 2 + core) * 2 + (rest & 1)
    spread = jnp.where(iota((BLOCKS, 768), 0) == slot, 1.0, 0.0).astype(BF16)
    order = jnp.broadcast_to(order_ref[...].astype(F32), (8, BLOCKS)).astype(BF16)
    block = jnp.dot(order, spread, preferred_element_type=F32)[0:1]
    match = iota((BLOCKS, 768), 0).astype(F32) == block
    part = jnp.right_shift(rest, 1) & 3
    for a in range(4):
        out_ref[a * BLOCKS : (a + 1) * BLOCKS, :] = jnp.where(match & (part == a), 1.0, 0.0).astype(BF16)


def params_kernel(place_ref, got_ref, out_ref):
    for x in range(4):
        rows = jnp.concatenate([got_ref[0, x], got_ref[1, x]], axis=0)
        placed = jnp.dot(place_ref[...], rows, preferred_element_type=F32).astype(BF16)
        for a in range(4):
            column = (4 * x + a) * LANE
            out_ref[:, column : column + LANE] = placed[a * BLOCKS : (a + 1) * BLOCKS]


VMEM = pl.BlockSpec(memory_space=pltpu.VMEM)
SMEM = pl.BlockSpec(memory_space=pltpu.SMEM)
ROOM = pltpu.CompilerParams(vmem_limit_bytes=32 * 1024 * 1024)


def on_device(grads, sign_rows, sign_cols, block_order, master, first_moment, second_moment):
    core = lax.axis_index("core")
    order_row = block_order.reshape(1, BLOCKS)
    rows_t = sign_rows.T

    halves = pl.pallas_call(
        rotate_kernel,
        out_shape=jax.ShapeDtypeStruct((2, 4, 96, 512), BF16),
        in_specs=[VMEM] * 4,
        out_specs=VMEM,
        compiler_params=ROOM,
        name="rotate",
    )(order_row, rows_t, sign_cols, grads[0])
    got = lax.all_gather(halves[0].reshape(384, 512), "core", axis=0, tiled=True).reshape(2, 4, 96, 512)
    other = lax.dynamic_index_in_dim(got, 1 - core, 0, keepdims=False)
    part = (halves[1].astype(F32) + other.astype(F32)).astype(BF16)
    got = lax.all_to_all(part, "x", 0, 0, tiled=True)
    part = jnp.sum(got.astype(F32), axis=0).astype(BF16)
    got = lax.all_to_all(part.reshape(12, 8, 512), "z", 0, 0, tiled=True)
    part = jnp.sum(got.astype(F32), axis=0)
    part = part.reshape(4, 2, 4, LANE).transpose(0, 2, 1, 3).reshape(4, 1, 8, LANE)
    sent = jnp.broadcast_to(part, (4, 8, 8, LANE)).reshape(32, 8, LANE)
    got = lax.all_to_all(sent, ("y_lo", "y_hi", "x"), 0, 0, tiled=True)

    owner = (lax.axis_index("y_lo") * 12 + lax.axis_index("z")) * 2 + core
    owned = lax.dynamic_slice_in_dim(block_order, owner * 2, 2)
    signs = pl.pallas_call(
        owned_signs_kernel,
        out_shape=jax.ShapeDtypeStruct((32, LANE), F32),
        in_specs=[SMEM, VMEM, VMEM],
        out_specs=VMEM,
        compiler_params=ROOM,
        cost_estimate=pl.CostEstimate(flops=2000000, bytes_accessed=200000, transcendentals=0),
        name="owned_signs",
    )(owned, rows_t, sign_cols)

    def by_row(value):
        return value.reshape(2, 16, LANE).transpose(1, 0, 2).reshape(32, LANE)

    def by_slot(value):
        return value.reshape(16, 2, LANE).transpose(1, 0, 2).reshape(2, BLOCK)

    state = jax.ShapeDtypeStruct((32, LANE), F32)
    new_master, new_first, new_second, sent = pl.pallas_call(
        adam_kernel,
        out_shape=(state, state, state, jax.ShapeDtypeStruct((48, 8, LANE), BF16)),
        in_specs=[VMEM] * 5,
        out_specs=(VMEM,) * 4,
        scratch_shapes=[pltpu.VMEM((32, LANE), F32)],
        compiler_params=ROOM,
        name="adam",
    )(got, signs, by_row(master), by_row(first_moment), by_row(second_moment))

    got = lax.all_to_all(sent, ("y_lo", "z"), 0, 0, tiled=True)
    sent = jnp.broadcast_to(got.reshape(1, 384, LANE), (4, 384, LANE))
    got = lax.all_to_all(sent, "x", 0, 0, tiled=True)
    got = lax.all_gather(got.reshape(1536, LANE), "core", axis=0, tiled=True).reshape(2, 4, 384, LANE)

    place = pl.pallas_call(
        place_kernel,
        out_shape=jax.ShapeDtypeStruct((768, 768), BF16),
        in_specs=[VMEM],
        out_specs=VMEM,
        compiler_params=ROOM,
        cost_estimate=pl.CostEstimate(flops=4000000, bytes_accessed=1200000, transcendentals=0),
        name="place",
    )(order_row)
    params = pl.pallas_call(
        params_kernel,
        out_shape=jax.ShapeDtypeStruct((BLOCKS, BLOCK), BF16),
        in_specs=[VMEM] * 2,
        out_specs=VMEM,
        compiler_params=ROOM,
        name="params",
    )(place, got)
    return by_slot(new_master), by_slot(new_first), by_slot(new_second), params


def solution(mesh):
    fine = Mesh(np.asarray(mesh.devices).reshape(SIZES), AXES)
    group = ("y_lo", "z", "core")
    placed = (
        P(AXES, None, None),
        P(),
        P(),
        P(),
        P(group, None),
        P(group, None),
        P(group, None),
    )
    return jax.shard_map(
        on_device,
        mesh=fine,
        in_specs=placed,
        out_specs=(P(group, None), P(group, None), P(group, None), P()),
        check_vma=False,
    )
```

time: 109 us -> 104 us (0.954)
  Pallas kernels: 0 us -> 7.48 us
  starting transfers between devices: 17.6 us -> 11.3 us
  blocking collectives: 59.4 us -> 64.4 us
  matrix products: 4.24 us -> 0 us
  other arithmetic: 3.84 us -> 0.19 us
  waiting for transfers between devices: 16.3 us -> 14.6 us
  local copies, waits for them, and re-layouts: 6.28 us -> 5.04 us
    all_gather x1 -> x2, blocking collectives: 6.97 us -> 21.5 us  [the longest x1 12.5 us: on_device(): lax.all_gather(halves[0].reshape(384, 512), 'core', axis=0, tiled=True)]
    all_to_all x3, blocking collectives: 52.5 us -> 42.9 us  [the longest x1 16.6 us: on_device(): got = lax.all_to_all(part.reshape(12, 8, 512), 'z', 0, 0, tiled=True)]
    pallas_call x0 -> x5, Pallas kernels: none -> 7.48 us  [the longest x1 3.19 us: on_device(): pl.pallas_call(rotate_kernel, out_shape=jax.ShapeDtypeStruct((2, 4, 96, 5...]
    all_to_all x1, starting transfers between devices: 14.4 us -> 7.81 us  [on_device(): got = lax.all_to_all(sent, ('y_lo', 'y_hi', 'x'), 0, 0, tiled=True)]
    dot_general x7 -> x0, matrix products: 4.24 us -> none  [the longest x1 1.49 us: on_device(): jnp.einsum('ba,rad->rbd', sub_float, mixed, precision=lax.Precision.HIGHEST)]
    all_to_all x1, waiting for transfers between devices: 12.1 us -> 8.76 us  [on_device(): got = lax.all_to_all(sent, ('y_lo', 'y_hi', 'x'), 0, 0, tiled=True)]
    unnamed x14 -> x20, local copies, waits for them, and re-layouts: 0.29 us -> 3.45 us
    gather x2 -> x0, local copies, waits for them, and re-layouts: 2.01 us -> none  [the longest x1 1.45 us: on_device(): jnp.take(sign_cols, owned_blocks, axis=0)]
  transfers between devices with their start and end apart: 2 -> 2, of which waited for: 2 -> 2; matrix products, arithmetic and copies ran while one was open for 2% -> 0% of each run, Pallas kernels for 0% -> 1%
where the time goes in v3:
time: 104 us
  blocking collectives  64.4 us (62%)
  waiting for transfers between devices  14.6 us (14%)
  starting transfers between devices  11.3 us (11%)
  Pallas kernels  7.48 us (7%)
  local copies, waits for them, and re-layouts  5.04 us (5%)
    all_to_all x1, blocking collectives, on_device(): got = lax.all_to_all(part.reshape(12, 8, 512), 'z', 0, 0, tiled=True)  16.6 us
    all_to_all x1, blocking collectives, on_device(): got = lax.all_to_all(sent, ('y_lo', 'z'), 0, 0, tiled=True)  16 us
    all_gather x1, blocking collectives, on_device(): lax.all_gather(halves[0].reshape(384, 512), 'core', axis=0, tiled=True)  12.5 us
    all_to_all x1, blocking collectives, on_device(): got = lax.all_to_all(part, 'x', 0, 0, tiled=True)  10.4 us
    all_gather x1, blocking collectives, on_device(): lax.all_gather(got.reshape(1536, LANE), 'core', axis=0, tiled=True)  8.94 us
    all_to_all x1, waiting for transfers between devices, on_device(): got = lax.all_to_all(sent, ('y_lo', 'y_hi', 'x'), 0, 0, tiled=True)  8.76 us
    all_to_all x1, starting transfers between devices, on_device(): got = lax.all_to_all(sent, ('y_lo', 'y_hi', 'x'), 0, 0, tiled=True)  7.81 us
    all_to_all x1, waiting for transfers between devices, on_device(): got = lax.all_to_all(sent, 'x', 0, 0, tiled=True)  5.86 us
  transfers between devices with their start and end apart: 2, of which 2 were waited for; matrix products, arithmetic and copies ran while one was open for 0% of the time, Pallas kernels for 1%

profile of v3, /device:TPU:1, one launch (start us, length us, event | category | flops | bytes accessed | tf_op | source)
XLA Modules:
  0.0 103.7 jit_solution(11232876554333000342)
XLA Ops:
  0.6 0.0 copy-start
  0.6 1.1 %copy-done = bf16[1,192,2048]{2,1,0:T(8,128)(2,1)S(1)} copy-done((bf16[1,192,2048]{2,1,0:T(8,128)(2,1)S(1)}, bf16[1,192,2048]{2,1,0:T(8,128)(2,1)}, u32[]{:S(2)}) %copy-start) | copy-done | bytes 786456
  1.8 0.0 copy-start.1
  1.8 0.9 copy-done.1
  2.7 0.0 copy-start.3
  2.7 0.7 copy-done.3
  3.4 0.0 copy-start.8
  3.4 0.7 copy-done.8
  4.1 3.2 %rotate.1 = bf16[2,4,96,512]{3,2,1,0:T(8,128)(2,1)S(1)} custom-call(s32[1,192]{1,0:T(1,128)S(1)} %bitcast.51, s32[16,192]{1,0:T(8,128)S(1)} %bitcast.46, s32[192,128]{1,0:T(8,128)S(1)} %copy-done.1, bf16[192,2048]{1,0:T(8,128)(2,1)S(1)} %bitcast.45), custom_call_target="tpu_custom_call" | custom-call | tf_op jit(solution)/shard_map/rotate/pallas_call | solution.py:150
  7.3 12.5 %all_gather.6 = bf16[768,512]{1,0:T(8,128)(2,1)S(1)} all-gather(bf16[384,512]{1,0:T(8,128)(2,1)S(1)} %bitcast.55), channel_id=1, replica_groups=mesh['y_lo'=4,'z'=12,'core'=2,'y_hi'=2,'x'=4] {'core'}, dimensions={0}, use_global_device_ids=true | all-gather | bytes 1179648 | tf_op jit(solution)/shard_map/all_gather | solution.py:158
  19.8 0.1 fusion
  19.9 0.0 copy-start.9
  19.9 0.0 copy-start.2
  19.9 0.0 copy-start.4
  20.0 0.0 copy-start.5
  20.0 0.0 copy-start.6
  20.0 0.0 copy-start.7
  20.0 10.4 %all_to_all.25 = bf16[4,96,512]{2,1,0:T(8,128)(2,1)S(1)} all-to-all(bf16[4,96,512]{2,1,0:T(8,128)(2,1)S(1)} %fusion), channel_id=1, replica_groups=mesh['y_lo'=4,'z'=12,'core'=2,'y_hi'=2,'x'=4] {'x'}, dimensions={0} | all-to-all | bytes 786432 | tf_op jit(solution)/shard_map/all_to_all | solution.py:161
  30.3 0.1 reduce_sum.21
  30.4 16.6 %all_to_all.26 = bf16[12,8,512]{2,1,0:T(8,128)(2,1)S(1)} all-to-all(bf16[12,8,512]{2,1,0:T(8,128)(2,1)S(1)} %bitcast.56), channel_id=1, replica_groups=mesh['y_lo'=4,'z'=12,'core'=2,'y_hi'=2,'x'=4] {'z'}, dimensions={0} | all-to-all | bytes 196608 | tf_op jit(solution)/shard_map/all_to_all | solution.py:163
  47.1 0.7 broadcast_in_dim.15
  47.7 7.8 %all-to-all-start.2 = ((f32[32,8,128]{2,1,0:T(8,128)}), f32[32,8,128]{2,1,0:T(8,128)S(1)}, u32[]{:S(2)}, u32[]{:S(2)}) async-start(f32[32,8,128]{2,1,0:T(8,128)} %bitcast.9), calls=%async_computation.2 | async-start | bytes 262144 | tf_op jit(solution)/shard_map/all_to_all | solution.py:167
  55.6 0.0 copy-done.9
  55.6 0.1 dynamic_slice.8.owned_ref
  55.6 0.0 copy-done.2
  55.6 0.0 copy-done.4
  55.6 0.7 owned_signs.1.signs_ref
  56.4 8.8 %all-to-all-done.2.got_ref = f32[32,8,128]{2,1,0:T(8,128)S(1)} async-done(((f32[32,8,128]{2,1,0:T(8,128)}), f32[32,8,128]{2,1,0:T(8,128)S(1)}, u32[]{:S(2)}, u32[]{:S(2)}) %all-to-all-start.2) | async-done | bytes 131104 | tf_op jit(solution)/shard_map/all_to_all | solution.py:167
  65.1 0.0 copy-done.5
  65.1 0.0 copy-done.6
  65.1 0.0 copy-done.7
  65.1 1.0 adam.1
  66.1 16.0 %all_to_all.27 = bf16[48,8,128]{2,1,0:T(8,128)(2,1)S(1)} all-to-all(bf16[48,8,128]{2,1,0:T(8,128)(2,1)S(1)} %get-tuple-element.11), channel_id=1, replica_groups=mesh['y_lo'=4,'z'=12,'core'=2,'y_hi'=2,'x'=4] {'y_lo','z'}, dimensions={0} | all-to-all | bytes 196608 | tf_op jit(solution)/shard_map/all_to_all | solution.py:198
  82.1 0.8 broadcast_in_dim.17
  82.9 3.5 %all-to-all-start.4 = ((bf16[4,384,128]{2,1,0:T(8,128)(2,1)}), bf16[4,384,128]{2,1,0:T(8,128)(2,1)S(1)}, u32[]{:S(2)}, u32[]{:S(2)}) async-start(bf16[4,384,128]{2,1,0:T(8,128)(2,1)} %broadcast_in_dim.17), calls=%async_computation.4 | async-start | bytes 786432 | tf_op jit(solution)/shard_map/all_to_all | solution.py:200
  86.3 0.3 place.1.place_ref
  86.7 5.9 %all-to-all-done.4 = bf16[4,384,128]{2,1,0:T(8,128)(2,1)S(1)} async-done(((bf16[4,384,128]{2,1,0:T(8,128)(2,1)}), bf16[4,384,128]{2,1,0:T(8,128)(2,1)S(1)}, u32[]{:S(2)}, u32[]{:S(2)}) %all-to-all-start.4) | async-done | bytes 393248 | tf_op jit(solution)/shard_map/all_to_all | solution.py:200
  92.5 8.9 %all_gather.7 = bf16[3072,128]{1,0:T(8,128)(2,1)S(1)} all-gather(bf16[1536,128]{1,0:T(8,128)(2,1)S(1)} %bitcast.54), channel_id=1, replica_groups=mesh['y_lo'=4,'z'=12,'core'=2,'y_hi'=2,'x'=4] {'core'}, dimensions={0}, use_global_device_ids=true | all-gather | bytes 1179648 | tf_op jit(solution)/shard_map/all_gather | solution.py:201
  101.5 2.3 %params.1 = bf16[192,2048]{1,0:T(8,128)(2,1)} custom-call(bf16[768,768]{1,0:T(8,128)(2,1)S(1)} %place.1.place_ref, bf16[2,4,384,128]{3,2,1,0:T(8,128)(2,1)S(1)} %bitcast.44), custom_call_target="tpu_custom_call" | custom-call | tf_op jit(solution)/shard_map/params/pallas_call | solution.py:212
  (4 shorter events, 0.1 us)
Async XLA Ops:
  0.6 1.1 %copy-start = (bf16[1,192,2048]{2,1,0:T(8,128)(2,1)S(1)}, bf16[1,192,2048]{2,1,0:T(8,128)(2,1)}, u32[]{:S(2)}) copy-start(bf16[1,192,2048]{2,1,0:T(8,128)(2,1)} %param.7) | copy-start | bytes 2359300
  1.8 0.9 copy-start.1
  2.7 0.7 copy-start.3
  3.4 0.7 copy-start.8
  19.9 35.6 %copy-start.9 = (s32[192]{0:T(256)S(1)}, s32[192]{0:T(256)}, u32[]{:S(2)}) copy-start(s32[192]{0:T(256)} %param.10) | copy-start | bytes 2308
  19.9 35.7 %copy-start.2 = (s32[192,128]{1,0:T(8,128)S(1)}, s32[192,128]{1,0:T(8,128)}, u32[]{:S(2)}) copy-start(s32[192,128]{1,0:T(8,128)} %cols_ref.3) | copy-start | bytes 294916
  19.9 35.7 %copy-start.4 = (s32[192,16]{0,1:T(8,128)S(1)}, s32[192,16]{0,1:T(8,128)}, u32[]{:S(2)}) copy-start(s32[192,16]{0,1:T(8,128)} %param.8) | copy-start | bytes 36868
  20.0 45.2 %copy-start.5 = (f32[2,2048]{1,0:T(2,128)S(1)}, f32[2,2048]{1,0:T(2,128)}, u32[]{:S(2)}) copy-start(f32[2,2048]{1,0:T(2,128)} %param.11) | copy-start | bytes 49156
  20.0 45.2 %copy-start.6 = (f32[2,2048]{1,0:T(2,128)S(1)}, f32[2,2048]{1,0:T(2,128)}, u32[]{:S(2)}) copy-start(f32[2,2048]{1,0:T(2,128)} %param.12) | copy-start | bytes 49156
  20.0 45.2 %copy-start.7 = (f32[2,2048]{1,0:T(2,128)S(1)}, f32[2,2048]{1,0:T(2,128)}, u32[]{:S(2)}) copy-start(f32[2,2048]{1,0:T(2,128)} %param.13) | copy-start | bytes 49156
  47.7 17.4 %all-to-all-start.2 = ((f32[32,8,128]{2,1,0:T(8,128)}), f32[32,8,128]{2,1,0:T(8,128)S(1)}, u32[]{:S(2)}, u32[]{:S(2)}) async-start(f32[32,8,128]{2,1,0:T(8,128)} %bitcast.9), calls=%async_computation.2 | async-start | bytes 262144 | tf_op jit(solution)/shard_map/all_to_all | solution.py:167
  82.9 9.7 %all-to-all-start.4 = ((bf16[4,384,128]{2,1,0:T(8,128)(2,1)}), bf16[4,384,128]{2,1,0:T(8,128)(2,1)S(1)}, u32[]{:S(2)}, u32[]{:S(2)}) async-start(bf16[4,384,128]{2,1,0:T(8,128)(2,1)} %broadcast_in_dim.17), calls=%async_computation.4 | async-start | bytes 786432 | tf_op jit(solution)/shard_map/all_to_all | solution.py:200

commit v4 on v3

--- a/solution.py
+++ b/solution.py
@@ -36,7 +36,20 @@
     return (1 - 2 * (both & 1)).astype(F32)
 
 
-def rotate_kernel(order_ref, rows_ref, cols_ref, grad_ref, out_ref):
+def rotate_kernel(order_hbm, rows_hbm, cols_hbm, grad_hbm, out_ref, order_ref, rows_ref, cols_ref, grad_ref, mixed_ref, sems):
+    small = [
+        pltpu.make_async_copy(order_hbm, order_ref, sems.at[0]),
+        pltpu.make_async_copy(rows_hbm, rows_ref, sems.at[1]),
+        pltpu.make_async_copy(cols_hbm, cols_ref, sems.at[2]),
+    ]
+    large = [
+        pltpu.make_async_copy(
+            grad_hbm.at[:, k * 512 : (k + 1) * 512], grad_ref.at[:, k * 512 : (k + 1) * 512], sems.at[3 + k]
+        )
+        for k in range(4)
+    ]
+    for copy in small + large:
+        copy.start()
     core = lax.axis_index("core")
     row = iota((BLOCKS, BLOCKS), 0)
     lane = iota((BLOCKS, BLOCKS), 1)
@@ -46,6 +59,9 @@
     z = jnp.right_shift(place, 3)
     owner = jnp.where(half == 1, core, 1 - core)
     slot = ((y_lo * 12 + z) * 2 + owner) * 2 + (place & 1)
+    table = parity_sign(iota((256, 256), 0) & iota((256, 256), 1), (4, 2, 1)).astype(BF16)
+    for copy in small:
+        copy.wait()
     order = order_ref[...].astype(F32)
     block = jnp.sum(jnp.where(slot == lane, order, 0.0), axis=1, keepdims=True)
     pick = jnp.where(block == lane.astype(F32), 1.0, 0.0).astype(BF16)
@@ -53,24 +69,40 @@
     col_bits = (2 * cols_ref[...] - 1).astype(F32).astype(BF16)
     row_signs = lax.dot_general(pick, row_bits, (((1,), (1,)), ((), ())), preferred_element_type=F32)
     col_signs = jnp.dot(pick, col_bits, preferred_element_type=F32)
-    table = parity_sign(iota((LANE, LANE), 0) & iota((LANE, LANE), 1), (4, 2, 1)).astype(BF16)
-    mixed = []
-    for a in range(16):
-        picked = jnp.dot(pick, grad_ref[:, a * LANE : (a + 1) * LANE], preferred_element_type=F32)
-        signed = (picked * col_signs * row_signs[:, a : a + 1]).astype(BF16)
-        mixed.append(jnp.dot(signed, table, preferred_element_type=F32))
-    span = 1
-    while span < 16:
-        for a in range(16):
-            if not a & span:
-                low, high = mixed[a], mixed[a + span]
-                mixed[a], mixed[a + span] = low + high, low - high
-        span *= 2
-    for a in range(16):
-        rotated = (mixed[a] * INV_ROOT).astype(BF16)
-        quarter, column = a // 4, (a % 4) * LANE
-        out_ref[0, quarter, :, column : column + LANE] = rotated[:96]
-        out_ref[1, quarter, :, column : column + LANE] = rotated[96:]
+    for k in range(8):
+        if k % 2 == 0:
+            large[k // 2].wait()
+        picked = jnp.dot(pick, grad_ref[:, k * 256 : (k + 1) * 256], preferred_element_type=F32)
+        signed = jnp.concatenate(
+            [
+                picked[:, :LANE] * col_signs * row_signs[:, 2 * k : 2 * k + 1],
+                picked[:, LANE:] * col_signs * row_signs[:, 2 * k + 1 : 2 * k + 2],
+            ],
+            axis=1,
+        ).astype(BF16)
+        mixed_ref[k] = jnp.dot(signed, table, preferred_element_type=F32)
+    for start in range(0, BLOCKS, 16):
+        mixed = [mixed_ref[k, start : start + 16] for k in range(8)]
+        for span in (1, 2, 4):
+            for k in range(8):
+                if not k & span:
+                    low, high = mixed[k], mixed[k + span]
+                    mixed[k], mixed[k + span] = low + high, low - high
+        for k in range(8):
+            rotated = (mixed[k] * INV_ROOT).astype(BF16)
+            out_ref[start // 96, k // 2, start % 96 : start % 96 + 16, (k % 2) * 256 : (k % 2) * 256 + 256] = rotated
+
+
+def owner_sum_kernel(got_ref, out_ref):
+    total = got_ref[0].astype(F32)
+    for z in range(1, 12):
+        total = total + got_ref[z].astype(F32)
+    for y_lo in range(4):
+        piece = jnp.concatenate(
+            [total[2 * y_lo : 2 * y_lo + 2, a * LANE : (a + 1) * LANE] for a in range(4)], axis=0
+        )
+        for member in range(8):
+            out_ref[8 * y_lo + member] = piece
 
 
 def owned_signs_kernel(owned_ref, rows_ref, cols_ref, out_ref):
@@ -115,30 +147,46 @@
 
 
 def place_kernel(order_ref, out_ref):
-    col = iota((BLOCKS, 768), 1)
-    core = (col >= 384).astype(jnp.int32)
-    rest = col - 384 * core
-    slot = (jnp.right_shift(rest, 3) * 2 + core) * 2 + (rest & 1)
-    spread = jnp.where(iota((BLOCKS, 768), 0) == slot, 1.0, 0.0).astype(BF16)
+    col = iota((BLOCKS, BLOCKS), 1)
+    core = (col >= 96).astype(jnp.int32)
+    rest = col - 96 * core
+    j = (rest >= 48).astype(jnp.int32)
+    slot = ((rest - 48 * j) * 2 + core) * 2 + j
+    spread = jnp.where(iota((BLOCKS, BLOCKS), 0) == slot, 1.0, 0.0).astype(BF16)
     order = jnp.broadcast_to(order_ref[...].astype(F32), (8, BLOCKS)).astype(BF16)
     block = jnp.dot(order, spread, preferred_element_type=F32)[0:1]
-    match = iota((BLOCKS, 768), 0).astype(F32) == block
-    part = jnp.right_shift(rest, 1) & 3
+    out_ref[...] = jnp.where(iota((BLOCKS, BLOCKS), 0).astype(F32) == block, 1.0, 0.0).astype(BF16)
+
+
+def repeat_kernel(got_ref, out_ref, wide_ref):
+    wide_ref[...] = got_ref[...].astype(F32)
     for a in range(4):
-        out_ref[a * BLOCKS : (a + 1) * BLOCKS, :] = jnp.where(match & (part == a), 1.0, 0.0).astype(BF16)
-
-
-def params_kernel(place_ref, got_ref, out_ref):
+        rows = jnp.concatenate(
+            [wide_ref[pl.ds(2 * a + j, 48, stride=8), :] for j in range(2)], axis=0
+        ).astype(BF16)
+        for x in range(4):
+            out_ref[x, :, a * LANE : (a + 1) * LANE] = rows
+
+
+def params_kernel(place_ref, got_ref, out_hbm, out_ref, sems):
+    copies = []
     for x in range(4):
         rows = jnp.concatenate([got_ref[0, x], got_ref[1, x]], axis=0)
-        placed = jnp.dot(place_ref[...], rows, preferred_element_type=F32).astype(BF16)
-        for a in range(4):
-            column = (4 * x + a) * LANE
-            out_ref[:, column : column + LANE] = placed[a * BLOCKS : (a + 1) * BLOCKS]
+        column = x * 512
+        placed = jnp.dot(place_ref[...], rows, preferred_element_type=F32)
+        out_ref[:, column : column + 512] = placed.astype(BF16)
+        copy = pltpu.make_async_copy(
+            out_ref.at[:, column : column + 512], out_hbm.at[:, column : column + 512], sems.at[x]
+        )
+        copy.start()
+        copies.append(copy)
+    for copy in copies:
+        copy.wait()
 
 
 VMEM = pl.BlockSpec(memory_space=pltpu.VMEM)
 SMEM = pl.BlockSpec(memory_space=pltpu.SMEM)
+HBM = pl.BlockSpec(memory_space=pltpu.HBM)
 ROOM = pltpu.CompilerParams(vmem_limit_bytes=32 * 1024 * 1024)
 
 
@@ -150,8 +198,16 @@
     halves = pl.pallas_call(
         rotate_kernel,
         out_shape=jax.ShapeDtypeStruct((2, 4, 96, 512), BF16),
-        in_specs=[VMEM] * 4,
-        out_specs=VMEM,
+        in_specs=[HBM] * 4,
+        out_specs=VMEM,
+        scratch_shapes=[
+            pltpu.VMEM((1, BLOCKS), jnp.int32),
+            pltpu.VMEM((16, BLOCKS), jnp.int32),
+            pltpu.VMEM((BLOCKS, LANE), jnp.int32),
+            pltpu.VMEM((BLOCKS, BLOCK), BF16),
+            pltpu.VMEM((8, BLOCKS, 256), F32),
+            pltpu.SemaphoreType.DMA((7,)),
+        ],
         compiler_params=ROOM,
         name="rotate",
     )(order_row, rows_t, sign_cols, grads[0])
@@ -161,9 +217,14 @@
     got = lax.all_to_all(part, "x", 0, 0, tiled=True)
     part = jnp.sum(got.astype(F32), axis=0).astype(BF16)
     got = lax.all_to_all(part.reshape(12, 8, 512), "z", 0, 0, tiled=True)
-    part = jnp.sum(got.astype(F32), axis=0)
-    part = part.reshape(4, 2, 4, LANE).transpose(0, 2, 1, 3).reshape(4, 1, 8, LANE)
-    sent = jnp.broadcast_to(part, (4, 8, 8, LANE)).reshape(32, 8, LANE)
+    sent = pl.pallas_call(
+        owner_sum_kernel,
+        out_shape=jax.ShapeDtypeStruct((32, 8, LANE), F32),
+        in_specs=[VMEM],
+        out_specs=VMEM,
+        compiler_params=ROOM,
+        name="owner_sum",
+    )(got)
     got = lax.all_to_all(sent, ("y_lo", "y_hi", "x"), 0, 0, tiled=True)
 
     owner = (lax.axis_index("y_lo") * 12 + lax.axis_index("z")) * 2 + core
@@ -196,13 +257,21 @@
     )(got, signs, by_row(master), by_row(first_moment), by_row(second_moment))
 
     got = lax.all_to_all(sent, ("y_lo", "z"), 0, 0, tiled=True)
-    sent = jnp.broadcast_to(got.reshape(1, 384, LANE), (4, 384, LANE))
+    sent = pl.pallas_call(
+        repeat_kernel,
+        out_shape=jax.ShapeDtypeStruct((4, 96, 512), BF16),
+        in_specs=[VMEM],
+        out_specs=VMEM,
+        scratch_shapes=[pltpu.VMEM((384, LANE), F32)],
+        compiler_params=ROOM,
+        name="repeat",
+    )(got.reshape(384, LANE))
     got = lax.all_to_all(sent, "x", 0, 0, tiled=True)
-    got = lax.all_gather(got.reshape(1536, LANE), "core", axis=0, tiled=True).reshape(2, 4, 384, LANE)
+    got = lax.all_gather(got.reshape(384, 512), "core", axis=0, tiled=True).reshape(2, 4, 96, 512)
 
     place = pl.pallas_call(
         place_kernel,
-        out_shape=jax.ShapeDtypeStruct((768, 768), BF16),
+        out_shape=jax.ShapeDtypeStruct((BLOCKS, BLOCKS), BF16),
         in_specs=[VMEM],
         out_specs=VMEM,
         compiler_params=ROOM,
@@ -213,7 +282,8 @@
         params_kernel,
         out_shape=jax.ShapeDtypeStruct((BLOCKS, BLOCK), BF16),
         in_specs=[VMEM] * 2,
-        out_specs=VMEM,
+        out_specs=HBM,
+        scratch_shapes=[pltpu.VMEM((BLOCKS, BLOCK), BF16), pltpu.SemaphoreType.DMA((4,))],
         compiler_params=ROOM,
         name="params",
     )(place, got)

time: 104 us -> 102 us (0.981)
    broadcast_in_dim x2 -> x0, local copies, waits for them, and re-layouts: 1.46 us -> none  [the longest x1 0.8 us: on_device(): sent = jnp.broadcast_to(got.reshape(1, 384, LANE), (4, 384, LANE))]
    pallas_call x1 -> x3, Pallas kernels: 0.33 us -> 1.69 us  [the longest x1 0.84 us: on_device(): pl.pallas_call(repeat_kernel, out_shape=jax.ShapeDtypeStruct((4, 96, 512)...]
    pallas_call x1, Pallas kernels: 2.26 us -> 1.11 us  [on_device(): pl.pallas_call(params_kernel, out_shape=jax.ShapeDtypeStruct((BLOCKS, BLO...]
    unnamed x20 -> x18, local copies, waits for them, and re-layouts: 3.45 us -> 4.04 us
where the time goes in v4:
time: 102 us
  blocking collectives  64.2 us (63%)
  waiting for transfers between devices  14.2 us (14%)
  starting transfers between devices  11.4 us (11%)
  Pallas kernels  6.93 us (7%)
  local copies, waits for them, and re-layouts  4.15 us (4%)
    all_to_all x1, blocking collectives, on_device(): got = lax.all_to_all(part.reshape(12, 8, 512), 'z', 0, 0, tiled=True)  16.6 us
    all_to_all x1, blocking collectives, on_device(): got = lax.all_to_all(sent, ('y_lo', 'z'), 0, 0, tiled=True)  16 us
    all_gather x1, blocking collectives, on_device(): lax.all_gather(halves[0].reshape(384, 512), 'core', axis=0, tiled=True)  12.5 us
    all_to_all x1, blocking collectives, on_device(): got = lax.all_to_all(part, 'x', 0, 0, tiled=True)  10.2 us
    all_gather x1, blocking collectives, on_device(): lax.all_gather(got.reshape(384, 512), 'core', axis=0, tiled=True)  8.94 us
    all_to_all x1, waiting for transfers between devices, on_device(): got = lax.all_to_all(sent, ('y_lo', 'y_hi', 'x'), 0, 0, tiled=True)  8.14 us
    all_to_all x1, starting transfers between devices, on_device(): got = lax.all_to_all(sent, ('y_lo', 'y_hi', 'x'), 0, 0, tiled=True)  7.95 us
    all_to_all x1, waiting for transfers between devices, on_device(): got = lax.all_to_all(sent, 'x', 0, 0, tiled=True)  6.02 us
  transfers between devices with their start and end apart: 2, of which 2 were waited for; matrix products, arithmetic and copies ran while one was open for 0% of the time, Pallas kernels for 1%

profile of v4, /device:TPU:1, one launch (start us, length us, event | category | flops | bytes accessed | tf_op | source)
XLA Modules:
  0.0 101.8 jit_solution(6854381910867044457)
XLA Ops:
  0.6 0.0 copy-start.8
  0.6 0.7 copy-done.8
  1.3 0.0 copy-start
  1.3 1.1 %copy-done = bf16[1,192,2048]{2,1,0:T(8,128)(2,1)S(1)} copy-done((bf16[1,192,2048]{2,1,0:T(8,128)(2,1)S(1)}, bf16[1,192,2048]{2,1,0:T(8,128)(2,1)}, u32[]{:S(2)}) %copy-start) | copy-done | bytes 786456
  2.4 0.0 copy-start.1
  2.5 0.9 copy-done.1
  3.3 0.0 copy-start.3
  3.3 0.7 copy-done.3
  4.1 2.4 %rotate.1 = bf16[2,4,96,512]{3,2,1,0:T(8,128)(2,1)S(1)} custom-call(s32[1,192]{1,0:T(1,128)S(1)} %bitcast.49, s32[16,192]{1,0:T(8,128)S(1)} %bitcast.44, s32[192,128]{1,0:T(8,128)S(1)} %copy-done.1, bf16[192,2048]{1,0:T(8,128)(2,1)S(1)} %bitcast.42), custom_call_target="tpu_custom_call" | custom-call | tf_op jit(solution)/shard_map/rotate/pallas_call | solution.py:198
  6.5 12.5 %all_gather.6 = bf16[768,512]{1,0:T(8,128)(2,1)S(1)} all-gather(bf16[384,512]{1,0:T(8,128)(2,1)S(1)} %bitcast.53), channel_id=1, replica_groups=mesh['y_lo'=4,'z'=12,'core'=2,'y_hi'=2,'x'=4] {'core'}, dimensions={0}, use_global_device_ids=true | all-gather | bytes 1179648 | tf_op jit(solution)/shard_map/all_gather | solution.py:214
  19.1 0.1 fusion
  19.2 10.2 %all_to_all.25 = bf16[4,96,512]{2,1,0:T(8,128)(2,1)S(1)} all-to-all(bf16[4,96,512]{2,1,0:T(8,128)(2,1)S(1)} %fusion), channel_id=1, replica_groups=mesh['y_lo'=4,'z'=12,'core'=2,'y_hi'=2,'x'=4] {'x'}, dimensions={0} | all-to-all | bytes 786432 | tf_op jit(solution)/shard_map/all_to_all | solution.py:217
  29.4 0.1 reduce_sum.12
  29.4 16.6 %all_to_all.26.got_ref = bf16[12,8,512]{2,1,0:T(8,128)(2,1)S(1)} all-to-all(bf16[12,8,512]{2,1,0:T(8,128)(2,1)S(1)} %bitcast.54), channel_id=1, replica_groups=mesh['y_lo'=4,'z'=12,'core'=2,'y_hi'=2,'x'=4] {'z'}, dimensions={0} | all-to-all | bytes 196608 | tf_op jit(solution)/shard_map/all_to_all | solution.py:219
  46.0 0.7 owner_sum.1
  46.7 0.0 copy-start.2
  46.7 7.9 %all-to-all-start.2 = ((f32[32,8,128]{2,1,0:T(8,128)}), f32[32,8,128]{2,1,0:T(8,128)S(1)}, u32[]{:S(2)}, u32[]{:S(2)}) async-start(f32[32,8,128]{2,1,0:T(8,128)} %owner_sum.1), calls=%async_computation.2 | async-start | bytes 262144 | tf_op jit(solution)/shard_map/all_to_all | solution.py:228
  54.7 0.0 copy-start.4
  54.7 0.1 dynamic_slice.8.owned_ref
  54.8 0.0 copy-done.2
  54.8 0.6 copy-done.4
  55.4 0.0 copy-start.5
  55.4 0.0 copy-start.6
  55.4 0.0 copy-start.7
  55.4 0.7 owned_signs.1.signs_ref
  56.1 8.1 %all-to-all-done.2.got_ref = f32[32,8,128]{2,1,0:T(8,128)S(1)} async-done(((f32[32,8,128]{2,1,0:T(8,128)}), f32[32,8,128]{2,1,0:T(8,128)S(1)}, u32[]{:S(2)}, u32[]{:S(2)}) %all-to-all-start.2) | async-done | bytes 131104 | tf_op jit(solution)/shard_map/all_to_all | solution.py:228
  64.3 0.0 copy-done.5
  64.3 0.0 copy-done.6
  64.3 0.0 copy-done.7
  64.3 1.0 adam.1
  65.2 16.0 %all_to_all.27 = bf16[48,8,128]{2,1,0:T(8,128)(2,1)S(1)} all-to-all(bf16[48,8,128]{2,1,0:T(8,128)(2,1)S(1)} %get-tuple-element.11), channel_id=1, replica_groups=mesh['y_lo'=4,'z'=12,'core'=2,'y_hi'=2,'x'=4] {'y_lo','z'}, dimensions={0} | all-to-all | bytes 196608 | tf_op jit(solution)/shard_map/all_to_all | solution.py:259
  81.2 0.8 repeat.1
  82.1 3.5 %all-to-all-start.4 = ((bf16[4,96,512]{2,1,0:T(8,128)(2,1)}), bf16[4,96,512]{2,1,0:T(8,128)(2,1)S(1)}, u32[]{:S(2)}, u32[]{:S(2)}) async-start(bf16[4,96,512]{2,1,0:T(8,128)(2,1)} %repeat.1), calls=%async_computation.4 | async-start | bytes 786432 | tf_op jit(solution)/shard_map/all_to_all | solution.py:269
  85.5 0.2 place.1.place_ref
  85.7 6.0 %all-to-all-done.4 = bf16[4,96,512]{2,1,0:T(8,128)(2,1)S(1)} async-done(((bf16[4,96,512]{2,1,0:T(8,128)(2,1)}), bf16[4,96,512]{2,1,0:T(8,128)(2,1)S(1)}, u32[]{:S(2)}, u32[]{:S(2)}) %all-to-all-start.4) | async-done | bytes 393248 | tf_op jit(solution)/shard_map/all_to_all | solution.py:269
  91.7 8.9 %all_gather.7 = bf16[768,512]{1,0:T(8,128)(2,1)S(1)} all-gather(bf16[384,512]{1,0:T(8,128)(2,1)S(1)} %bitcast.52), channel_id=1, replica_groups=mesh['y_lo'=4,'z'=12,'core'=2,'y_hi'=2,'x'=4] {'core'}, dimensions={0}, use_global_device_ids=true | all-gather | bytes 1179648 | tf_op jit(solution)/shard_map/all_gather | solution.py:270
  100.7 1.1 %params.1 = bf16[192,2048]{1,0:T(8,128)(2,1)} custom-call(bf16[192,192]{1,0:T(8,128)(2,1)S(1)} %place.1.place_ref, bf16[2,4,96,512]{3,2,1,0:T(8,128)(2,1)S(1)} %bitcast.41), custom_call_target="tpu_custom_call" | custom-call | tf_op jit(solution)/shard_map/params/pallas_call | solution.py:281
  (1 shorter events, 0.0 us)
Async XLA Ops:
  0.6 0.7 copy-start.8
  1.3 1.1 %copy-start = (bf16[1,192,2048]{2,1,0:T(8,128)(2,1)S(1)}, bf16[1,192,2048]{2,1,0:T(8,128)(2,1)}, u32[]{:S(2)}) copy-start(bf16[1,192,2048]{2,1,0:T(8,128)(2,1)} %param.7) | copy-start | bytes 2359300
  2.4 0.9 copy-start.1
  3.3 0.7 copy-start.3
  46.7 8.1 %copy-start.2 = (s32[192,128]{1,0:T(8,128)S(1)}, s32[192,128]{1,0:T(8,128)}, u32[]{:S(2)}) copy-start(s32[192,128]{1,0:T(8,128)} %cols_ref.1) | copy-start | bytes 294916
  46.7 17.6 %all-to-all-start.2 = ((f32[32,8,128]{2,1,0:T(8,128)}), f32[32,8,128]{2,1,0:T(8,128)S(1)}, u32[]{:S(2)}, u32[]{:S(2)}) async-start(f32[32,8,128]{2,1,0:T(8,128)} %owner_sum.1), calls=%async_computation.2 | async-start | bytes 262144 | tf_op jit(solution)/shard_map/all_to_all | solution.py:228
  54.7 0.7 copy-start.4
  55.4 8.9 %copy-start.5 = (f32[2,2048]{1,0:T(2,128)S(1)}, f32[2,2048]{1,0:T(2,128)}, u32[]{:S(2)}) copy-start(f32[2,2048]{1,0:T(2,128)} %param.11) | copy-start | bytes 49156
  55.4 8.9 %copy-start.6 = (f32[2,2048]{1,0:T(2,128)S(1)}, f32[2,2048]{1,0:T(2,128)}, u32[]{:S(2)}) copy-start(f32[2,2048]{1,0:T(2,128)} %param.12) | copy-start | bytes 49156
  55.4 8.9 %copy-start.7 = (f32[2,2048]{1,0:T(2,128)S(1)}, f32[2,2048]{1,0:T(2,128)}, u32[]{:S(2)}) copy-start(f32[2,2048]{1,0:T(2,128)} %param.13) | copy-start | bytes 49156
  82.1 9.7 %all-to-all-start.4 = ((bf16[4,96,512]{2,1,0:T(8,128)(2,1)}), bf16[4,96,512]{2,1,0:T(8,128)(2,1)S(1)}, u32[]{:S(2)}, u32[]{:S(2)}) async-start(bf16[4,96,512]{2,1,0:T(8,128)(2,1)} %repeat.1), calls=%async_computation.4 | async-start | bytes 786432 | tf_op jit(solution)/shard_map/all_to_all | solution.py:269

commit v5 on v4

--- a/solution.py
+++ b/solution.py
@@ -210,13 +210,36 @@
         ],
         compiler_params=ROOM,
         name="rotate",
-    )(order_row, rows_t, sign_cols, grads[0])
+    )(*(pltpu.with_memory_space_constraint(each, pltpu.HBM) for each in (order_row, rows_t, sign_cols, grads[0])))
     got = lax.all_gather(halves[0].reshape(384, 512), "core", axis=0, tiled=True).reshape(2, 4, 96, 512)
     other = lax.dynamic_index_in_dim(got, 1 - core, 0, keepdims=False)
     part = (halves[1].astype(F32) + other.astype(F32)).astype(BF16)
     got = lax.all_to_all(part, "x", 0, 0, tiled=True)
     part = jnp.sum(got.astype(F32), axis=0).astype(BF16)
+    part, order_late, rows_late, cols_late = lax.optimization_barrier((part, block_order, rows_t, sign_cols))
     got = lax.all_to_all(part.reshape(12, 8, 512), "z", 0, 0, tiled=True)
+    owner = (lax.axis_index("y_lo") * 12 + lax.axis_index("z")) * 2 + core
+    owned = lax.dynamic_slice_in_dim(order_late, owner * 2, 2)
+    signs = pl.pallas_call(
+        owned_signs_kernel,
+        out_shape=jax.ShapeDtypeStruct((32, LANE), F32),
+        in_specs=[SMEM, VMEM, VMEM],
+        out_specs=VMEM,
+        compiler_params=ROOM,
+        cost_estimate=pl.CostEstimate(flops=2000000, bytes_accessed=200000, transcendentals=0),
+        name="owned_signs",
+    )(owned, rows_late, cols_late)
+
+    place = pl.pallas_call(
+        place_kernel,
+        out_shape=jax.ShapeDtypeStruct((BLOCKS, BLOCKS), BF16),
+        in_specs=[VMEM],
+        out_specs=VMEM,
+        compiler_params=ROOM,
+        cost_estimate=pl.CostEstimate(flops=4000000, bytes_accessed=1200000, transcendentals=0),
+        name="place",
+    )(order_late.reshape(1, BLOCKS))
+    got, signs, place = lax.optimization_barrier((got, signs, place))
     sent = pl.pallas_call(
         owner_sum_kernel,
         out_shape=jax.ShapeDtypeStruct((32, 8, LANE), F32),
@@ -226,18 +249,6 @@
         name="owner_sum",
     )(got)
     got = lax.all_to_all(sent, ("y_lo", "y_hi", "x"), 0, 0, tiled=True)
-
-    owner = (lax.axis_index("y_lo") * 12 + lax.axis_index("z")) * 2 + core
-    owned = lax.dynamic_slice_in_dim(block_order, owner * 2, 2)
-    signs = pl.pallas_call(
-        owned_signs_kernel,
-        out_shape=jax.ShapeDtypeStruct((32, LANE), F32),
-        in_specs=[SMEM, VMEM, VMEM],
-        out_specs=VMEM,
-        compiler_params=ROOM,
-        cost_estimate=pl.CostEstimate(flops=2000000, bytes_accessed=200000, transcendentals=0),
-        name="owned_signs",
-    )(owned, rows_t, sign_cols)
 
     def by_row(value):
         return value.reshape(2, 16, LANE).transpose(1, 0, 2).reshape(32, LANE)
@@ -269,15 +280,6 @@
     got = lax.all_to_all(sent, "x", 0, 0, tiled=True)
     got = lax.all_gather(got.reshape(384, 512), "core", axis=0, tiled=True).reshape(2, 4, 96, 512)
 
-    place = pl.pallas_call(
-        place_kernel,
-        out_shape=jax.ShapeDtypeStruct((BLOCKS, BLOCKS), BF16),
-        in_specs=[VMEM],
-        out_specs=VMEM,
-        compiler_params=ROOM,
-        cost_estimate=pl.CostEstimate(flops=4000000, bytes_accessed=1200000, transcendentals=0),
-        name="place",
-    )(order_row)
     params = pl.pallas_call(
         params_kernel,
         out_shape=jax.ShapeDtypeStruct((BLOCKS, BLOCK), BF16),

time: 102 us -> 97.7 us (0.958)
  blocking collectives: 64.2 us -> 73.6 us
  waiting for transfers between devices: 14.2 us -> 8.4 us
  starting transfers between devices: 11.4 us -> 6.8 us
  local copies, waits for them, and re-layouts: 4.15 us -> 0.8 us
    all_to_all x1 -> x2, blocking collectives: 16.6 us -> 26 us  [the longest x1 17.3 us: on_device(): got = lax.all_to_all(sent, ('y_lo', 'y_hi', 'x'), 0, 0, tiled=True)]
    all_to_all x2 -> x1, waiting for transfers between devices: 14.2 us -> 8.4 us  [on_device(): got = lax.all_to_all(part.reshape(12, 8, 512), 'z', 0, 0, tiled=True)]
    all_to_all x2 -> x1, starting transfers between devices: 11.4 us -> 6.8 us  [on_device(): got = lax.all_to_all(part.reshape(12, 8, 512), 'z', 0, 0, tiled=True)]
    unnamed x18 -> x12, local copies, waits for them, and re-layouts: 4.04 us -> 0.7 us
  transfers between devices with their start and end apart: 2 -> 1, of which waited for: 2 -> 1; matrix products, arithmetic and copies ran while one was open for 0% -> 0% of each run, Pallas kernels for 1% -> 1%
where the time goes in v5:
time: 97.7 us; the launch traced here: 97.2 us
  blocking collectives  73.6 us (75%)
  waiting for transfers between devices  8.4 us (9%)
  starting transfers between devices  6.8 us (7%)
  Pallas kernels  6.01 us (6%)
    all_to_all x1, blocking collectives, on_device(): got = lax.all_to_all(sent, ('y_lo', 'y_hi', 'x'), 0, 0, tiled=True)  17.3 us
    all_to_all x1, blocking collectives, on_device(): got = lax.all_to_all(sent, ('y_lo', 'z'), 0, 0, tiled=True)  16 us
    all_gather x1, blocking collectives, on_device(): lax.all_gather(halves[0].reshape(384, 512), 'core', axis=0, tiled=True)  12.5 us
    all_to_all x1, blocking collectives, on_device(): got = lax.all_to_all(part, 'x', 0, 0, tiled=True)  10.2 us
    all_gather x1, blocking collectives, on_device(): lax.all_gather(got.reshape(384, 512), 'core', axis=0, tiled=True)  8.94 us
    all_to_all x1, blocking collectives, on_device(): got = lax.all_to_all(sent, 'x', 0, 0, tiled=True)  8.62 us
    all_to_all x1, waiting for transfers between devices, on_device(): got = lax.all_to_all(part.reshape(12, 8, 512), 'z', 0, 0, tiled=True)  8.4 us
    all_to_all x1, starting transfers between devices, on_device(): got = lax.all_to_all(part.reshape(12, 8, 512), 'z', 0, 0, tiled=True)  6.8 us
  transfers between devices with their start and end apart: 1, of which 1 were waited for; matrix products, arithmetic and copies ran while one was open for 0% of the time, Pallas kernels for 1%

profile of v5, /device:TPU:1, one launch (start us, length us, event | category | flops | bytes accessed | tf_op | source)
XLA Modules:
  0.0 97.2 jit_solution(15727681868377037118)
XLA Ops:
  0.6 2.9 %rotate.1 = bf16[2,4,96,512]{3,2,1,0:T(8,128)(2,1)S(1)} custom-call(s32[1,192]{1,0:T(1,128)} %bitcast.49, s32[16,192]{1,0:T(8,128)} %bitcast.44, s32[192,128]{1,0:T(8,128)} %cols_ref, bf16[192,2048]{1,0:T(8,128)(2,1)} %bitcast.54), custom_call_target="tpu_custom_call" | custom-call | tf_op jit(solution)/shard_map/rotate/pallas_call | solution.py:198
  3.6 12.5 %all_gather.6 = bf16[768,512]{1,0:T(8,128)(2,1)S(1)} all-gather(bf16[384,512]{1,0:T(8,128)(2,1)S(1)} %bitcast.53), channel_id=1, replica_groups=mesh['y_lo'=4,'z'=12,'core'=2,'y_hi'=2,'x'=4] {'core'}, dimensions={0}, use_global_device_ids=true | all-gather | bytes 1179648 | tf_op jit(solution)/shard_map/all_gather | solution.py:214
  16.1 0.1 fusion
  16.2 10.2 %all_to_all.25 = bf16[4,96,512]{2,1,0:T(8,128)(2,1)S(1)} all-to-all(bf16[4,96,512]{2,1,0:T(8,128)(2,1)S(1)} %fusion), channel_id=1, replica_groups=mesh['y_lo'=4,'z'=12,'core'=2,'y_hi'=2,'x'=4] {'x'}, dimensions={0} | all-to-all | bytes 786432 | tf_op jit(solution)/shard_map/all_to_all | solution.py:217
  26.4 0.7 reduce_sum.12
  27.1 0.0 copy-start
  27.1 6.8 %all-to-all-start.1 = ((bf16[12,8,512]{2,1,0:T(8,128)(2,1)}), bf16[12,8,512]{2,1,0:T(8,128)(2,1)S(1)}, u32[]{:S(2)}, u32[]{:S(2)}) async-start(bf16[12,8,512]{2,1,0:T(8,128)(2,1)} %bitcast.6), calls=%async_computation.1 | async-start | bytes 196608 | tf_op jit(solution)/shard_map/all_to_all | solution.py:220
  33.9 0.0 copy-start.1
  34.0 0.0 copy-start.5
  34.0 0.7 copy-done.5
  34.7 0.1 dynamic_slice.8.owned_ref
  34.7 0.0 copy-done
  34.7 0.0 copy-done.1
  34.7 0.7 owned_signs.1.signs_ref
  35.5 0.2 place.1.place_ref
  35.7 8.4 %all-to-all-done.1.got_ref = bf16[12,8,512]{2,1,0:T(8,128)(2,1)S(1)} async-done(((bf16[12,8,512]{2,1,0:T(8,128)(2,1)}), bf16[12,8,512]{2,1,0:T(8,128)(2,1)S(1)}, u32[]{:S(2)}, u32[]{:S(2)}) %all-to-all-start.1) | async-done | bytes 98336 | tf_op jit(solution)/shard_map/all_to_all | solution.py:220
  44.1 0.0 copy-start.2
  44.1 0.0 copy-start.3
  44.1 0.0 copy-start.4
  44.1 17.3 %all_to_all.26.got_ref = f32[32,8,128]{2,1,0:T(8,128)S(1)} all-to-all(f32[32,8,128]{2,1,0:T(8,128)S(1)} %owner_sum.1), channel_id=1, replica_groups=mesh['y_lo'=4,'z'=12,'core'=2,'y_hi'=2,'x'=4] {'y_lo','y_hi','x'}, dimensions={0} | all-to-all | bytes 262144 | tf_op jit(solution)/shard_map/all_to_all | solution.py:251
  61.5 0.0 copy-done.2
  61.5 0.0 copy-done.3
  61.5 0.0 copy-done.4
  61.5 1.0 adam.1
  62.4 16.0 %all_to_all.27 = bf16[48,8,128]{2,1,0:T(8,128)(2,1)S(1)} all-to-all(bf16[48,8,128]{2,1,0:T(8,128)(2,1)S(1)} %get-tuple-element.25), channel_id=1, replica_groups=mesh['y_lo'=4,'z'=12,'core'=2,'y_hi'=2,'x'=4] {'y_lo','z'}, dimensions={0} | all-to-all | bytes 196608 | tf_op jit(solution)/shard_map/all_to_all | solution.py:270
  78.4 0.1 repeat.1
  78.5 8.6 %all_to_all.28 = bf16[4,96,512]{2,1,0:T(8,128)(2,1)S(1)} all-to-all(bf16[4,96,512]{2,1,0:T(8,128)(2,1)S(1)} %repeat.1), channel_id=1, replica_groups=mesh['y_lo'=4,'z'=12,'core'=2,'y_hi'=2,'x'=4] {'x'}, dimensions={0} | all-to-all | bytes 786432 | tf_op jit(solution)/shard_map/all_to_all | solution.py:280
  87.1 8.9 %all_gather.7 = bf16[768,512]{1,0:T(8,128)(2,1)S(1)} all-gather(bf16[384,512]{1,0:T(8,128)(2,1)S(1)} %bitcast.52), channel_id=1, replica_groups=mesh['y_lo'=4,'z'=12,'core'=2,'y_hi'=2,'x'=4] {'core'}, dimensions={0}, use_global_device_ids=true | all-gather | bytes 1179648 | tf_op jit(solution)/shard_map/all_gather | solution.py:281
  96.1 1.1 %params.1 = bf16[192,2048]{1,0:T(8,128)(2,1)} custom-call(bf16[192,192]{1,0:T(8,128)(2,1)S(1)} %place.1.place_ref, bf16[2,4,96,512]{3,2,1,0:T(8,128)(2,1)S(1)} %bitcast.42), custom_call_target="tpu_custom_call" | custom-call | tf_op jit(solution)/shard_map/params/pallas_call | solution.py:283
  (2 shorter events, 0.1 us)
Async XLA Ops:
  27.1 7.6 %copy-start = (s32[192,128]{1,0:T(8,128)S(1)}, s32[192,128]{1,0:T(8,128)}, u32[]{:S(2)}) copy-start(s32[192,128]{1,0:T(8,128)} %cols_ref) | copy-start | bytes 294916
  27.1 16.9 %all-to-all-start.1 = ((bf16[12,8,512]{2,1,0:T(8,128)(2,1)}), bf16[12,8,512]{2,1,0:T(8,128)(2,1)S(1)}, u32[]{:S(2)}, u32[]{:S(2)}) async-start(bf16[12,8,512]{2,1,0:T(8,128)(2,1)} %bitcast.6), calls=%async_computation.1 | async-start | bytes 196608 | tf_op jit(solution)/shard_map/all_to_all | solution.py:220
  33.9 0.8 copy-start.1
  34.0 0.7 copy-start.5
  44.1 17.4 %copy-start.2 = (f32[2,2048]{1,0:T(2,128)S(1)}, f32[2,2048]{1,0:T(2,128)}, u32[]{:S(2)}) copy-start(f32[2,2048]{1,0:T(2,128)} %param.11) | copy-start | bytes 49156
  44.1 17.4 %copy-start.3 = (f32[2,2048]{1,0:T(2,128)S(1)}, f32[2,2048]{1,0:T(2,128)}, u32[]{:S(2)}) copy-start(f32[2,2048]{1,0:T(2,128)} %param.12) | copy-start | bytes 49156
  44.1 17.4 %copy-start.4 = (f32[2,2048]{1,0:T(2,128)S(1)}, f32[2,2048]{1,0:T(2,128)}, u32[]{:S(2)}) copy-start(f32[2,2048]{1,0:T(2,128)} %param.13) | copy-start | bytes 49156

commit v6 on v5

--- a/solution.py
+++ b/solution.py
@@ -36,21 +36,20 @@
     return (1 - 2 * (both & 1)).astype(F32)
 
 
-def rotate_kernel(order_hbm, rows_hbm, cols_hbm, grad_hbm, out_ref, order_ref, rows_ref, cols_ref, grad_ref, mixed_ref, sems):
+def rotate_kernel(
+    order_hbm, rows_hbm, cols_hbm, grad_hbm, out_ref, signs_ref, place_ref, order_ref, rows_ref, cols_ref, grad_ref, mixed_ref, sems
+):
     small = [
         pltpu.make_async_copy(order_hbm, order_ref, sems.at[0]),
         pltpu.make_async_copy(rows_hbm, rows_ref, sems.at[1]),
         pltpu.make_async_copy(cols_hbm, cols_ref, sems.at[2]),
     ]
-    large = [
-        pltpu.make_async_copy(
-            grad_hbm.at[:, k * 512 : (k + 1) * 512], grad_ref.at[:, k * 512 : (k + 1) * 512], sems.at[3 + k]
-        )
-        for k in range(4)
-    ]
-    for copy in small + large:
+    large = pltpu.make_async_copy(grad_hbm, grad_ref, sems.at[3])
+    for copy in small:
         copy.start()
+    large.start()
     core = lax.axis_index("core")
+    own = ((lax.axis_index("y_lo") * 12 + lax.axis_index("z")) * 2 + core) * 2
     row = iota((BLOCKS, BLOCKS), 0)
     lane = iota((BLOCKS, BLOCKS), 1)
     half = (row >= 96).astype(jnp.int32)
@@ -60,6 +59,12 @@
     owner = jnp.where(half == 1, core, 1 - core)
     slot = ((y_lo * 12 + z) * 2 + owner) * 2 + (place & 1)
     table = parity_sign(iota((256, 256), 0) & iota((256, 256), 1), (4, 2, 1)).astype(BF16)
+    spread = jnp.where(iota((32, 16), 1) == jnp.right_shift(iota((32, 16), 0), 1), 1.0, 0.0).astype(BF16)
+    core_of = (lane >= 96).astype(jnp.int32)
+    rest = lane - 96 * core_of
+    j_of = (rest >= 48).astype(jnp.int32)
+    slot_of = ((rest - 48 * j_of) * 2 + core_of) * 2 + j_of
+    scatter = jnp.where(row == slot_of, 1.0, 0.0).astype(BF16)
     for copy in small:
         copy.wait()
     order = order_ref[...].astype(F32)
@@ -69,18 +74,28 @@
     col_bits = (2 * cols_ref[...] - 1).astype(F32).astype(BF16)
     row_signs = lax.dot_general(pick, row_bits, (((1,), (1,)), ((), ())), preferred_element_type=F32)
     col_signs = jnp.dot(pick, col_bits, preferred_element_type=F32)
+
+    wanted = iota((32, BLOCKS), 1) == own + (iota((32, BLOCKS), 0) & 1)
+    own_block = jnp.sum(jnp.where(wanted, order, 0.0), axis=1, keepdims=True)
+    own_pick = jnp.where(own_block == iota((32, BLOCKS), 1).astype(F32), 1.0, 0.0)
+    wide = jnp.dot(spread, row_bits, preferred_element_type=F32)
+    own_rows = jnp.sum(wide * own_pick, axis=1, keepdims=True)
+    signs_ref[...] = own_rows * jnp.dot(own_pick.astype(BF16), col_bits, preferred_element_type=F32)
+    orders = jnp.broadcast_to(order, (8, BLOCKS)).astype(BF16)
+    placed = jnp.dot(orders, scatter, preferred_element_type=F32)[0:1]
+    place_ref[...] = jnp.where(row.astype(F32) == placed, 1.0, 0.0).astype(BF16)
+
+    large.wait()
+    picked = jnp.dot(pick, grad_ref[...], preferred_element_type=F32)
+    signed = []
     for k in range(8):
-        if k % 2 == 0:
-            large[k // 2].wait()
-        picked = jnp.dot(pick, grad_ref[:, k * 256 : (k + 1) * 256], preferred_element_type=F32)
-        signed = jnp.concatenate(
-            [
-                picked[:, :LANE] * col_signs * row_signs[:, 2 * k : 2 * k + 1],
-                picked[:, LANE:] * col_signs * row_signs[:, 2 * k + 1 : 2 * k + 2],
-            ],
-            axis=1,
-        ).astype(BF16)
-        mixed_ref[k] = jnp.dot(signed, table, preferred_element_type=F32)
+        pair = [
+            picked[:, a * LANE : (a + 1) * LANE] * col_signs * row_signs[:, a : a + 1] for a in (2 * k, 2 * k + 1)
+        ]
+        signed.append(jnp.concatenate(pair, axis=1).astype(BF16))
+    product = jnp.dot(jnp.concatenate(signed, axis=0), table, preferred_element_type=F32)
+    for k in range(8):
+        mixed_ref[k] = product[k * BLOCKS : (k + 1) * BLOCKS]
     for start in range(0, BLOCKS, 16):
         mixed = [mixed_ref[k, start : start + 16] for k in range(8)]
         for span in (1, 2, 4):
@@ -103,20 +118,6 @@
         )
         for member in range(8):
             out_ref[8 * y_lo + member] = piece
-
-
-def owned_signs_kernel(owned_ref, rows_ref, cols_ref, out_ref):
-    row = iota((32, BLOCKS), 0)
-    lane = iota((32, BLOCKS), 1)
-    wanted = jnp.where((row & 1) == 0, owned_ref[0], owned_ref[1])
-    pick = jnp.where(lane == wanted, 1.0, 0.0)
-    spread = jnp.where(iota((32, 16), 1) == jnp.right_shift(iota((32, 16), 0), 1), 1.0, 0.0).astype(BF16)
-    row_bits = (2 * rows_ref[...] - 1).astype(F32).astype(BF16)
-    col_bits = (2 * cols_ref[...] - 1).astype(F32).astype(BF16)
-    wide = jnp.dot(spread, row_bits, preferred_element_type=F32)
-    row_signs = jnp.sum(wide * pick, axis=1, keepdims=True)
-    col_signs = jnp.dot(pick.astype(BF16), col_bits, preferred_element_type=F32)
-    out_ref[...] = row_signs * col_signs
 
 
 def adam_kernel(got_ref, signs_ref, master_ref, first_ref, second_ref, new_master_ref, new_first_ref, new_second_ref, sent_ref, held_ref):
@@ -146,18 +147,6 @@
         sent_ref[member] = mine
 
 
-def place_kernel(order_ref, out_ref):
-    col = iota((BLOCKS, BLOCKS), 1)
-    core = (col >= 96).astype(jnp.int32)
-    rest = col - 96 * core
-    j = (rest >= 48).astype(jnp.int32)
-    slot = ((rest - 48 * j) * 2 + core) * 2 + j
-    spread = jnp.where(iota((BLOCKS, BLOCKS), 0) == slot, 1.0, 0.0).astype(BF16)
-    order = jnp.broadcast_to(order_ref[...].astype(F32), (8, BLOCKS)).astype(BF16)
-    block = jnp.dot(order, spread, preferred_element_type=F32)[0:1]
-    out_ref[...] = jnp.where(iota((BLOCKS, BLOCKS), 0).astype(F32) == block, 1.0, 0.0).astype(BF16)
-
-
 def repeat_kernel(got_ref, out_ref, wide_ref):
     wide_ref[...] = got_ref[...].astype(F32)
     for a in range(4):
@@ -168,8 +157,16 @@
             out_ref[x, :, a * LANE : (a + 1) * LANE] = rows
 
 
-def params_kernel(place_ref, got_ref, out_hbm, out_ref, sems):
-    copies = []
+def params_kernel(
+    place_ref, got_ref, master_ref, first_ref, second_ref, out_hbm, master_hbm, first_hbm, second_hbm, out_ref, sems
+):
+    copies = [
+        pltpu.make_async_copy(master_ref, master_hbm, sems.at[4]),
+        pltpu.make_async_copy(first_ref, first_hbm, sems.at[5]),
+        pltpu.make_async_copy(second_ref, second_hbm, sems.at[6]),
+    ]
+    for copy in copies:
+        copy.start()
     for x in range(4):
         rows = jnp.concatenate([got_ref[0, x], got_ref[1, x]], axis=0)
         column = x * 512
@@ -185,7 +182,6 @@
 
 
 VMEM = pl.BlockSpec(memory_space=pltpu.VMEM)
-SMEM = pl.BlockSpec(memory_space=pltpu.SMEM)
 HBM = pl.BlockSpec(memory_space=pltpu.HBM)
 ROOM = pltpu.CompilerParams(vmem_limit_bytes=32 * 1024 * 1024)
 
@@ -195,18 +191,22 @@
     order_row = block_order.reshape(1, BLOCKS)
     rows_t = sign_rows.T
 
-    halves = pl.pallas_call(
+    halves, signs, place = pl.pallas_call(
         rotate_kernel,
-        out_shape=jax.ShapeDtypeStruct((2, 4, 96, 512), BF16),
+        out_shape=(
+            jax.ShapeDtypeStruct((2, 4, 96, 512), BF16),
+            jax.ShapeDtypeStruct((32, LANE), F32),
+            jax.ShapeDtypeStruct((BLOCKS, BLOCKS), BF16),
+        ),
         in_specs=[HBM] * 4,
-        out_specs=VMEM,
+        out_specs=(VMEM,) * 3,
         scratch_shapes=[
             pltpu.VMEM((1, BLOCKS), jnp.int32),
             pltpu.VMEM((16, BLOCKS), jnp.int32),
             pltpu.VMEM((BLOCKS, LANE), jnp.int32),
             pltpu.VMEM((BLOCKS, BLOCK), BF16),
             pltpu.VMEM((8, BLOCKS, 256), F32),
-            pltpu.SemaphoreType.DMA((7,)),
+            pltpu.SemaphoreType.DMA((4,)),
         ],
         compiler_params=ROOM,
         name="rotate",
@@ -216,30 +216,7 @@
     part = (halves[1].astype(F32) + other.astype(F32)).astype(BF16)
     got = lax.all_to_all(part, "x", 0, 0, tiled=True)
     part = jnp.sum(got.astype(F32), axis=0).astype(BF16)
-    part, order_late, rows_late, cols_late = lax.optimization_barrier((part, block_order, rows_t, sign_cols))
     got = lax.all_to_all(part.reshape(12, 8, 512), "z", 0, 0, tiled=True)
-    owner = (lax.axis_index("y_lo") * 12 + lax.axis_index("z")) * 2 + core
-    owned = lax.dynamic_slice_in_dim(order_late, owner * 2, 2)
-    signs = pl.pallas_call(
-        owned_signs_kernel,
-        out_shape=jax.ShapeDtypeStruct((32, LANE), F32),
-        in_specs=[SMEM, VMEM, VMEM],
-        out_specs=VMEM,
-        compiler_params=ROOM,
-        cost_estimate=pl.CostEstimate(flops=2000000, bytes_accessed=200000, transcendentals=0),
-        name="owned_signs",
-    )(owned, rows_late, cols_late)
-
-    place = pl.pallas_call(
-        place_kernel,
-        out_shape=jax.ShapeDtypeStruct((BLOCKS, BLOCKS), BF16),
-        in_specs=[VMEM],
-        out_specs=VMEM,
-        compiler_params=ROOM,
-        cost_estimate=pl.CostEstimate(flops=4000000, bytes_accessed=1200000, transcendentals=0),
-        name="place",
-    )(order_late.reshape(1, BLOCKS))
-    got, signs, place = lax.optimization_barrier((got, signs, place))
     sent = pl.pallas_call(
         owner_sum_kernel,
         out_shape=jax.ShapeDtypeStruct((32, 8, LANE), F32),
@@ -256,10 +233,10 @@
     def by_slot(value):
         return value.reshape(16, 2, LANE).transpose(1, 0, 2).reshape(2, BLOCK)
 
-    state = jax.ShapeDtypeStruct((32, LANE), F32)
-    new_master, new_first, new_second, sent = pl.pallas_call(
+    kept = pltpu.VMEM((32, LANE), F32)
+    *states, sent = pl.pallas_call(
         adam_kernel,
-        out_shape=(state, state, state, jax.ShapeDtypeStruct((48, 8, LANE), BF16)),
+        out_shape=(kept, kept, kept, jax.ShapeDtypeStruct((48, 8, LANE), BF16)),
         in_specs=[VMEM] * 5,
         out_specs=(VMEM,) * 4,
         scratch_shapes=[pltpu.VMEM((32, LANE), F32)],
@@ -280,16 +257,17 @@
     got = lax.all_to_all(sent, "x", 0, 0, tiled=True)
     got = lax.all_gather(got.reshape(384, 512), "core", axis=0, tiled=True).reshape(2, 4, 96, 512)
 
-    params = pl.pallas_call(
+    state = jax.ShapeDtypeStruct((32, LANE), F32)
+    params, *states = pl.pallas_call(
         params_kernel,
-        out_shape=jax.ShapeDtypeStruct((BLOCKS, BLOCK), BF16),
-        in_specs=[VMEM] * 2,
-        out_specs=HBM,
-        scratch_shapes=[pltpu.VMEM((BLOCKS, BLOCK), BF16), pltpu.SemaphoreType.DMA((4,))],
+        out_shape=(jax.ShapeDtypeStruct((BLOCKS, BLOCK), BF16), state, state, state),
+        in_specs=[VMEM] * 5,
+        out_specs=(HBM,) * 4,
+        scratch_shapes=[pltpu.VMEM((BLOCKS, BLOCK), BF16), pltpu.SemaphoreType.DMA((7,))],
         compiler_params=ROOM,
         name="params",
-    )(place, got)
-    return by_slot(new_master), by_slot(new_first), by_slot(new_second), params
+    )(place, got, *states)
+    return *(by_slot(state) for state in states), params
 
 
 def solution(mesh):

time: 97.7 us -> 95.3 us (0.975)
  blocking collectives: 73.6 us -> 90.2 us
  waiting for transfers between devices: 8.4 us -> 0 us
  starting transfers between devices: 6.8 us -> 0 us
  Pallas kernels: 6.01 us -> 3.77 us
    all_to_all x0 -> x1, blocking collectives: none -> 16.6 us  [on_device(): got = lax.all_to_all(part.reshape(12, 8, 512), 'z', 0, 0, tiled=True)]
    all_to_all x1 -> x0, waiting for transfers between devices: 8.4 us -> none  [on_device(): got = lax.all_to_all(part.reshape(12, 8, 512), 'z', 0, 0, tiled=True)]
    all_to_all x1 -> x0, starting transfers between devices: 6.8 us -> none  [on_device(): got = lax.all_to_all(part.reshape(12, 8, 512), 'z', 0, 0, tiled=True)]
    pallas_call x5 -> x3, Pallas kernels: 5.89 us -> 3.65 us  [the longest x1 2.15 us: on_device(): pl.pallas_call(rotate_kernel, out_shape=(jax.ShapeDtypeStruct((2, 4, 96,...]
  transfers between devices with their start and end apart: 1 -> 0, of which waited for: 1 -> 0; matrix products, arithmetic and copies ran while one was open for 0% -> 0% of each run, Pallas kernels for 1% -> 0%
where the time goes in v6:
time: 95.3 us; the launch traced here: 94.9 us
  blocking collectives  90.2 us (95%)
  Pallas kernels  3.77 us (4%)
    all_to_all x1, blocking collectives, on_device(): got = lax.all_to_all(sent, ('y_lo', 'y_hi', 'x'), 0, 0, tiled=True)  17.3 us
    all_to_all x1, blocking collectives, on_device(): got = lax.all_to_all(part.reshape(12, 8, 512), 'z', 0, 0, tiled=True)  16.6 us
    all_to_all x1, blocking collectives, on_device(): got = lax.all_to_all(sent, ('y_lo', 'z'), 0, 0, tiled=True)  16 us
    all_gather x1, blocking collectives, on_device(): lax.all_gather(halves[0].reshape(384, 512), 'core', axis=0, tiled=True)  12.5 us
    all_to_all x1, blocking collectives, on_device(): got = lax.all_to_all(part, 'x', 0, 0, tiled=True)  10.2 us
    all_gather x1, blocking collectives, on_device(): lax.all_gather(got.reshape(384, 512), 'core', axis=0, tiled=True)  8.94 us
    all_to_all x1, blocking collectives, on_device(): got = lax.all_to_all(sent, 'x', 0, 0, tiled=True)  8.62 us
    pallas_call x1, Pallas kernels, on_device(): pl.pallas_call(rotate_kernel, out_shape=(jax.ShapeDtypeStruct((2, 4, 96,...  2.15 us

profile of v6, /device:TPU:1, one launch (start us, length us, event | category | flops | bytes accessed | tf_op | source)
XLA Modules:
  0.0 94.9 jit_solution(11620418524908730020)
XLA Ops:
  0.6 2.1 %rotate.1 = (bf16[2,4,96,512]{3,2,1,0:T(8,128)(2,1)S(1)}, f32[32,128]{1,0:T(8,128)S(1)}, bf16[192,192]{1,0:T(8,128)(2,1)S(1)}) custom-call(s32[1,192]{1,0:T(1,128)} %bitcast.52, s32[16,192]{1,0:T(8,128)} %bitcast.51, s32[192,128]{1,0:T(8,128)} %cols_hbm.1, bf16[192,2048]{1,0:T(8,128)(2,1)} %bitcast.49), custom_call_target="tpu_custom_call" | custom-call | tf_op jit(solution)/shard_map/rotate/pallas_call | solution.py:194
  2.8 12.5 %all_gather.6 = bf16[768,512]{1,0:T(8,128)(2,1)S(1)} all-gather(bf16[384,512]{1,0:T(8,128)(2,1)S(1)} %bitcast.48), channel_id=1, replica_groups=mesh['y_lo'=4,'z'=12,'core'=2,'y_hi'=2,'x'=4] {'core'}, dimensions={0}, use_global_device_ids=true | all-gather | bytes 1179648 | tf_op jit(solution)/shard_map/all_gather | solution.py:214
  15.3 0.1 fusion
  15.5 10.2 %all_to_all.25 = bf16[4,96,512]{2,1,0:T(8,128)(2,1)S(1)} all-to-all(bf16[4,96,512]{2,1,0:T(8,128)(2,1)S(1)} %fusion), channel_id=1, replica_groups=mesh['y_lo'=4,'z'=12,'core'=2,'y_hi'=2,'x'=4] {'x'}, dimensions={0} | all-to-all | bytes 786432 | tf_op jit(solution)/shard_map/all_to_all | solution.py:217
  25.7 0.1 reduce_sum.12
  25.7 16.6 %all_to_all.26.got_ref = bf16[12,8,512]{2,1,0:T(8,128)(2,1)S(1)} all-to-all(bf16[12,8,512]{2,1,0:T(8,128)(2,1)S(1)} %bitcast.50), channel_id=1, replica_groups=mesh['y_lo'=4,'z'=12,'core'=2,'y_hi'=2,'x'=4] {'z'}, dimensions={0} | all-to-all | bytes 196608 | tf_op jit(solution)/shard_map/all_to_all | solution.py:219
  42.4 0.0 copy-start
  42.4 0.0 copy-start.1
  42.4 0.0 copy-start.2
  42.4 17.3 %all_to_all.27.got_ref = f32[32,8,128]{2,1,0:T(8,128)S(1)} all-to-all(f32[32,8,128]{2,1,0:T(8,128)S(1)} %owner_sum.1), channel_id=1, replica_groups=mesh['y_lo'=4,'z'=12,'core'=2,'y_hi'=2,'x'=4] {'y_lo','y_hi','x'}, dimensions={0} | all-to-all | bytes 262144 | tf_op jit(solution)/shard_map/all_to_all | solution.py:228
  59.7 0.0 copy-done
  59.7 0.0 copy-done.1
  59.7 0.0 copy-done.2
  59.7 0.4 adam.1
  60.1 16.0 %all_to_all.28 = bf16[48,8,128]{2,1,0:T(8,128)(2,1)S(1)} all-to-all(bf16[48,8,128]{2,1,0:T(8,128)(2,1)S(1)} %get-tuple-element.18), channel_id=1, replica_groups=mesh['y_lo'=4,'z'=12,'core'=2,'y_hi'=2,'x'=4] {'y_lo','z'}, dimensions={0} | all-to-all | bytes 196608 | tf_op jit(solution)/shard_map/all_to_all | solution.py:247
  76.1 0.1 repeat.1
  76.2 8.6 %all_to_all.29 = bf16[4,96,512]{2,1,0:T(8,128)(2,1)S(1)} all-to-all(bf16[4,96,512]{2,1,0:T(8,128)(2,1)S(1)} %repeat.1), channel_id=1, replica_groups=mesh['y_lo'=4,'z'=12,'core'=2,'y_hi'=2,'x'=4] {'x'}, dimensions={0} | all-to-all | bytes 786432 | tf_op jit(solution)/shard_map/all_to_all | solution.py:257
  84.8 8.9 %all_gather.7 = bf16[768,512]{1,0:T(8,128)(2,1)S(1)} all-gather(bf16[384,512]{1,0:T(8,128)(2,1)S(1)} %bitcast.47), channel_id=1, replica_groups=mesh['y_lo'=4,'z'=12,'core'=2,'y_hi'=2,'x'=4] {'core'}, dimensions={0}, use_global_device_ids=true | all-gather | bytes 1179648 | tf_op jit(solution)/shard_map/all_gather | solution.py:258
  93.8 1.1 %params.1 = (bf16[192,2048]{1,0:T(8,128)(2,1)}, f32[32,128]{1,0:T(8,128)}, f32[32,128]{1,0:T(8,128)}, f32[32,128]{1,0:T(8,128)}) custom-call(bf16[192,192]{1,0:T(8,128)(2,1)S(1)} %get-tuple-element.15.place_ref, bf16[2,4,96,512]{3,2,1,0:T(8,128)(2,1)S(1)} %bitcast.41, f32[32,128]{1,0:T(8,128)S(1)} %get-tuple-element.19.master_ref, ...), custom_call_target="tpu_custom_call" | custom-call | tf_op jit(solution)/shard_map/params/pallas_call | solution.py:261
  (2 shorter events, 0.1 us)
Async XLA Ops:
  42.4 17.4 %copy-start = (f32[2,2048]{1,0:T(2,128)S(1)}, f32[2,2048]{1,0:T(2,128)}, u32[]{:S(2)}) copy-start(f32[2,2048]{1,0:T(2,128)} %param.11) | copy-start | bytes 49156
  42.4 17.4 %copy-start.1 = (f32[2,2048]{1,0:T(2,128)S(1)}, f32[2,2048]{1,0:T(2,128)}, u32[]{:S(2)}) copy-start(f32[2,2048]{1,0:T(2,128)} %param.12) | copy-start | bytes 49156
  42.4 17.4 %copy-start.2 = (f32[2,2048]{1,0:T(2,128)S(1)}, f32[2,2048]{1,0:T(2,128)}, u32[]{:S(2)}) copy-start(f32[2,2048]{1,0:T(2,128)} %param.13) | copy-start | bytes 49156

commit v7 on v6

--- a/solution.py
+++ b/solution.py
@@ -54,8 +54,8 @@
     lane = iota((BLOCKS, BLOCKS), 1)
     half = (row >= 96).astype(jnp.int32)
     place = row - 96 * half
-    y_lo = jnp.right_shift(place, 1) & 3
-    z = jnp.right_shift(place, 3)
+    y_lo = sum((place >= bound).astype(jnp.int32) for bound in (24, 48, 72))
+    z = jnp.right_shift(place - 24 * y_lo, 1)
     owner = jnp.where(half == 1, core, 1 - core)
     slot = ((y_lo * 12 + z) * 2 + owner) * 2 + (place & 1)
     table = parity_sign(iota((256, 256), 0) & iota((256, 256), 1), (4, 2, 1)).astype(BF16)
@@ -96,34 +96,34 @@
     product = jnp.dot(jnp.concatenate(signed, axis=0), table, preferred_element_type=F32)
     for k in range(8):
         mixed_ref[k] = product[k * BLOCKS : (k + 1) * BLOCKS]
-    for start in range(0, BLOCKS, 16):
-        mixed = [mixed_ref[k, start : start + 16] for k in range(8)]
+    for start in range(0, BLOCKS, 24):
+        mixed = [mixed_ref[k, start : start + 24] for k in range(8)]
         for span in (1, 2, 4):
             for k in range(8):
                 if not k & span:
                     low, high = mixed[k], mixed[k + span]
                     mixed[k], mixed[k + span] = low + high, low - high
-        for k in range(8):
-            rotated = (mixed[k] * INV_ROOT).astype(BF16)
-            out_ref[start // 96, k // 2, start % 96 : start % 96 + 16, (k % 2) * 256 : (k % 2) * 256 + 256] = rotated
-
-
-def owner_sum_kernel(got_ref, out_ref):
+        for x in range(4):
+            pair = mixed[2 * x], mixed[2 * x + 1]
+            rows = [part[:, c : c + LANE] * INV_ROOT for part in pair for c in (0, LANE)]
+            out_ref[start // 96, (start % 96) // 24 * 4 + x] = jnp.concatenate(rows, axis=0).astype(BF16)
+
+
+def plane_sum_kernel(got_ref, out_ref):
     total = got_ref[0].astype(F32)
-    for z in range(1, 12):
-        total = total + got_ref[z].astype(F32)
-    for y_lo in range(4):
-        piece = jnp.concatenate(
-            [total[2 * y_lo : 2 * y_lo + 2, a * LANE : (a + 1) * LANE] for a in range(4)], axis=0
-        )
+    for member in range(1, 16):
+        total = total + got_ref[member].astype(F32)
+    for z in range(12):
+        rows = [total[24 * a + 2 * z : 24 * a + 2 * z + 2] for a in range(4)]
+        piece = jnp.concatenate(rows, axis=0).astype(BF16)
         for member in range(8):
-            out_ref[8 * y_lo + member] = piece
+            out_ref[8 * z + member] = piece
 
 
 def adam_kernel(got_ref, signs_ref, master_ref, first_ref, second_ref, new_master_ref, new_first_ref, new_second_ref, sent_ref, held_ref):
-    total = got_ref[0:4]
-    for y in range(1, 8):
-        total = total + got_ref[4 * y : 4 * y + 4]
+    total = got_ref[0:4].astype(F32)
+    for source in range(1, 24):
+        total = total + got_ref[4 * source : 4 * source + 4].astype(F32)
     gradient = total.reshape(32, LANE)
     new_first = beta_one * first_ref[...] + (1.0 - beta_one) * gradient
     new_second = beta_two * second_ref[...] + (1.0 - beta_two) * gradient * gradient
@@ -194,7 +194,7 @@
     halves, signs, place = pl.pallas_call(
         rotate_kernel,
         out_shape=(
-            jax.ShapeDtypeStruct((2, 4, 96, 512), BF16),
+            jax.ShapeDtypeStruct((2, 16, 96, LANE), BF16),
             jax.ShapeDtypeStruct((32, LANE), F32),
             jax.ShapeDtypeStruct((BLOCKS, BLOCKS), BF16),
         ),
@@ -211,21 +211,19 @@
         compiler_params=ROOM,
         name="rotate",
     )(*(pltpu.with_memory_space_constraint(each, pltpu.HBM) for each in (order_row, rows_t, sign_cols, grads[0])))
-    got = lax.all_gather(halves[0].reshape(384, 512), "core", axis=0, tiled=True).reshape(2, 4, 96, 512)
+    got = lax.all_gather(halves[0].reshape(1536, LANE), "core", axis=0, tiled=True).reshape(2, 16, 96, LANE)
     other = lax.dynamic_index_in_dim(got, 1 - core, 0, keepdims=False)
     part = (halves[1].astype(F32) + other.astype(F32)).astype(BF16)
-    got = lax.all_to_all(part, "x", 0, 0, tiled=True)
-    part = jnp.sum(got.astype(F32), axis=0).astype(BF16)
-    got = lax.all_to_all(part.reshape(12, 8, 512), "z", 0, 0, tiled=True)
+    got = lax.all_to_all(part, ("y_lo", "x"), 0, 0, tiled=True)
     sent = pl.pallas_call(
-        owner_sum_kernel,
-        out_shape=jax.ShapeDtypeStruct((32, 8, LANE), F32),
+        plane_sum_kernel,
+        out_shape=jax.ShapeDtypeStruct((96, 8, LANE), BF16),
         in_specs=[VMEM],
         out_specs=VMEM,
         compiler_params=ROOM,
-        name="owner_sum",
+        name="plane_sum",
     )(got)
-    got = lax.all_to_all(sent, ("y_lo", "y_hi", "x"), 0, 0, tiled=True)
+    got = lax.all_to_all(sent, ("z", "y_hi", "x"), 0, 0, tiled=True)
 
     def by_row(value):
         return value.reshape(2, 16, LANE).transpose(1, 0, 2).reshape(32, LANE)

time: 95.3 us -> 99.6 us (1.045)
  blocking collectives: 90.2 us -> 94.6 us
    all_to_all x1, blocking collectives: 16 us -> 20.1 us  [on_device(): got = lax.all_to_all(sent, ('y_lo', 'z'), 0, 0, tiled=True)]
    all_to_all x3 -> x2, blocking collectives: 44.1 us -> 45.9 us  [the longest x1 31.1 us: on_device(): got = lax.all_to_all(sent, ('z', 'y_hi', 'x'), 0, 0, tiled=True)]
    all_gather x1, blocking collectives: 8.94 us -> 7.41 us  [on_device(): lax.all_gather(got.reshape(384, 512), 'core', axis=0, tiled=True)]
where the time goes in v7:
time: 99.6 us; the launch traced here: 99.3 us
  blocking collectives  94.6 us (95%)
  Pallas kernels  3.83 us (4%)
    all_to_all x1, blocking collectives, on_device(): got = lax.all_to_all(sent, ('z', 'y_hi', 'x'), 0, 0, tiled=True)  31.1 us
    all_to_all x1, blocking collectives, on_device(): got = lax.all_to_all(sent, ('y_lo', 'z'), 0, 0, tiled=True)  20.1 us
    all_to_all x1, blocking collectives, on_device(): got = lax.all_to_all(part, ('y_lo', 'x'), 0, 0, tiled=True)  14.8 us
    all_gather x1, blocking collectives, on_device(): lax.all_gather(halves[0].reshape(1536, LANE), 'core', axis=0, tiled=True)  12.5 us
    all_to_all x1, blocking collectives, on_device(): got = lax.all_to_all(sent, 'x', 0, 0, tiled=True)  8.62 us
    all_gather x1, blocking collectives, on_device(): lax.all_gather(got.reshape(384, 512), 'core', axis=0, tiled=True)  7.41 us
    pallas_call x1, Pallas kernels, on_device(): pl.pallas_call(rotate_kernel, out_shape=(jax.ShapeDtypeStruct((2, 16, 96,...  2.15 us

profile of v7, /device:TPU:1, one launch (start us, length us, event | category | flops | bytes accessed | tf_op | source)
XLA Modules:
  0.0 99.3 jit_solution(17943160709213687658)
XLA Ops:
  0.6 2.1 %rotate.1 = (bf16[2,16,96,128]{3,2,1,0:T(8,128)(2,1)S(1)}, f32[32,128]{1,0:T(8,128)S(1)}, bf16[192,192]{1,0:T(8,128)(2,1)S(1)}) custom-call(s32[1,192]{1,0:T(1,128)} %bitcast.50, s32[16,192]{1,0:T(8,128)} %bitcast.49, s32[192,128]{1,0:T(8,128)} %cols_hbm.1, bf16[192,2048]{1,0:T(8,128)(2,1)} %bitcast.48), custom_call_target="tpu_custom_call" | custom-call | tf_op jit(solution)/shard_map/rotate/pallas_call | solution.py:194
  2.8 12.5 %all_gather.6 = bf16[3072,128]{1,0:T(8,128)(2,1)S(1)} all-gather(bf16[1536,128]{1,0:T(8,128)(2,1)S(1)} %bitcast.47), channel_id=1, replica_groups=mesh['y_lo'=4,'z'=12,'core'=2,'y_hi'=2,'x'=4] {'core'}, dimensions={0}, use_global_device_ids=true | all-gather | bytes 1179648 | tf_op jit(solution)/shard_map/all_gather | solution.py:214
  15.3 0.1 fusion
  15.5 14.8 %all_to_all.20.got_ref = bf16[16,96,128]{2,1,0:T(8,128)(2,1)S(1)} all-to-all(bf16[16,96,128]{2,1,0:T(8,128)(2,1)S(1)} %fusion), channel_id=1, replica_groups=mesh['y_lo'=4,'z'=12,'core'=2,'y_hi'=2,'x'=4] {'y_lo','x'}, dimensions={0} | all-to-all | bytes 786432 | tf_op jit(solution)/shard_map/all_to_all | solution.py:217
  30.3 0.1 plane_sum.1
  30.4 0.0 copy-start
  30.4 0.0 copy-start.1
  30.4 0.0 copy-start.2
  30.4 31.1 %all_to_all.21.got_ref = bf16[96,8,128]{2,1,0:T(8,128)(2,1)S(1)} all-to-all(bf16[96,8,128]{2,1,0:T(8,128)(2,1)S(1)} %plane_sum.1), channel_id=1, replica_groups=mesh['y_lo'=4,'z'=12,'core'=2,'y_hi'=2,'x'=4] {'z','y_hi','x'}, dimensions={0} | all-to-all | bytes 393216 | tf_op jit(solution)/shard_map/all_to_all | solution.py:226
  61.5 0.0 copy-done
  61.5 0.0 copy-done.1
  61.5 0.0 copy-done.2
  61.5 0.4 adam.1
  61.9 20.1 %all_to_all.22 = bf16[48,8,128]{2,1,0:T(8,128)(2,1)S(1)} all-to-all(bf16[48,8,128]{2,1,0:T(8,128)(2,1)S(1)} %get-tuple-element.18), channel_id=1, replica_groups=mesh['y_lo'=4,'z'=12,'core'=2,'y_hi'=2,'x'=4] {'y_lo','z'}, dimensions={0} | all-to-all | bytes 196608 | tf_op jit(solution)/shard_map/all_to_all | solution.py:245
  82.0 0.1 repeat.1
  82.1 8.6 %all_to_all.23 = bf16[4,96,512]{2,1,0:T(8,128)(2,1)S(1)} all-to-all(bf16[4,96,512]{2,1,0:T(8,128)(2,1)S(1)} %repeat.1), channel_id=1, replica_groups=mesh['y_lo'=4,'z'=12,'core'=2,'y_hi'=2,'x'=4] {'x'}, dimensions={0} | all-to-all | bytes 786432 | tf_op jit(solution)/shard_map/all_to_all | solution.py:255
  90.7 7.4 %all_gather.7 = bf16[768,512]{1,0:T(8,128)(2,1)S(1)} all-gather(bf16[384,512]{1,0:T(8,128)(2,1)S(1)} %bitcast.46), channel_id=1, replica_groups=mesh['y_lo'=4,'z'=12,'core'=2,'y_hi'=2,'x'=4] {'core'}, dimensions={0}, use_global_device_ids=true | all-gather | bytes 1179648 | tf_op jit(solution)/shard_map/all_gather | solution.py:256
  98.1 1.1 %params.1 = (bf16[192,2048]{1,0:T(8,128)(2,1)}, f32[32,128]{1,0:T(8,128)}, f32[32,128]{1,0:T(8,128)}, f32[32,128]{1,0:T(8,128)}) custom-call(bf16[192,192]{1,0:T(8,128)(2,1)S(1)} %get-tuple-element.15.place_ref, bf16[2,4,96,512]{3,2,1,0:T(8,128)(2,1)S(1)} %bitcast.40, f32[32,128]{1,0:T(8,128)S(1)} %get-tuple-element.19.master_ref, ...), custom_call_target="tpu_custom_call" | custom-call | tf_op jit(solution)/shard_map/params/pallas_call | solution.py:259
  (1 shorter events, 0.0 us)
Async XLA Ops:
  30.4 31.1 %copy-start = (f32[2,2048]{1,0:T(2,128)S(1)}, f32[2,2048]{1,0:T(2,128)}, u32[]{:S(2)}) copy-start(f32[2,2048]{1,0:T(2,128)} %param.11) | copy-start | bytes 49156
  30.4 31.1 %copy-start.1 = (f32[2,2048]{1,0:T(2,128)S(1)}, f32[2,2048]{1,0:T(2,128)}, u32[]{:S(2)}) copy-start(f32[2,2048]{1,0:T(2,128)} %param.12) | copy-start | bytes 49156
  30.4 31.1 %copy-start.2 = (f32[2,2048]{1,0:T(2,128)S(1)}, f32[2,2048]{1,0:T(2,128)}, u32[]{:S(2)}) copy-start(f32[2,2048]{1,0:T(2,128)} %param.13) | copy-start | bytes 49156

commit v8 on v7

v8 whole, which is shorter than its diff:
```python
import math

import jax
import jax.numpy as jnp
import numpy as np
from jax import lax
from jax.experimental import pallas as pl
from jax.experimental.pallas import tpu as pltpu
from jax.sharding import Mesh, PartitionSpec as P

beta_one = 0.9
beta_two = 0.95
first_fix = 1.0 - math.exp(100.0 * math.log(0.9))
second_fix = 1.0 - math.exp(100.0 * math.log(0.95))
learn_rate = 0.25
weight_decay = 0.1
epsilon = 1e-08

AXES = ("y_lo", "z", "core", "y_hi", "x")
SIZES = (4, 12, 2, 2, 4)
BLOCKS = 192
BLOCK = 2048
LANE = 128
INV_ROOT = 1.0 / math.sqrt(BLOCK)
F32 = jnp.float32
BF16 = jnp.bfloat16


def iota(shape, axis):
    return lax.broadcasted_iota(jnp.int32, shape, axis)


def parity_sign(both, bits):
    for shift in bits:
        both = both ^ jnp.right_shift(both, shift)
    return (1 - 2 * (both & 1)).astype(F32)


def rotate_kernel(
    order_hbm, rows_hbm, cols_hbm, grad_hbm, out_ref, signs_ref, place_ref, order_ref, rows_ref, cols_ref, grad_ref, mixed_ref, sems
):
    small = [
        pltpu.make_async_copy(order_hbm, order_ref, sems.at[0]),
        pltpu.make_async_copy(rows_hbm, rows_ref, sems.at[1]),
        pltpu.make_async_copy(cols_hbm, cols_ref, sems.at[2]),
    ]
    large = pltpu.make_async_copy(grad_hbm, grad_ref, sems.at[3])
    for copy in small:
        copy.start()
    large.start()
    core = lax.axis_index("core")
    row = iota((BLOCKS, BLOCKS), 0)
    lane = iota((BLOCKS, BLOCKS), 1)
    half = (row >= 96).astype(jnp.int32)
    place = row - 96 * half
    y_lo = sum((place >= bound).astype(jnp.int32) for bound in (24, 48, 72))
    z = jnp.right_shift(place - 24 * y_lo, 1)
    owner = jnp.where(half == 1, core, 1 - core)
    slot = ((y_lo * 12 + z) * 2 + owner) * 2 + (place & 1)
    table = parity_sign(iota((256, 256), 0) & iota((256, 256), 1), (4, 2, 1)).astype(BF16)
    spread = jnp.where(iota((32, 16), 1) == jnp.right_shift(iota((32, 16), 0), 1), 1.0, 0.0).astype(BF16)
    wide_lane = iota((BLOCKS, 384), 1)
    core_of = (wide_lane >= 192).astype(jnp.int32)
    rest = wide_lane - 192 * core_of
    y_of = sum((rest >= bound).astype(jnp.int32) for bound in (48, 96, 144))
    rest = rest - 48 * y_of
    parity = (rest >= 24).astype(jnp.int32)
    rest = rest - 24 * parity
    slot_of = ((y_of * 12 + jnp.right_shift(rest, 1)) * 2 + core_of) * 2 + (rest & 1)
    wide_row = iota((BLOCKS, 384), 0)
    scatter = jnp.where(wide_row == slot_of, 1.0, 0.0).astype(BF16)
    for copy in small:
        copy.wait()
    order = order_ref[...].astype(F32)
    block = jnp.sum(jnp.where(slot == lane, order, 0.0), axis=1, keepdims=True)
    pick = jnp.where(block == lane.astype(F32), 1.0, 0.0).astype(BF16)
    row_bits = (2 * rows_ref[...] - 1).astype(F32).astype(BF16)
    col_bits = (2 * cols_ref[...] - 1).astype(F32).astype(BF16)
    row_signs = lax.dot_general(pick, row_bits, (((1,), (1,)), ((), ())), preferred_element_type=F32)
    col_signs = jnp.dot(pick, col_bits, preferred_element_type=F32)

    wide = jnp.dot(spread, row_bits, preferred_element_type=F32)
    for i, axis in enumerate(("x", "y_lo")):
        own = ((lax.axis_index(axis) * 12 + lax.axis_index("z")) * 2 + core) * 2
        wanted = iota((32, BLOCKS), 1) == own + (iota((32, BLOCKS), 0) & 1)
        own_block = jnp.sum(jnp.where(wanted, order, 0.0), axis=1, keepdims=True)
        own_pick = jnp.where(own_block == iota((32, BLOCKS), 1).astype(F32), 1.0, 0.0)
        own_rows = jnp.sum(wide * own_pick, axis=1, keepdims=True)
        signs_ref[i] = own_rows * jnp.dot(own_pick.astype(BF16), col_bits, preferred_element_type=F32)
    orders = jnp.broadcast_to(order, (8, BLOCKS)).astype(BF16)
    placed = jnp.dot(orders, scatter, preferred_element_type=F32)[0:1]
    match = wide_row.astype(F32) == placed
    for i in range(2):
        place_ref[i] = jnp.where(match & (parity == i), 1.0, 0.0).astype(BF16)

    large.wait()
    picked = jnp.dot(pick, grad_ref[...], preferred_element_type=F32)
    signed = []
    for k in range(8):
        pair = [
            picked[:, a * LANE : (a + 1) * LANE] * col_signs * row_signs[:, a : a + 1] for a in (2 * k, 2 * k + 1)
        ]
        signed.append(jnp.concatenate(pair, axis=1).astype(BF16))
    product = jnp.dot(jnp.concatenate(signed, axis=0), table, preferred_element_type=F32)
    for k in range(8):
        mixed_ref[k] = product[k * BLOCKS : (k + 1) * BLOCKS]
    for start in range(0, BLOCKS, 24):
        mixed = [mixed_ref[k, start : start + 24] for k in range(8)]
        for span in (1, 2, 4):
            for k in range(8):
                if not k & span:
                    low, high = mixed[k], mixed[k + span]
                    mixed[k], mixed[k + span] = low + high, low - high
        for x in range(4):
            pair = mixed[2 * x], mixed[2 * x + 1]
            rows = [part[:, c : c + LANE] * INV_ROOT for part in pair for c in (0, LANE)]
            out_ref[start // 96, (start % 96) // 24 * 4 + x] = jnp.concatenate(rows, axis=0).astype(BF16)


def x_sum_kernel(got_ref, out_ref):
    total = got_ref[0].astype(F32)
    for x in range(1, 4):
        total = total + got_ref[x].astype(F32)
    for z in range(12):
        rows = [total[24 * a + 2 * z : 24 * a + 2 * z + 2] for a in range(16)]
        out_ref[z] = jnp.concatenate(rows, axis=0).astype(BF16)


def z_sum_kernel(got_ref, out_ref):
    total = got_ref[0].astype(F32)
    for z in range(1, 12):
        total = total + got_ref[z].astype(F32)
    for y in range(8):
        out_ref[y] = total


def adam_step(gradient, signs, master, first, second):
    new_first = beta_one * first + (1.0 - beta_one) * gradient
    new_second = beta_two * second + (1.0 - beta_two) * gradient * gradient
    update = new_first / first_fix / (jnp.sqrt(new_second / second_fix) + epsilon)
    row, col = iota((32, 32), 0), iota((32, 32), 1)
    same = ((row ^ col) & 1) == 0
    sub = jnp.where(same, parity_sign(jnp.right_shift(row & col, 1), (2, 1)), 0.0)
    table = parity_sign(iota((LANE, LANE), 0) & iota((LANE, LANE), 1), (4, 2, 1))
    restored = jnp.dot(sub, update, precision=lax.Precision.HIGHEST, preferred_element_type=F32)
    restored = jnp.dot(restored, table, precision=lax.Precision.HIGHEST, preferred_element_type=F32)
    restored = restored * INV_ROOT * signs
    new_master = master - learn_rate * (restored + weight_decay * master)
    return new_master, new_first, new_second


def adam_kernel(got_ref, signs_ref, state_ref, sent_ref, terms_ref):
    gradient = got_ref[0]
    for y in range(1, 8):
        gradient = gradient + got_ref[y]
    new_master, _, _ = adam_step(gradient, signs_ref[0], state_ref[0], state_ref[1], state_ref[2])
    mine = new_master.astype(BF16)
    for z in range(12):
        sent_ref[z] = mine
    for i in range(3):
        term = gradient.astype(BF16)
        terms_ref[i] = term
        gradient = gradient - term.astype(F32)


def repeat_kernel(got_ref, terms_ref, out_ref):
    wide = [got_ref[z].astype(F32) for z in range(12)]
    for pair in range(8):
        rows = [wide[z][2 * a : 2 * a + 2] for a in (2 * pair, 2 * pair + 1) for z in range(12)]
        piece = jnp.concatenate(rows, axis=0).astype(BF16)
        for x in range(4):
            out_ref[x, 48 * pair : 48 * pair + 48] = piece
    for i in range(3):
        for x in range(4):
            out_ref[x, 384 + 32 * i : 416 + 32 * i] = terms_ref[i]


def params_kernel(
    place_ref, got_ref, signs_ref, state_ref, out_hbm, master_hbm, first_hbm, second_hbm, out_ref, new_ref, sems
):
    rows = jnp.concatenate(
        [
            jnp.concatenate(
                [got_ref[c, y, 48 * pair : 48 * pair + 48] for c in range(2) for y in range(4)], axis=0
            )
            for pair in range(8)
        ],
        axis=1,
    )
    copies = []
    for half in range(2):
        part = rows[:, 512 * half : 512 * half + 512]
        for i in range(2):
            placed = jnp.dot(place_ref[i], part, preferred_element_type=F32).astype(BF16)
            for k in range(4):
                column = (8 * half + 2 * k + i) * LANE
                out_ref[:, column : column + LANE] = placed[:, k * LANE : (k + 1) * LANE]
        columns = slice(1024 * half, 1024 * half + 1024)
        copies.append(pltpu.make_async_copy(out_ref.at[:, columns], out_hbm.at[:, columns], sems.at[half]))
        copies[-1].start()
    terms = got_ref.at[lax.axis_index("core"), lax.axis_index("y_lo")]
    gradient = terms[384:416].astype(F32) + terms[416:448].astype(F32) + terms[448:480].astype(F32)
    news = adam_step(gradient, signs_ref[1], state_ref[0], state_ref[1], state_ref[2])
    for i, target in enumerate((master_hbm, first_hbm, second_hbm)):
        new_ref[i] = news[i]
        copies.append(pltpu.make_async_copy(new_ref.at[i], target, sems.at[2 + i]))
        copies[-1].start()
    for copy in copies:
        copy.wait()


VMEM = pl.BlockSpec(memory_space=pltpu.VMEM)
HBM = pl.BlockSpec(memory_space=pltpu.HBM)
ROOM = pltpu.CompilerParams(vmem_limit_bytes=32 * 1024 * 1024)


def on_device(grads, sign_rows, sign_cols, block_order, master, first_moment, second_moment):
    core = lax.axis_index("core")
    order_row = block_order.reshape(1, BLOCKS)
    rows_t = sign_rows.T

    def by_row(value):
        return value.reshape(2, 16, LANE).transpose(1, 0, 2).reshape(32, LANE)

    def by_slot(value):
        return value.reshape(16, 2, LANE).transpose(1, 0, 2).reshape(2, BLOCK)

    state = jnp.stack([by_row(each) for each in (master, first_moment, second_moment)])
    mine = jnp.where(lax.axis_index("y_lo") == lax.axis_index("x"), state, 0.0)
    lent = lax.psum_scatter(jnp.broadcast_to(mine, (4, 3, 32, LANE)), "y_lo", scatter_dimension=0)

    halves, signs, place = pl.pallas_call(
        rotate_kernel,
        out_shape=(
            jax.ShapeDtypeStruct((2, 16, 96, LANE), BF16),
            jax.ShapeDtypeStruct((2, 32, LANE), F32),
            jax.ShapeDtypeStruct((2, BLOCKS, 384), BF16),
        ),
        in_specs=[HBM] * 4,
        out_specs=(VMEM,) * 3,
        scratch_shapes=[
            pltpu.VMEM((1, BLOCKS), jnp.int32),
            pltpu.VMEM((16, BLOCKS), jnp.int32),
            pltpu.VMEM((BLOCKS, LANE), jnp.int32),
            pltpu.VMEM((BLOCKS, BLOCK), BF16),
            pltpu.VMEM((8, BLOCKS, 256), F32),
            pltpu.SemaphoreType.DMA((4,)),
        ],
        compiler_params=ROOM,
        name="rotate",
    )(*(pltpu.with_memory_space_constraint(each, pltpu.HBM) for each in (order_row, rows_t, sign_cols, grads[0])))
    got = lax.all_gather(halves[0].reshape(1536, LANE), "core", axis=0, tiled=True).reshape(2, 16, 96, LANE)
    other = lax.dynamic_index_in_dim(got, 1 - core, 0, keepdims=False)
    part = (halves[1].astype(F32) + other.astype(F32)).astype(BF16)
    got = lax.all_to_all(part.reshape(4, 384, LANE), "x", 0, 0, tiled=True)

    def local(kernel, name, out_shape, *operands):
        return pl.pallas_call(
            kernel,
            out_shape=out_shape,
            in_specs=[VMEM] * len(operands),
            out_specs=jax.tree.map(lambda _: VMEM, out_shape),
            compiler_params=ROOM,
            name=name,
        )(*operands)

    sent = local(x_sum_kernel, "x_sum", jax.ShapeDtypeStruct((12, 32, LANE), BF16), got)
    got = lax.all_to_all(sent, "z", 0, 0, tiled=True)
    sent = local(z_sum_kernel, "z_sum", jax.ShapeDtypeStruct((8, 32, LANE), F32), got)
    got = lax.all_to_all(sent, ("y_lo", "y_hi"), 0, 0, tiled=True)
    shapes = (jax.ShapeDtypeStruct((12, 32, LANE), BF16), jax.ShapeDtypeStruct((3, 32, LANE), BF16))
    sent, terms = local(adam_kernel, "adam", shapes, got, signs, lent)
    got = lax.all_to_all(sent, "z", 0, 0, tiled=True)
    sent = local(repeat_kernel, "repeat", jax.ShapeDtypeStruct((4, 480, LANE), BF16), got, terms)
    got = lax.all_to_all(sent, "x", 0, 0, tiled=True)
    got = lax.all_gather(got.reshape(1920, LANE), "core", axis=0, tiled=True).reshape(2, 4, 480, LANE)

    kept = jax.ShapeDtypeStruct((32, LANE), F32)
    params, *news = pl.pallas_call(
        params_kernel,
        out_shape=(jax.ShapeDtypeStruct((BLOCKS, BLOCK), BF16), kept, kept, kept),
        in_specs=[VMEM] * 4,
        out_specs=(HBM,) * 4,
        scratch_shapes=[
            pltpu.VMEM((BLOCKS, BLOCK), BF16),
            pltpu.VMEM((3, 32, LANE), F32),
            pltpu.SemaphoreType.DMA((5,)),
        ],
        compiler_params=ROOM,
        name="params",
    )(place, got, signs, state)
    return *(by_slot(new) for new in news), params


def solution(mesh):
    fine = Mesh(np.asarray(mesh.devices).reshape(SIZES), AXES)
    group = ("y_lo", "z", "core")
    placed = (
        P(AXES, None, None),
        P(),
        P(),
        P(),
        P(group, None),
        P(group, None),
        P(group, None),
    )
    return jax.shard_map(
        on_device,
        mesh=fine,
        in_specs=placed,
        out_specs=(P(group, None), P(group, None), P(group, None), P()),
        check_vma=False,
    )
```

time: 99.6 us -> 122 us (1.22)
  blocking collectives: 94.6 us -> 50 us
  waiting for transfers between devices: 0 us -> 33.3 us
  starting transfers between devices: 0 us -> 16.3 us
  between operations: 0.71 us -> 14.1 us
  Pallas kernels: 3.83 us -> 5.46 us
  local copies, waits for them, and re-layouts: 0.05 us -> 1.53 us
    all_to_all x3 -> x1, blocking collectives: 66 us -> 19 us  [on_device(): got = lax.all_to_all(sent, 'z', 0, 0, tiled=True)]
    all_to_all x0 -> x3, waiting for transfers between devices: none -> 17.1 us  [the longest x1 9.29 us: on_device(): got = lax.all_to_all(sent, 'z', 0, 0, tiled=True)]
    all_to_all x0 -> x3, starting transfers between devices: none -> 16.2 us  [the longest x1 6.82 us: on_device(): got = lax.all_to_all(sent, ('y_lo', 'y_hi'), 0, 0, tiled=True)]
    reduce_scatter x0 -> x1, waiting for transfers between devices: none -> 16.2 us  [on_device(): lax.psum_scatter(jnp.broadcast_to(mine, (4, 3, 32, LANE)), 'y_lo', scatte...]
    all_to_all x1, blocking collectives: 8.62 us -> 10.5 us  [on_device(): got = lax.all_to_all(sent, 'x', 0, 0, tiled=True)]
    pallas_call x3 -> x4, Pallas kernels: 0.55 us -> 1.81 us  [local(): pl.pallas_call(kernel, out_shape=out_shape, in_specs=[VMEM] * len(operand...]
  transfers between devices with their start and end apart: 0 -> 4, of which waited for: 0 -> 3; matrix products, arithmetic and copies ran while one was open for 0% -> 1% of each run, Pallas kernels for 0% -> 1%
where the time goes in v8:
time: 122 us
  blocking collectives  50 us (41%)
  waiting for transfers between devices  33.3 us (27%)
  starting transfers between devices  16.3 us (13%)
  between operations  14.1 us (12%)
  Pallas kernels  5.46 us (4%)
  local copies, waits for them, and re-layouts  1.53 us (1%)
    all_to_all x1, blocking collectives, on_device(): got = lax.all_to_all(sent, 'z', 0, 0, tiled=True)  19 us
    reduce_scatter x1, waiting for transfers between devices, on_device(): lax.psum_scatter(jnp.broadcast_to(mine, (4, 3, 32, LANE)), 'y_lo', scatte...  16.2 us
    all_gather x1, blocking collectives, on_device(): lax.all_gather(halves[0].reshape(1536, LANE), 'core', axis=0, tiled=True)  12.5 us
    all_to_all x1, blocking collectives, on_device(): got = lax.all_to_all(sent, 'x', 0, 0, tiled=True)  10.5 us
    all_to_all x1, waiting for transfers between devices, on_device(): got = lax.all_to_all(sent, 'z', 0, 0, tiled=True)  9.29 us
    all_gather x1, blocking collectives, on_device(): lax.all_gather(got.reshape(1920, LANE), 'core', axis=0, tiled=True)  7.9 us
    all_to_all x1, waiting for transfers between devices, on_device(): got = lax.all_to_all(part.reshape(4, 384, LANE), 'x', 0, 0, tiled=True)  7.78 us
    all_to_all x1, starting transfers between devices, on_device(): got = lax.all_to_all(sent, ('y_lo', 'y_hi'), 0, 0, tiled=True)  6.82 us
  transfers between devices with their start and end apart: 4, of which 3 were waited for; matrix products, arithmetic and copies ran while one was open for 1% of the time, Pallas kernels for 1%

profile of v8, /device:TPU:1, one launch (start us, length us, event | category | flops | bytes accessed | tf_op | source)
XLA Modules:
  0.0 121.6 jit_solution(1601214418443434172)
XLA Ops:
  7.2 2.1 %rotate.1 = (bf16[2,16,96,128]{3,2,1,0:T(8,128)(2,1)S(1)}, f32[2,32,128]{2,1,0:T(8,128)S(1)}, bf16[2,192,384]{2,1,0:T(8,128)(2,1)S(1)}) custom-call(s32[1,192]{1,0:T(1,128)} %bitcast.49, s32[16,192]{1,0:T(8,128)} %bitcast.45, s32[192,128]{1,0:T(8,128)} %cols_hbm.1, bf16[192,2048]{1,0:T(8,128)(2,1)} %bitcast.44), custom_call_target="tpu_custom_call" | custom-call | tf_op jit(solution)/shard_map/rotate/pallas_call | solution.py:232
  9.4 12.5 %all_gather.6 = bf16[3072,128]{1,0:T(8,128)(2,1)S(1)} all-gather(bf16[1536,128]{1,0:T(8,128)(2,1)S(1)} %bitcast.43), channel_id=1, replica_groups=mesh['y_lo'=4,'z'=12,'core'=2,'y_hi'=2,'x'=4] {'core'}, dimensions={0}, use_global_device_ids=true | all-gather | bytes 1179648 | tf_op jit(solution)/shard_map/all_gather | solution.py:252
  21.9 0.8 add_convert_fusion
  22.7 3.5 %all-to-all-start = ((bf16[4,384,128]{2,1,0:T(8,128)(2,1)}), bf16[4,384,128]{2,1,0:T(8,128)(2,1)S(1)}, u32[]{:S(2)}, u32[]{:S(2)}) async-start(bf16[4,384,128]{2,1,0:T(8,128)(2,1)} %bitcast.5), calls=%async_computation | async-start | bytes 786432 | tf_op jit(solution)/shard_map/all_to_all | solution.py:255
  26.2 7.8 %all-to-all-done.got_ref = bf16[4,384,128]{2,1,0:T(8,128)(2,1)S(1)} async-done(((bf16[4,384,128]{2,1,0:T(8,128)(2,1)}), bf16[4,384,128]{2,1,0:T(8,128)(2,1)S(1)}, u32[]{:S(2)}, u32[]{:S(2)}) %all-to-all-start) | async-done | bytes 393248 | tf_op jit(solution)/shard_map/all_to_all | solution.py:255
  34.0 0.7 x_sum.1
  34.7 0.0 copy-start.1
  34.7 0.0 copy-start.2
  34.7 0.0 copy-start.3
  34.7 6.0 %all-to-all-start.1 = ((bf16[12,32,128]{2,1,0:T(8,128)(2,1)}), bf16[12,32,128]{2,1,0:T(8,128)(2,1)S(1)}, u32[]{:S(2)}, u32[]{:S(2)}) async-start(bf16[12,32,128]{2,1,0:T(8,128)(2,1)} %x_sum.1), calls=%async_computation.1 | async-start | bytes 196608 | tf_op jit(solution)/shard_map/all_to_all | solution.py:268
  40.7 0.0 reduce-scatter.2.cloned.1.call-start
  40.7 0.0 copy-done.1
  40.7 0.0 copy-done.2
  40.7 0.0 copy-done.3
  40.8 0.7 broadcast_in_dim.8
  41.5 0.0 reduce-scatter.2.cloned.1.call-update
  41.5 9.3 %all-to-all-done.1.got_ref = bf16[12,32,128]{2,1,0:T(8,128)(2,1)S(1)} async-done(((bf16[12,32,128]{2,1,0:T(8,128)(2,1)}), bf16[12,32,128]{2,1,0:T(8,128)(2,1)S(1)}, u32[]{:S(2)}, u32[]{:S(2)}) %all-to-all-start.1) | async-done | bytes 98336 | tf_op jit(solution)/shard_map/all_to_all | solution.py:268
  50.8 0.7 z_sum.1
  51.5 6.8 %all-to-all-start.2 = ((f32[8,32,128]{2,1,0:T(8,128)}), f32[8,32,128]{2,1,0:T(8,128)S(1)}, u32[]{:S(2)}, u32[]{:S(2)}) async-start(f32[8,32,128]{2,1,0:T(8,128)} %z_sum.1), calls=%async_computation.2 | async-start | bytes 262144 | tf_op jit(solution)/shard_map/all_to_all | solution.py:270
  58.3 16.2 %reduce-scatter.2.cloned.1.call-done = f32[1,3,32,128]{3,2,1,0:T(8,128)} async-done(((f32[4,3,32,128]{3,2,1,0:T(8,128)}), f32[1,3,32,128]{3,2,1,0:T(8,128)}) %reduce-scatter.2.cloned.1.call-update) | async-done | bytes 49168 | tf_op jit(solution)/shard_map/reduce_scatter | solution.py:230
  74.5 0.0 all-to-all-done.2.got_ref
  74.5 0.0 copy-start
  74.5 0.8 copy-done
  75.3 0.4 adam.1
  75.7 19.0 %all_to_all.25.got_ref = bf16[12,32,128]{2,1,0:T(8,128)(2,1)S(1)} all-to-all(bf16[12,32,128]{2,1,0:T(8,128)(2,1)S(1)} %get-tuple-element.16), channel_id=1, replica_groups=mesh['y_lo'=4,'z'=12,'core'=2,'y_hi'=2,'x'=4] {'z'}, dimensions={0} | all-to-all | bytes 196608 | tf_op jit(solution)/shard_map/all_to_all | solution.py:273
  94.7 0.1 repeat.1
  94.8 10.5 %all_to_all.26 = bf16[4,480,128]{2,1,0:T(8,128)(2,1)S(1)} all-to-all(bf16[4,480,128]{2,1,0:T(8,128)(2,1)S(1)} %repeat.1), channel_id=1, replica_groups=mesh['y_lo'=4,'z'=12,'core'=2,'y_hi'=2,'x'=4] {'x'}, dimensions={0} | all-to-all | bytes 983040 | tf_op jit(solution)/shard_map/all_to_all | solution.py:275
  105.3 7.9 %all_gather.7 = bf16[3840,128]{1,0:T(8,128)(2,1)S(1)} all-gather(bf16[1920,128]{1,0:T(8,128)(2,1)S(1)} %bitcast.41), channel_id=1, replica_groups=mesh['y_lo'=4,'z'=12,'core'=2,'y_hi'=2,'x'=4] {'core'}, dimensions={0}, use_global_device_ids=true | all-gather | bytes 1474560 | tf_op jit(solution)/shard_map/all_gather | solution.py:276
  113.2 1.5 %params.1 = (bf16[192,2048]{1,0:T(8,128)(2,1)}, f32[32,128]{1,0:T(8,128)}, f32[32,128]{1,0:T(8,128)}, f32[32,128]{1,0:T(8,128)}) custom-call(bf16[2,192,384]{2,1,0:T(8,128)(2,1)S(1)} %get-tuple-element.13.place_ref, bf16[2,4,480,128]{3,2,1,0:T(8,128)(2,1)S(1)} %bitcast.39, f32[2,32,128]{2,1,0:T(8,128)S(1)} %get-tuple-element.15.signs_ref, ...), custom_call_target="tpu_custom_call" | custom-call | tf_op jit(solution)/shard_map/params/pallas_call | solution.py:279
  (2 shorter events, 0.0 us)
Async XLA Ops:
  22.7 11.3 %all-to-all-start = ((bf16[4,384,128]{2,1,0:T(8,128)(2,1)}), bf16[4,384,128]{2,1,0:T(8,128)(2,1)S(1)}, u32[]{:S(2)}, u32[]{:S(2)}) async-start(bf16[4,384,128]{2,1,0:T(8,128)(2,1)} %bitcast.5), calls=%async_computation | async-start | bytes 786432 | tf_op jit(solution)/shard_map/all_to_all | solution.py:255
  34.7 6.0 %copy-start.1 = (f32[2,2048]{1,0:T(2,128)S(1)}, f32[2,2048]{1,0:T(2,128)}, u32[]{:S(2)}) copy-start(f32[2,2048]{1,0:T(2,128)} %param.13) | copy-start | bytes 49156
  34.7 6.0 %copy-start.2 = (f32[2,2048]{1,0:T(2,128)S(1)}, f32[2,2048]{1,0:T(2,128)}, u32[]{:S(2)}) copy-start(f32[2,2048]{1,0:T(2,128)} %param.12) | copy-start | bytes 49156
  34.7 6.0 %copy-start.3 = (f32[2,2048]{1,0:T(2,128)S(1)}, f32[2,2048]{1,0:T(2,128)}, u32[]{:S(2)}) copy-start(f32[2,2048]{1,0:T(2,128)} %param.11) | copy-start | bytes 49156
  34.7 16.1 %all-to-all-start.1 = ((bf16[12,32,128]{2,1,0:T(8,128)(2,1)}), bf16[12,32,128]{2,1,0:T(8,128)(2,1)S(1)}, u32[]{:S(2)}, u32[]{:S(2)}) async-start(bf16[12,32,128]{2,1,0:T(8,128)(2,1)} %x_sum.1), calls=%async_computation.1 | async-start | bytes 196608 | tf_op jit(solution)/shard_map/all_to_all | solution.py:268
  40.7 33.8 %reduce-scatter.2.cloned.1.call-start = ((), (), s32[]{:S(2)}) async-start(), calls=%async_computation.6 | async-start | bytes 245760 | tf_op jit(solution)/shard_map/reduce_scatter | solution.py:230
  51.5 23.1 %all-to-all-start.2 = ((f32[8,32,128]{2,1,0:T(8,128)}), f32[8,32,128]{2,1,0:T(8,128)S(1)}, u32[]{:S(2)}, u32[]{:S(2)}) async-start(f32[8,32,128]{2,1,0:T(8,128)} %z_sum.1), calls=%async_computation.2 | async-start | bytes 262144 | tf_op jit(solution)/shard_map/all_to_all | solution.py:270
  74.5 0.8 copy-start
Sparse Core Ops, SparseCore 0:
  45.2 29.2 reduce-scatter.1

commit v9 on v8

--- a/solution.py
+++ b/solution.py
@@ -226,8 +226,6 @@
         return value.reshape(16, 2, LANE).transpose(1, 0, 2).reshape(2, BLOCK)
 
     state = jnp.stack([by_row(each) for each in (master, first_moment, second_moment)])
-    mine = jnp.where(lax.axis_index("y_lo") == lax.axis_index("x"), state, 0.0)
-    lent = lax.psum_scatter(jnp.broadcast_to(mine, (4, 3, 32, LANE)), "y_lo", scatter_dimension=0)
 
     halves, signs, place = pl.pallas_call(
         rotate_kernel,
@@ -265,6 +263,9 @@
         )(*operands)
 
     sent = local(x_sum_kernel, "x_sum", jax.ShapeDtypeStruct((12, 32, LANE), BF16), got)
+    sent, state = lax.optimization_barrier((sent, state))
+    swap = [(4 * y_lo + x, 4 * x + y_lo) for y_lo in range(4) for x in range(4)]
+    lent = lax.ppermute(state, ("y_lo", "x"), swap)
     got = lax.all_to_all(sent, "z", 0, 0, tiled=True)
     sent = local(z_sum_kernel, "z_sum", jax.ShapeDtypeStruct((8, 32, LANE), F32), got)
     got = lax.all_to_all(sent, ("y_lo", "y_hi"), 0, 0, tiled=True)

time: 122 us -> 93.4 us (0.77)
  waiting for transfers between devices: 33.3 us -> 13.8 us
  between operations: 14.1 us -> 0.73 us
  blocking collectives: 50 us -> 61.6 us
  starting transfers between devices: 16.3 us -> 11.1 us
  local copies, waits for them, and re-layouts: 1.53 us -> 0.04 us
    reduce_scatter x1 -> x0, waiting for transfers between devices: 16.2 us -> none  [on_device(): lax.psum_scatter(jnp.broadcast_to(mine, (4, 3, 32, LANE)), 'y_lo', scatte...]
    all_to_all x1 -> x2, blocking collectives: 19 us -> 28.5 us  [on_device(): got = lax.all_to_all(sent, 'z', 0, 0, tiled=True)]
    all_to_all x1 -> x0, waiting for transfers between devices: 9.29 us -> none  [on_device(): got = lax.all_to_all(sent, 'z', 0, 0, tiled=True)]
    all_to_all x1, waiting for transfers between devices: 0.01 us -> 6.06 us  [on_device(): got = lax.all_to_all(sent, ('y_lo', 'y_hi'), 0, 0, tiled=True)]
    all_to_all x1 -> x0, starting transfers between devices: 5.96 us -> none  [on_device(): got = lax.all_to_all(sent, 'z', 0, 0, tiled=True)]
    all_gather x1, blocking collectives: 7.9 us -> 9.77 us  [on_device(): lax.all_gather(got.reshape(1920, LANE), 'core', axis=0, tiled=True)]
  transfers between devices with their start and end apart: 4 -> 3, of which waited for: 3 -> 2; matrix products, arithmetic and copies ran while one was open for 1% -> 0% of each run, Pallas kernels for 1% -> 0%
where the time goes in v9:
time: 93.4 us; the launch traced here: 92.9 us
  blocking collectives  61.6 us (66%)
  waiting for transfers between devices  13.8 us (15%)
  starting transfers between devices  11.1 us (12%)
  Pallas kernels  4.83 us (5%)
    all_to_all x2, blocking collectives, on_device(): got = lax.all_to_all(sent, 'z', 0, 0, tiled=True)  28.5 us
    all_gather x1, blocking collectives, on_device(): lax.all_gather(halves[0].reshape(1536, LANE), 'core', axis=0, tiled=True)  12.5 us
    all_to_all x1, blocking collectives, on_device(): got = lax.all_to_all(sent, 'x', 0, 0, tiled=True)  10.7 us
    all_gather x1, blocking collectives, on_device(): lax.all_gather(got.reshape(1920, LANE), 'core', axis=0, tiled=True)  9.77 us
    all_to_all x1, waiting for transfers between devices, on_device(): got = lax.all_to_all(part.reshape(4, 384, LANE), 'x', 0, 0, tiled=True)  7.75 us
    all_to_all x1, starting transfers between devices, on_device(): got = lax.all_to_all(sent, ('y_lo', 'y_hi'), 0, 0, tiled=True)  6.82 us
    all_to_all x1, waiting for transfers between devices, on_device(): got = lax.all_to_all(sent, ('y_lo', 'y_hi'), 0, 0, tiled=True)  6.06 us
    all_to_all x1, starting transfers between devices, on_device(): got = lax.all_to_all(part.reshape(4, 384, LANE), 'x', 0, 0, tiled=True)  3.59 us
  transfers between devices with their start and end apart: 3, of which 2 were waited for; matrix products, arithmetic and copies ran while one was open for 0% of the time, Pallas kernels for 0%

profile of v9, /device:TPU:1, one launch (start us, length us, event | category | flops | bytes accessed | tf_op | source)
XLA Modules:
  0.0 92.9 jit_solution(3339719202805857031)
XLA Ops:
  0.6 2.1 %rotate.1 = (bf16[2,16,96,128]{3,2,1,0:T(8,128)(2,1)S(1)}, f32[2,32,128]{2,1,0:T(8,128)S(1)}, bf16[2,192,384]{2,1,0:T(8,128)(2,1)S(1)}) custom-call(s32[1,192]{1,0:T(1,128)} %bitcast.47, s32[16,192]{1,0:T(8,128)} %bitcast.43, s32[192,128]{1,0:T(8,128)} %cols_hbm.1, bf16[192,2048]{1,0:T(8,128)(2,1)} %bitcast.42), custom_call_target="tpu_custom_call" | custom-call | tf_op jit(solution)/shard_map/rotate/pallas_call | solution.py:230
  2.8 12.5 %all_gather.6 = bf16[3072,128]{1,0:T(8,128)(2,1)S(1)} all-gather(bf16[1536,128]{1,0:T(8,128)(2,1)S(1)} %bitcast.41), channel_id=1, replica_groups=mesh['y_lo'=4,'z'=12,'core'=2,'y_hi'=2,'x'=4] {'core'}, dimensions={0}, use_global_device_ids=true | all-gather | bytes 1179648 | tf_op jit(solution)/shard_map/all_gather | solution.py:250
  15.3 0.8 add_convert_fusion
  16.2 0.0 copy-start
  16.2 0.0 copy-start.1
  16.2 0.0 copy-start.2
  16.2 3.6 %all-to-all-start = ((bf16[4,384,128]{2,1,0:T(8,128)(2,1)}), bf16[4,384,128]{2,1,0:T(8,128)(2,1)S(1)}, u32[]{:S(2)}, u32[]{:S(2)}) async-start(bf16[4,384,128]{2,1,0:T(8,128)(2,1)} %bitcast.5), calls=%async_computation | async-start | bytes 786432 | tf_op jit(solution)/shard_map/all_to_all | solution.py:253
  19.8 0.0 copy-done
  19.8 0.0 copy-done.1
  19.8 0.0 copy-done.2
  19.8 7.7 %all-to-all-done.got_ref = bf16[4,384,128]{2,1,0:T(8,128)(2,1)S(1)} async-done(((bf16[4,384,128]{2,1,0:T(8,128)(2,1)}), bf16[4,384,128]{2,1,0:T(8,128)(2,1)S(1)}, u32[]{:S(2)}, u32[]{:S(2)}) %all-to-all-start) | async-done | bytes 393248 | tf_op jit(solution)/shard_map/all_to_all | solution.py:253
  27.6 0.1 x_sum.1
  27.7 15.7 %all_to_all.25.got_ref = bf16[12,32,128]{2,1,0:T(8,128)(2,1)S(1)} all-to-all(bf16[12,32,128]{2,1,0:T(8,128)(2,1)S(1)} %x_sum.1), channel_id=1, replica_groups=mesh['y_lo'=4,'z'=12,'core'=2,'y_hi'=2,'x'=4] {'z'}, dimensions={0} | all-to-all | bytes 196608 | tf_op jit(solution)/shard_map/all_to_all | solution.py:269
  43.4 0.7 z_sum.1
  44.1 6.8 %all-to-all-start.2 = ((f32[8,32,128]{2,1,0:T(8,128)}), f32[8,32,128]{2,1,0:T(8,128)S(1)}, u32[]{:S(2)}, u32[]{:S(2)}) async-start(f32[8,32,128]{2,1,0:T(8,128)} %z_sum.1), calls=%async_computation.2 | async-start | bytes 262144 | tf_op jit(solution)/shard_map/all_to_all | solution.py:271
  50.9 0.7 collective-permute-start
  51.6 0.0 collective-permute-done.state_ref
  51.6 6.1 %all-to-all-done.2.got_ref = f32[8,32,128]{2,1,0:T(8,128)S(1)} async-done(((f32[8,32,128]{2,1,0:T(8,128)}), f32[8,32,128]{2,1,0:T(8,128)S(1)}, u32[]{:S(2)}, u32[]{:S(2)}) %all-to-all-start.2) | async-done | bytes 131104 | tf_op jit(solution)/shard_map/all_to_all | solution.py:271
  57.6 0.4 adam.1
  58.0 12.8 %all_to_all.26.got_ref = bf16[12,32,128]{2,1,0:T(8,128)(2,1)S(1)} all-to-all(bf16[12,32,128]{2,1,0:T(8,128)(2,1)S(1)} %get-tuple-element.20), channel_id=1, replica_groups=mesh['y_lo'=4,'z'=12,'core'=2,'y_hi'=2,'x'=4] {'z'}, dimensions={0} | all-to-all | bytes 196608 | tf_op jit(solution)/shard_map/all_to_all | solution.py:274
  70.8 0.1 repeat.1
  70.9 10.7 %all_to_all.27 = bf16[4,480,128]{2,1,0:T(8,128)(2,1)S(1)} all-to-all(bf16[4,480,128]{2,1,0:T(8,128)(2,1)S(1)} %repeat.1), channel_id=1, replica_groups=mesh['y_lo'=4,'z'=12,'core'=2,'y_hi'=2,'x'=4] {'x'}, dimensions={0} | all-to-all | bytes 983040 | tf_op jit(solution)/shard_map/all_to_all | solution.py:276
  81.6 9.8 %all_gather.7 = bf16[3840,128]{1,0:T(8,128)(2,1)S(1)} all-gather(bf16[1920,128]{1,0:T(8,128)(2,1)S(1)} %bitcast.39), channel_id=1, replica_groups=mesh['y_lo'=4,'z'=12,'core'=2,'y_hi'=2,'x'=4] {'core'}, dimensions={0}, use_global_device_ids=true | all-gather | bytes 1474560 | tf_op jit(solution)/shard_map/all_gather | solution.py:277
  91.4 1.5 %params.1 = (bf16[192,2048]{1,0:T(8,128)(2,1)}, f32[32,128]{1,0:T(8,128)}, f32[32,128]{1,0:T(8,128)}, f32[32,128]{1,0:T(8,128)}) custom-call(bf16[2,192,384]{2,1,0:T(8,128)(2,1)S(1)} %get-tuple-element.15.place_ref, bf16[2,4,480,128]{3,2,1,0:T(8,128)(2,1)S(1)} %bitcast.38, f32[2,32,128]{2,1,0:T(8,128)S(1)} %get-tuple-element.18.signs_ref, ...), custom_call_target="tpu_custom_call" | custom-call | tf_op jit(solution)/shard_map/params/pallas_call | solution.py:280
  (2 shorter events, 0.0 us)
Async XLA Ops:
  16.2 3.6 %copy-start = (f32[2,2048]{1,0:T(2,128)S(1)}, f32[2,2048]{1,0:T(2,128)}, u32[]{:S(2)}) copy-start(f32[2,2048]{1,0:T(2,128)} %param.13) | copy-start | bytes 49156
  16.2 3.6 %copy-start.1 = (f32[2,2048]{1,0:T(2,128)S(1)}, f32[2,2048]{1,0:T(2,128)}, u32[]{:S(2)}) copy-start(f32[2,2048]{1,0:T(2,128)} %param.12) | copy-start | bytes 49156
  16.2 3.6 %copy-start.2 = (f32[2,2048]{1,0:T(2,128)S(1)}, f32[2,2048]{1,0:T(2,128)}, u32[]{:S(2)}) copy-start(f32[2,2048]{1,0:T(2,128)} %param.11) | copy-start | bytes 49156
  16.2 11.4 %all-to-all-start = ((bf16[4,384,128]{2,1,0:T(8,128)(2,1)}), bf16[4,384,128]{2,1,0:T(8,128)(2,1)S(1)}, u32[]{:S(2)}, u32[]{:S(2)}) async-start(bf16[4,384,128]{2,1,0:T(8,128)(2,1)} %bitcast.5), calls=%async_computation | async-start | bytes 786432 | tf_op jit(solution)/shard_map/all_to_all | solution.py:253
  44.1 13.6 %all-to-all-start.2 = ((f32[8,32,128]{2,1,0:T(8,128)}), f32[8,32,128]{2,1,0:T(8,128)S(1)}, u32[]{:S(2)}, u32[]{:S(2)}) async-start(f32[8,32,128]{2,1,0:T(8,128)} %z_sum.1), calls=%async_computation.2 | async-start | bytes 262144 | tf_op jit(solution)/shard_map/all_to_all | solution.py:271
  50.9 0.7 collective-permute-start

commit v10 on v9

--- a/solution.py
+++ b/solution.py
@@ -250,6 +250,7 @@
     got = lax.all_gather(halves[0].reshape(1536, LANE), "core", axis=0, tiled=True).reshape(2, 16, 96, LANE)
     other = lax.dynamic_index_in_dim(got, 1 - core, 0, keepdims=False)
     part = (halves[1].astype(F32) + other.astype(F32)).astype(BF16)
+    part, state = lax.optimization_barrier((part, state))
     got = lax.all_to_all(part.reshape(4, 384, LANE), "x", 0, 0, tiled=True)
 
     def local(kernel, name, out_shape, *operands):
@@ -264,8 +265,13 @@
 
     sent = local(x_sum_kernel, "x_sum", jax.ShapeDtypeStruct((12, 32, LANE), BF16), got)
     sent, state = lax.optimization_barrier((sent, state))
-    swap = [(4 * y_lo + x, 4 * x + y_lo) for y_lo in range(4) for x in range(4)]
-    lent = lax.ppermute(state, ("y_lo", "x"), swap)
+    lend = []
+    for x in range(4):
+        for y in (x, x + 4):
+            for up, right in ((2, 0), (1, 1), (-1, -1), (0, 2)):
+                source, target = (y, (x + right) % 4), ((y + up) % 8, x)
+                lend.append(tuple((row % 4 * 2 + row // 4) * 4 + column for row, column in (source, target)))
+    lent = lax.ppermute(state, ("y_lo", "y_hi", "x"), lend)
     got = lax.all_to_all(sent, "z", 0, 0, tiled=True)
     sent = local(z_sum_kernel, "z_sum", jax.ShapeDtypeStruct((8, 32, LANE), F32), got)
     got = lax.all_to_all(sent, ("y_lo", "y_hi"), 0, 0, tiled=True)

time: 93.4 us -> 92.5 us (level)
  waiting for transfers between devices: 13.8 us -> 2.53 us
  blocking collectives: 61.6 us -> 71.9 us
    all_to_all x0 -> x1, blocking collectives: none -> 10.2 us  [on_device(): got = lax.all_to_all(part.reshape(4, 384, LANE), 'x', 0, 0, tiled=True)]
    all_to_all x1 -> x0, waiting for transfers between devices: 7.75 us -> none  [on_device(): got = lax.all_to_all(part.reshape(4, 384, LANE), 'x', 0, 0, tiled=True)]
    all_to_all x1, waiting for transfers between devices: 6.06 us -> 0.47 us  [on_device(): got = lax.all_to_all(sent, ('y_lo', 'y_hi'), 0, 0, tiled=True)]
    ppermute x1, starting transfers between devices: 0.65 us -> 4.26 us  [on_device(): lent = lax.ppermute(state, ('y_lo', 'y_hi', 'x'), lend)]
    all_to_all x1 -> x0, starting transfers between devices: 3.59 us -> none  [on_device(): got = lax.all_to_all(part.reshape(4, 384, LANE), 'x', 0, 0, tiled=True)]
    ppermute x1, waiting for transfers between devices: 0.01 us -> 2.06 us  [on_device(): lent = lax.ppermute(state, ('y_lo', 'y_hi', 'x'), lend)]
  transfers between devices with their start and end apart: 3 -> 2, of which waited for: 2 -> 2; matrix products, arithmetic and copies ran while one was open for 0% -> 0% of each run, Pallas kernels for 0% -> 0%
where the time goes in v10:
time: 92.5 us; the launch traced here: 91.9 us
  blocking collectives  71.9 us (78%)
  starting transfers between devices  11.1 us (12%)
  Pallas kernels  4.83 us (5%)
  waiting for transfers between devices  2.53 us (3%)
    all_to_all x2, blocking collectives, on_device(): got = lax.all_to_all(sent, 'z', 0, 0, tiled=True)  29.3 us
    all_gather x1, blocking collectives, on_device(): lax.all_gather(halves[0].reshape(1536, LANE), 'core', axis=0, tiled=True)  12.5 us
    all_to_all x1, blocking collectives, on_device(): got = lax.all_to_all(sent, 'x', 0, 0, tiled=True)  10.2 us
    all_to_all x1, blocking collectives, on_device(): got = lax.all_to_all(part.reshape(4, 384, LANE), 'x', 0, 0, tiled=True)  10.2 us
    all_gather x1, blocking collectives, on_device(): lax.all_gather(got.reshape(1920, LANE), 'core', axis=0, tiled=True)  9.72 us
    all_to_all x1, starting transfers between devices, on_device(): got = lax.all_to_all(sent, ('y_lo', 'y_hi'), 0, 0, tiled=True)  6.82 us
    ppermute x1, starting transfers between devices, on_device(): lent = lax.ppermute(state, ('y_lo', 'y_hi', 'x'), lend)  4.26 us
    pallas_call x1, Pallas kernels, on_device(): pl.pallas_call(rotate_kernel, out_shape=(jax.ShapeDtypeStruct((2, 16, 96,...  2.15 us
  transfers between devices with their start and end apart: 2, of which 2 were waited for; matrix products, arithmetic and copies ran while one was open for 0% of the time, Pallas kernels for 0%

profile of v10, /device:TPU:1, one launch (start us, length us, event | category | flops | bytes accessed | tf_op | source)
XLA Modules:
  0.0 91.9 jit_solution(17947349130994350523)
XLA Ops:
  0.6 2.1 %rotate.1 = (bf16[2,16,96,128]{3,2,1,0:T(8,128)(2,1)S(1)}, f32[2,32,128]{2,1,0:T(8,128)S(1)}, bf16[2,192,384]{2,1,0:T(8,128)(2,1)S(1)}) custom-call(s32[1,192]{1,0:T(1,128)} %bitcast.50, s32[16,192]{1,0:T(8,128)} %bitcast.46, s32[192,128]{1,0:T(8,128)} %cols_hbm.1, bf16[192,2048]{1,0:T(8,128)(2,1)} %bitcast.45), custom_call_target="tpu_custom_call" | custom-call | tf_op jit(solution)/shard_map/rotate/pallas_call | solution.py:230
  2.8 12.5 %all_gather.6 = bf16[3072,128]{1,0:T(8,128)(2,1)S(1)} all-gather(bf16[1536,128]{1,0:T(8,128)(2,1)S(1)} %bitcast.44), channel_id=1, replica_groups=mesh['y_lo'=4,'z'=12,'core'=2,'y_hi'=2,'x'=4] {'core'}, dimensions={0}, use_global_device_ids=true | all-gather | bytes 1179648 | tf_op jit(solution)/shard_map/all_gather | solution.py:250
  15.3 0.0 copy-start
  15.3 0.0 copy-start.1
  15.3 0.0 copy-start.2
  15.3 0.1 fusion
  15.4 0.6 copy-done
  16.1 0.0 copy-done.1
  16.1 0.0 copy-done.2
  16.1 10.2 %all_to_all.25.got_ref = bf16[4,384,128]{2,1,0:T(8,128)(2,1)S(1)} all-to-all(bf16[4,384,128]{2,1,0:T(8,128)(2,1)S(1)} %bitcast.43), channel_id=1, replica_groups=mesh['y_lo'=4,'z'=12,'core'=2,'y_hi'=2,'x'=4] {'x'}, dimensions={0} | all-to-all | bytes 786432 | tf_op jit(solution)/shard_map/all_to_all | solution.py:254
  26.3 0.1 x_sum.1
  26.4 16.6 %all_to_all.26.got_ref = bf16[12,32,128]{2,1,0:T(8,128)(2,1)S(1)} all-to-all(bf16[12,32,128]{2,1,0:T(8,128)(2,1)S(1)} %x_sum.1), channel_id=1, replica_groups=mesh['y_lo'=4,'z'=12,'core'=2,'y_hi'=2,'x'=4] {'z'}, dimensions={0} | all-to-all | bytes 196608 | tf_op jit(solution)/shard_map/all_to_all | solution.py:275
  43.0 0.7 z_sum.1
  43.7 6.8 %all-to-all-start.2 = ((f32[8,32,128]{2,1,0:T(8,128)}), f32[8,32,128]{2,1,0:T(8,128)S(1)}, u32[]{:S(2)}, u32[]{:S(2)}) async-start(f32[8,32,128]{2,1,0:T(8,128)} %z_sum.1), calls=%async_computation.2 | async-start | bytes 262144 | tf_op jit(solution)/shard_map/all_to_all | solution.py:277
  50.5 4.3 %collective-permute-start = (f32[3,32,128]{2,1,0:T(8,128)S(1)}, f32[3,32,128]{2,1,0:T(8,128)S(1)}, u32[]{:S(2)}, u32[]{:S(2)}) collective-permute-start(f32[3,32,128]{2,1,0:T(8,128)S(1)} %pad_maximum_fusion.state_ref), channel_id=1, source_target_pairs={{0,384},{1,192},{3,580},{2,0},{4,388},{5,196},{7,576},{6,4},{193,5... | collective-permute-start | bytes 147464 | tf_op jit(solution)/shard_map/ppermute | solution.py:274
  54.7 2.1 %collective-permute-done.state_ref = f32[3,32,128]{2,1,0:T(8,128)S(1)} collective-permute-done((f32[3,32,128]{2,1,0:T(8,128)S(1)}, f32[3,32,128]{2,1,0:T(8,128)S(1)}, u32[]{:S(2)}, u32[]{:S(2)}) %collective-permute-start) | collective-permute-done | bytes 49184 | tf_op jit(solution)/shard_map/ppermute | solution.py:274
  56.8 0.5 all-to-all-done.2.got_ref
  57.3 0.4 adam.1
  57.6 12.7 %all_to_all.27.got_ref = bf16[12,32,128]{2,1,0:T(8,128)(2,1)S(1)} all-to-all(bf16[12,32,128]{2,1,0:T(8,128)(2,1)S(1)} %get-tuple-element.24), channel_id=1, replica_groups=mesh['y_lo'=4,'z'=12,'core'=2,'y_hi'=2,'x'=4] {'z'}, dimensions={0} | all-to-all | bytes 196608 | tf_op jit(solution)/shard_map/all_to_all | solution.py:280
  70.3 0.1 repeat.1
  70.4 10.2 %all_to_all.28 = bf16[4,480,128]{2,1,0:T(8,128)(2,1)S(1)} all-to-all(bf16[4,480,128]{2,1,0:T(8,128)(2,1)S(1)} %repeat.1), channel_id=1, replica_groups=mesh['y_lo'=4,'z'=12,'core'=2,'y_hi'=2,'x'=4] {'x'}, dimensions={0} | all-to-all | bytes 983040 | tf_op jit(solution)/shard_map/all_to_all | solution.py:282
  80.6 9.7 %all_gather.7 = bf16[3840,128]{1,0:T(8,128)(2,1)S(1)} all-gather(bf16[1920,128]{1,0:T(8,128)(2,1)S(1)} %bitcast.41), channel_id=1, replica_groups=mesh['y_lo'=4,'z'=12,'core'=2,'y_hi'=2,'x'=4] {'core'}, dimensions={0}, use_global_device_ids=true | all-gather | bytes 1474560 | tf_op jit(solution)/shard_map/all_gather | solution.py:283
  90.4 1.5 %params.1 = (bf16[192,2048]{1,0:T(8,128)(2,1)}, f32[32,128]{1,0:T(8,128)}, f32[32,128]{1,0:T(8,128)}, f32[32,128]{1,0:T(8,128)}) custom-call(bf16[2,192,384]{2,1,0:T(8,128)(2,1)S(1)} %get-tuple-element.17.place_ref, bf16[2,4,480,128]{3,2,1,0:T(8,128)(2,1)S(1)} %bitcast.40, f32[2,32,128]{2,1,0:T(8,128)S(1)} %get-tuple-element.22.signs_ref, ...), custom_call_target="tpu_custom_call" | custom-call | tf_op jit(solution)/shard_map/params/pallas_call | solution.py:286
  (2 shorter events, 0.0 us)
Async XLA Ops:
  15.3 0.7 copy-start
  15.3 0.7 copy-start.1
  15.3 0.7 copy-start.2
  43.7 13.6 %all-to-all-start.2 = ((f32[8,32,128]{2,1,0:T(8,128)}), f32[8,32,128]{2,1,0:T(8,128)S(1)}, u32[]{:S(2)}, u32[]{:S(2)}) async-start(f32[8,32,128]{2,1,0:T(8,128)} %z_sum.1), calls=%async_computation.2 | async-start | bytes 262144 | tf_op jit(solution)/shard_map/all_to_all | solution.py:277
  50.5 6.3 %collective-permute-start = (f32[3,32,128]{2,1,0:T(8,128)S(1)}, f32[3,32,128]{2,1,0:T(8,128)S(1)}, u32[]{:S(2)}, u32[]{:S(2)}) collective-permute-start(f32[3,32,128]{2,1,0:T(8,128)S(1)} %pad_maximum_fusion.state_ref), channel_id=1, source_target_pairs={{0,384},{1,192},{3,580},{2,0},{4,388},{5,196},{7,576},{6,4},{193,5... | collective-permute-start | bytes 147464 | tf_op jit(solution)/shard_map/ppermute | solution.py:274

commit v11 on v10

--- a/solution.py
+++ b/solution.py
@@ -37,7 +37,8 @@
 
 
 def rotate_kernel(
-    order_hbm, rows_hbm, cols_hbm, grad_hbm, out_ref, signs_ref, place_ref, order_ref, rows_ref, cols_ref, grad_ref, mixed_ref, sems
+    order_hbm, rows_hbm, cols_hbm, grad_hbm, master_hbm, first_hbm, second_hbm,
+    out_ref, signs_ref, place_ref, state_ref, order_ref, rows_ref, cols_ref, grad_ref, mixed_ref, sems
 ):
     small = [
         pltpu.make_async_copy(order_hbm, order_ref, sems.at[0]),
@@ -45,9 +46,12 @@
         pltpu.make_async_copy(cols_hbm, cols_ref, sems.at[2]),
     ]
     large = pltpu.make_async_copy(grad_hbm, grad_ref, sems.at[3])
-    for copy in small:
+    states = [
+        pltpu.make_async_copy(each, state_ref.at[i], sems.at[4 + i])
+        for i, each in enumerate((master_hbm, first_hbm, second_hbm))
+    ]
+    for copy in small + [large] + states:
         copy.start()
-    large.start()
     core = lax.axis_index("core")
     row = iota((BLOCKS, BLOCKS), 0)
     lane = iota((BLOCKS, BLOCKS), 1)
@@ -115,6 +119,8 @@
             pair = mixed[2 * x], mixed[2 * x + 1]
             rows = [part[:, c : c + LANE] * INV_ROOT for part in pair for c in (0, LANE)]
             out_ref[start // 96, (start % 96) // 24 * 4 + x] = jnp.concatenate(rows, axis=0).astype(BF16)
+    for copy in states:
+        copy.wait()
 
 
 def x_sum_kernel(got_ref, out_ref):
@@ -188,22 +194,22 @@
         axis=1,
     )
     copies = []
-    for half in range(2):
-        part = rows[:, 512 * half : 512 * half + 512]
+    for quarter in range(4):
+        part = rows[:, 256 * quarter : 256 * quarter + 256]
         for i in range(2):
             placed = jnp.dot(place_ref[i], part, preferred_element_type=F32).astype(BF16)
-            for k in range(4):
-                column = (8 * half + 2 * k + i) * LANE
+            for k in range(2):
+                column = (4 * quarter + 2 * k + i) * LANE
                 out_ref[:, column : column + LANE] = placed[:, k * LANE : (k + 1) * LANE]
-        columns = slice(1024 * half, 1024 * half + 1024)
-        copies.append(pltpu.make_async_copy(out_ref.at[:, columns], out_hbm.at[:, columns], sems.at[half]))
+        columns = slice(512 * quarter, 512 * quarter + 512)
+        copies.append(pltpu.make_async_copy(out_ref.at[:, columns], out_hbm.at[:, columns], sems.at[quarter]))
         copies[-1].start()
     terms = got_ref.at[lax.axis_index("core"), lax.axis_index("y_lo")]
     gradient = terms[384:416].astype(F32) + terms[416:448].astype(F32) + terms[448:480].astype(F32)
     news = adam_step(gradient, signs_ref[1], state_ref[0], state_ref[1], state_ref[2])
     for i, target in enumerate((master_hbm, first_hbm, second_hbm)):
         new_ref[i] = news[i]
-        copies.append(pltpu.make_async_copy(new_ref.at[i], target, sems.at[2 + i]))
+        copies.append(pltpu.make_async_copy(new_ref.at[i], target, sems.at[4 + i]))
         copies[-1].start()
     for copy in copies:
         copy.wait()
@@ -225,32 +231,31 @@
     def by_slot(value):
         return value.reshape(16, 2, LANE).transpose(1, 0, 2).reshape(2, BLOCK)
 
-    state = jnp.stack([by_row(each) for each in (master, first_moment, second_moment)])
-
-    halves, signs, place = pl.pallas_call(
+    inputs = order_row, rows_t, sign_cols, grads[0], by_row(master), by_row(first_moment), by_row(second_moment)
+    halves, signs, place, state = pl.pallas_call(
         rotate_kernel,
         out_shape=(
             jax.ShapeDtypeStruct((2, 16, 96, LANE), BF16),
             jax.ShapeDtypeStruct((2, 32, LANE), F32),
             jax.ShapeDtypeStruct((2, BLOCKS, 384), BF16),
+            jax.ShapeDtypeStruct((3, 32, LANE), F32),
         ),
-        in_specs=[HBM] * 4,
-        out_specs=(VMEM,) * 3,
+        in_specs=[HBM] * 7,
+        out_specs=(VMEM,) * 4,
         scratch_shapes=[
             pltpu.VMEM((1, BLOCKS), jnp.int32),
             pltpu.VMEM((16, BLOCKS), jnp.int32),
             pltpu.VMEM((BLOCKS, LANE), jnp.int32),
             pltpu.VMEM((BLOCKS, BLOCK), BF16),
             pltpu.VMEM((8, BLOCKS, 256), F32),
-            pltpu.SemaphoreType.DMA((4,)),
+            pltpu.SemaphoreType.DMA((7,)),
         ],
         compiler_params=ROOM,
         name="rotate",
-    )(*(pltpu.with_memory_space_constraint(each, pltpu.HBM) for each in (order_row, rows_t, sign_cols, grads[0])))
+    )(*(pltpu.with_memory_space_constraint(each, pltpu.HBM) for each in inputs))
     got = lax.all_gather(halves[0].reshape(1536, LANE), "core", axis=0, tiled=True).reshape(2, 16, 96, LANE)
     other = lax.dynamic_index_in_dim(got, 1 - core, 0, keepdims=False)
     part = (halves[1].astype(F32) + other.astype(F32)).astype(BF16)
-    part, state = lax.optimization_barrier((part, state))
     got = lax.all_to_all(part.reshape(4, 384, LANE), "x", 0, 0, tiled=True)
 
     def local(kernel, name, out_shape, *operands):
@@ -291,7 +296,7 @@
         scratch_shapes=[
             pltpu.VMEM((BLOCKS, BLOCK), BF16),
             pltpu.VMEM((3, 32, LANE), F32),
-            pltpu.SemaphoreType.DMA((5,)),
+            pltpu.SemaphoreType.DMA((7,)),
         ],
         compiler_params=ROOM,
         name="params",

time: 92.5 us -> 91.7 us (level)
  no operation moved by 1% of the time
where the time goes in v11:
time: 91.7 us; the launch traced here: 91.3 us
  blocking collectives  72 us (79%)
  starting transfers between devices  11.1 us (12%)
  Pallas kernels  4.89 us (5%)
  waiting for transfers between devices  2.53 us (3%)
    all_to_all x2, blocking collectives, on_device(): got = lax.all_to_all(sent, 'z', 0, 0, tiled=True)  29.3 us
    all_gather x1, blocking collectives, on_device(): lax.all_gather(halves[0].reshape(1536, LANE), 'core', axis=0, tiled=True)  12.5 us
    all_to_all x1, blocking collectives, on_device(): got = lax.all_to_all(sent, 'x', 0, 0, tiled=True)  10.2 us
    all_to_all x1, blocking collectives, on_device(): got = lax.all_to_all(part.reshape(4, 384, LANE), 'x', 0, 0, tiled=True)  10.2 us
    all_gather x1, blocking collectives, on_device(): lax.all_gather(got.reshape(1920, LANE), 'core', axis=0, tiled=True)  9.72 us
    all_to_all x1, starting transfers between devices, on_device(): got = lax.all_to_all(sent, ('y_lo', 'y_hi'), 0, 0, tiled=True)  6.82 us
    ppermute x1, starting transfers between devices, on_device(): lent = lax.ppermute(state, ('y_lo', 'y_hi', 'x'), lend)  4.26 us
    pallas_call x1, Pallas kernels, on_device(): pl.pallas_call(rotate_kernel, out_shape=(jax.ShapeDtypeStruct((2, 16, 96,...  2.17 us
  transfers between devices with their start and end apart: 2, of which 2 were waited for; matrix products, arithmetic and copies ran while one was open for 0% of the time, Pallas kernels for 0%

profile of v11, /device:TPU:1, one launch (start us, length us, event | category | flops | bytes accessed | tf_op | source)
XLA Modules:
  0.0 91.3 jit_solution(17461065303288670517)
XLA Ops:
  0.6 2.2 %rotate.1 = (bf16[2,16,96,128]{3,2,1,0:T(8,128)(2,1)S(1)}, f32[2,32,128]{2,1,0:T(8,128)S(1)}, bf16[2,192,384]{2,1,0:T(8,128)(2,1)S(1)}, f32[3,32,128]{2,1,0:T(8,128)S(1)}) custom-call(s32[1,192]{1,0:T(1,128)} %bitcast.48, s32[16,192]{1,0:T(8,128)} %bitcast.44, s32[192,128]{1,0:T(8,128)} %cols_hbm.1, bf16[192,2048]{1,0:T(8,128)(2,1)} %bitcast.43, ...), custom_call_target="tpu_custom_call" | custom-call | tf_op jit(solution)/shard_map/rotate/pallas_call | solution.py:235
  2.9 12.5 %all_gather.6 = bf16[3072,128]{1,0:T(8,128)(2,1)S(1)} all-gather(bf16[1536,128]{1,0:T(8,128)(2,1)S(1)} %bitcast.42), channel_id=1, replica_groups=mesh['y_lo'=4,'z'=12,'core'=2,'y_hi'=2,'x'=4] {'core'}, dimensions={0}, use_global_device_ids=true | all-gather | bytes 1179648 | tf_op jit(solution)/shard_map/all_gather | solution.py:256
  15.4 0.1 add_convert_fusion
  15.5 10.2 %all_to_all.25.got_ref = bf16[4,384,128]{2,1,0:T(8,128)(2,1)S(1)} all-to-all(bf16[4,384,128]{2,1,0:T(8,128)(2,1)S(1)} %bitcast.41), channel_id=1, replica_groups=mesh['y_lo'=4,'z'=12,'core'=2,'y_hi'=2,'x'=4] {'x'}, dimensions={0} | all-to-all | bytes 786432 | tf_op jit(solution)/shard_map/all_to_all | solution.py:259
  25.7 0.1 x_sum.1
  25.8 16.6 %all_to_all.26.got_ref = bf16[12,32,128]{2,1,0:T(8,128)(2,1)S(1)} all-to-all(bf16[12,32,128]{2,1,0:T(8,128)(2,1)S(1)} %x_sum.1), channel_id=1, replica_groups=mesh['y_lo'=4,'z'=12,'core'=2,'y_hi'=2,'x'=4] {'z'}, dimensions={0} | all-to-all | bytes 196608 | tf_op jit(solution)/shard_map/all_to_all | solution.py:280
  42.4 0.7 z_sum.1
  43.1 6.8 %all-to-all-start.2 = ((f32[8,32,128]{2,1,0:T(8,128)}), f32[8,32,128]{2,1,0:T(8,128)S(1)}, u32[]{:S(2)}, u32[]{:S(2)}) async-start(f32[8,32,128]{2,1,0:T(8,128)} %z_sum.1), calls=%async_computation.2 | async-start | bytes 262144 | tf_op jit(solution)/shard_map/all_to_all | solution.py:282
  49.9 4.3 %collective-permute-start = (f32[3,32,128]{2,1,0:T(8,128)S(1)}, f32[3,32,128]{2,1,0:T(8,128)S(1)}, u32[]{:S(2)}, u32[]{:S(2)}) collective-permute-start(f32[3,32,128]{2,1,0:T(8,128)S(1)} %get-tuple-element.21.state_ref), channel_id=1, source_target_pairs={{0,384},{1,192},{3,580},{2,0},{4,388},{5,196},{7,576},{6,4},{193,5... | collective-permute-start | bytes 147464 | tf_op jit(solution)/shard_map/ppermute | solution.py:279
  54.1 2.1 %collective-permute-done.state_ref = f32[3,32,128]{2,1,0:T(8,128)S(1)} collective-permute-done((f32[3,32,128]{2,1,0:T(8,128)S(1)}, f32[3,32,128]{2,1,0:T(8,128)S(1)}, u32[]{:S(2)}, u32[]{:S(2)}) %collective-permute-start) | collective-permute-done | bytes 49184 | tf_op jit(solution)/shard_map/ppermute | solution.py:279
  56.2 0.5 all-to-all-done.2.got_ref
  56.7 0.4 adam.1
  57.0 12.7 %all_to_all.27.got_ref = bf16[12,32,128]{2,1,0:T(8,128)(2,1)S(1)} all-to-all(bf16[12,32,128]{2,1,0:T(8,128)(2,1)S(1)} %get-tuple-element.22), channel_id=1, replica_groups=mesh['y_lo'=4,'z'=12,'core'=2,'y_hi'=2,'x'=4] {'z'}, dimensions={0} | all-to-all | bytes 196608 | tf_op jit(solution)/shard_map/all_to_all | solution.py:285
  69.7 0.1 repeat.1
  69.8 10.2 %all_to_all.28 = bf16[4,480,128]{2,1,0:T(8,128)(2,1)S(1)} all-to-all(bf16[4,480,128]{2,1,0:T(8,128)(2,1)S(1)} %repeat.1), channel_id=1, replica_groups=mesh['y_lo'=4,'z'=12,'core'=2,'y_hi'=2,'x'=4] {'x'}, dimensions={0} | all-to-all | bytes 983040 | tf_op jit(solution)/shard_map/all_to_all | solution.py:287
  80.0 9.7 %all_gather.7 = bf16[3840,128]{1,0:T(8,128)(2,1)S(1)} all-gather(bf16[1920,128]{1,0:T(8,128)(2,1)S(1)} %bitcast.39), channel_id=1, replica_groups=mesh['y_lo'=4,'z'=12,'core'=2,'y_hi'=2,'x'=4] {'core'}, dimensions={0}, use_global_device_ids=true | all-gather | bytes 1474560 | tf_op jit(solution)/shard_map/all_gather | solution.py:288
  89.8 1.5 %params.1 = (bf16[192,2048]{1,0:T(8,128)(2,1)}, f32[32,128]{1,0:T(8,128)}, f32[32,128]{1,0:T(8,128)}, f32[32,128]{1,0:T(8,128)}) custom-call(bf16[2,192,384]{2,1,0:T(8,128)(2,1)S(1)} %get-tuple-element.16.place_ref, bf16[2,4,480,128]{3,2,1,0:T(8,128)(2,1)S(1)} %bitcast.38, f32[2,32,128]{2,1,0:T(8,128)S(1)} %get-tuple-element.20.signs_ref, ...), custom_call_target="tpu_custom_call" | custom-call | tf_op jit(solution)/shard_map/params/pallas_call | solution.py:291
  (1 shorter events, 0.0 us)
Async XLA Ops:
  43.1 13.6 %all-to-all-start.2 = ((f32[8,32,128]{2,1,0:T(8,128)}), f32[8,32,128]{2,1,0:T(8,128)S(1)}, u32[]{:S(2)}, u32[]{:S(2)}) async-start(f32[8,32,128]{2,1,0:T(8,128)} %z_sum.1), calls=%async_computation.2 | async-start | bytes 262144 | tf_op jit(solution)/shard_map/all_to_all | solution.py:282
  49.9 6.3 %collective-permute-start = (f32[3,32,128]{2,1,0:T(8,128)S(1)}, f32[3,32,128]{2,1,0:T(8,128)S(1)}, u32[]{:S(2)}, u32[]{:S(2)}) collective-permute-start(f32[3,32,128]{2,1,0:T(8,128)S(1)} %get-tuple-element.21.state_ref), channel_id=1, source_target_pairs={{0,384},{1,192},{3,580},{2,0},{4,388},{5,196},{7,576},{6,4},{193,5... | collective-permute-start | bytes 147464 | tf_op jit(solution)/shard_map/ppermute | solution.py:279

commit v12 on v11

--- a/solution.py
+++ b/solution.py
@@ -279,6 +279,7 @@
     lent = lax.ppermute(state, ("y_lo", "y_hi", "x"), lend)
     got = lax.all_to_all(sent, "z", 0, 0, tiled=True)
     sent = local(z_sum_kernel, "z_sum", jax.ShapeDtypeStruct((8, 32, LANE), F32), got)
+    sent, lent = lax.optimization_barrier((sent, lent))
     got = lax.all_to_all(sent, ("y_lo", "y_hi"), 0, 0, tiled=True)
     shapes = (jax.ShapeDtypeStruct((12, 32, LANE), BF16), jax.ShapeDtypeStruct((3, 32, LANE), BF16))
     sent, terms = local(adam_kernel, "adam", shapes, got, signs, lent)

time: 91.7 us -> 95.2 us (1.038)
  waiting for transfers between devices: 2.53 us -> 5.9 us
    all_to_all x2 -> x1, blocking collectives: 29.3 us -> 15.2 us  [on_device(): got = lax.all_to_all(sent, 'z', 0, 0, tiled=True)]
    all_to_all x0 -> x1, blocking collectives: none -> 13.3 us  [on_device(): got = lax.all_to_all(sent, ('y_lo', 'y_hi'), 0, 0, tiled=True)]
    all_to_all x1, waiting for transfers between devices: 0.47 us -> 5.89 us  [on_device(): got = lax.all_to_all(sent, 'z', 0, 0, tiled=True)]
    ppermute x1, waiting for transfers between devices: 2.06 us -> 0.01 us  [on_device(): lent = lax.ppermute(state, ('y_lo', 'y_hi', 'x'), lend)]
  transfers between devices with their start and end apart: 2 -> 2, of which waited for: 2 -> 1; matrix products, arithmetic and copies ran while one was open for 0% -> 0% of each run, Pallas kernels for 0% -> 0%
where the time goes in v12:
time: 95.2 us; the launch traced here: 94.8 us
  blocking collectives  72.3 us (76%)
  starting transfers between devices  10.9 us (11%)
  waiting for transfers between devices  5.9 us (6%)
  Pallas kernels  4.88 us (5%)
    all_to_all x1, blocking collectives, on_device(): got = lax.all_to_all(sent, 'z', 0, 0, tiled=True)  15.2 us
    all_to_all x1, blocking collectives, on_device(): got = lax.all_to_all(sent, ('y_lo', 'y_hi'), 0, 0, tiled=True)  13.3 us
    all_gather x1, blocking collectives, on_device(): lax.all_gather(halves[0].reshape(1536, LANE), 'core', axis=0, tiled=True)  12.5 us
    all_to_all x1, blocking collectives, on_device(): got = lax.all_to_all(sent, 'x', 0, 0, tiled=True)  10.5 us
    all_gather x1, blocking collectives, on_device(): lax.all_gather(got.reshape(1920, LANE), 'core', axis=0, tiled=True)  10.4 us
    all_to_all x1, blocking collectives, on_device(): got = lax.all_to_all(part.reshape(4, 384, LANE), 'x', 0, 0, tiled=True)  10.2 us
    all_to_all x1, starting transfers between devices, on_device(): got = lax.all_to_all(sent, 'z', 0, 0, tiled=True)  6.67 us
    all_to_all x1, waiting for transfers between devices, on_device(): got = lax.all_to_all(sent, 'z', 0, 0, tiled=True)  5.89 us
  transfers between devices with their start and end apart: 2, of which 1 were waited for; matrix products, arithmetic and copies ran while one was open for 0% of the time, Pallas kernels for 0%

profile of v12, /device:TPU:1, one launch (start us, length us, event | category | flops | bytes accessed | tf_op | source)
XLA Modules:
  0.0 94.8 jit_solution(3119337545964581986)
XLA Ops:
  0.6 2.2 %rotate.1 = (bf16[2,16,96,128]{3,2,1,0:T(8,128)(2,1)S(1)}, f32[2,32,128]{2,1,0:T(8,128)S(1)}, bf16[2,192,384]{2,1,0:T(8,128)(2,1)S(1)}, f32[3,32,128]{2,1,0:T(8,128)S(1)}) custom-call(s32[1,192]{1,0:T(1,128)} %bitcast.48, s32[16,192]{1,0:T(8,128)} %bitcast.44, s32[192,128]{1,0:T(8,128)} %cols_hbm.1, bf16[192,2048]{1,0:T(8,128)(2,1)} %bitcast.43, ...), custom_call_target="tpu_custom_call" | custom-call | tf_op jit(solution)/shard_map/rotate/pallas_call | solution.py:235
  2.9 12.5 %all_gather.6 = bf16[3072,128]{1,0:T(8,128)(2,1)S(1)} all-gather(bf16[1536,128]{1,0:T(8,128)(2,1)S(1)} %bitcast.42), channel_id=1, replica_groups=mesh['y_lo'=4,'z'=12,'core'=2,'y_hi'=2,'x'=4] {'core'}, dimensions={0}, use_global_device_ids=true | all-gather | bytes 1179648 | tf_op jit(solution)/shard_map/all_gather | solution.py:256
  15.4 0.1 add_convert_fusion
  15.5 10.2 %all_to_all.25.got_ref = bf16[4,384,128]{2,1,0:T(8,128)(2,1)S(1)} all-to-all(bf16[4,384,128]{2,1,0:T(8,128)(2,1)S(1)} %bitcast.41), channel_id=1, replica_groups=mesh['y_lo'=4,'z'=12,'core'=2,'y_hi'=2,'x'=4] {'x'}, dimensions={0} | all-to-all | bytes 786432 | tf_op jit(solution)/shard_map/all_to_all | solution.py:259
  25.7 0.7 x_sum.1
  26.4 6.7 %all-to-all-start.1 = ((bf16[12,32,128]{2,1,0:T(8,128)(2,1)}), bf16[12,32,128]{2,1,0:T(8,128)(2,1)S(1)}, u32[]{:S(2)}, u32[]{:S(2)}) async-start(bf16[12,32,128]{2,1,0:T(8,128)(2,1)} %x_sum.1), calls=%async_computation.1 | async-start | bytes 196608 | tf_op jit(solution)/shard_map/all_to_all | solution.py:280
  33.1 4.2 %collective-permute-start = (f32[3,32,128]{2,1,0:T(8,128)S(1)}, f32[3,32,128]{2,1,0:T(8,128)S(1)}, u32[]{:S(2)}, u32[]{:S(2)}) collective-permute-start(f32[3,32,128]{2,1,0:T(8,128)S(1)} %get-tuple-element.22.state_ref), channel_id=1, source_target_pairs={{0,384},{1,192},{3,580},{2,0},{4,388},{5,196},{7,576},{6,4},{193,5... | collective-permute-start | bytes 147464 | tf_op jit(solution)/shard_map/ppermute | solution.py:279
  37.3 5.9 %all-to-all-done.1.got_ref = bf16[12,32,128]{2,1,0:T(8,128)(2,1)S(1)} async-done(((bf16[12,32,128]{2,1,0:T(8,128)(2,1)}), bf16[12,32,128]{2,1,0:T(8,128)(2,1)S(1)}, u32[]{:S(2)}, u32[]{:S(2)}) %all-to-all-start.1) | async-done | bytes 98336 | tf_op jit(solution)/shard_map/all_to_all | solution.py:280
  43.2 0.0 collective-permute-done.state_ref
  43.3 13.3 %all_to_all.26.got_ref = f32[8,32,128]{2,1,0:T(8,128)S(1)} all-to-all(f32[8,32,128]{2,1,0:T(8,128)S(1)} %z_sum.1), channel_id=1, replica_groups=mesh['y_lo'=4,'z'=12,'core'=2,'y_hi'=2,'x'=4] {'y_lo','y_hi'}, dimensions={0} | all-to-all | bytes 262144 | tf_op jit(solution)/shard_map/all_to_all | solution.py:283
  56.6 0.4 adam.1
  57.0 15.2 %all_to_all.27.got_ref = bf16[12,32,128]{2,1,0:T(8,128)(2,1)S(1)} all-to-all(bf16[12,32,128]{2,1,0:T(8,128)(2,1)S(1)} %get-tuple-element.26), channel_id=1, replica_groups=mesh['y_lo'=4,'z'=12,'core'=2,'y_hi'=2,'x'=4] {'z'}, dimensions={0} | all-to-all | bytes 196608 | tf_op jit(solution)/shard_map/all_to_all | solution.py:286
  72.2 0.1 repeat.1
  72.3 10.5 %all_to_all.28 = bf16[4,480,128]{2,1,0:T(8,128)(2,1)S(1)} all-to-all(bf16[4,480,128]{2,1,0:T(8,128)(2,1)S(1)} %repeat.1), channel_id=1, replica_groups=mesh['y_lo'=4,'z'=12,'core'=2,'y_hi'=2,'x'=4] {'x'}, dimensions={0} | all-to-all | bytes 983040 | tf_op jit(solution)/shard_map/all_to_all | solution.py:288
  82.8 10.4 %all_gather.7 = bf16[3840,128]{1,0:T(8,128)(2,1)S(1)} all-gather(bf16[1920,128]{1,0:T(8,128)(2,1)S(1)} %bitcast.39), channel_id=1, replica_groups=mesh['y_lo'=4,'z'=12,'core'=2,'y_hi'=2,'x'=4] {'core'}, dimensions={0}, use_global_device_ids=true | all-gather | bytes 1474560 | tf_op jit(solution)/shard_map/all_gather | solution.py:289
  93.2 1.5 %params.1 = (bf16[192,2048]{1,0:T(8,128)(2,1)}, f32[32,128]{1,0:T(8,128)}, f32[32,128]{1,0:T(8,128)}, f32[32,128]{1,0:T(8,128)}) custom-call(bf16[2,192,384]{2,1,0:T(8,128)(2,1)S(1)} %get-tuple-element.18.place_ref, bf16[2,4,480,128]{3,2,1,0:T(8,128)(2,1)S(1)} %bitcast.38, f32[2,32,128]{2,1,0:T(8,128)S(1)} %get-tuple-element.24.signs_ref, ...), custom_call_target="tpu_custom_call" | custom-call | tf_op jit(solution)/shard_map/params/pallas_call | solution.py:292
  (2 shorter events, 0.0 us)
Async XLA Ops:
  26.4 16.8 %all-to-all-start.1 = ((bf16[12,32,128]{2,1,0:T(8,128)(2,1)}), bf16[12,32,128]{2,1,0:T(8,128)(2,1)S(1)}, u32[]{:S(2)}, u32[]{:S(2)}) async-start(bf16[12,32,128]{2,1,0:T(8,128)(2,1)} %x_sum.1), calls=%async_computation.1 | async-start | bytes 196608 | tf_op jit(solution)/shard_map/all_to_all | solution.py:280
  33.1 10.1 %collective-permute-start = (f32[3,32,128]{2,1,0:T(8,128)S(1)}, f32[3,32,128]{2,1,0:T(8,128)S(1)}, u32[]{:S(2)}, u32[]{:S(2)}) collective-permute-start(f32[3,32,128]{2,1,0:T(8,128)S(1)} %get-tuple-element.22.state_ref), channel_id=1, source_target_pairs={{0,384},{1,192},{3,580},{2,0},{4,388},{5,196},{7,576},{6,4},{193,5... | collective-permute-start | bytes 147464 | tf_op jit(solution)/shard_map/ppermute | solution.py:279
